TPU v7x, 512 devices: a whole 4x8x8 slice. The times are simulated.
512 devices in a mesh: seq: 16 (over x_hi, z), head: 8 (over y), cand: 4 (over x_lo, core).
Axes of the slice: x: 4 (x_hi: 2, x_lo: 2; x = x_hi * 2 + x_lo), y: 8, z: 8, core: 2. Of those that a mesh axis runs over, the one named last changes fastest.
Arguments:
- hidden: bfloat16 [256, 16384], P('cand', 'seq'), may hold values from -6 to 6
- query_weight: bfloat16 [16384, 2048], P('seq', 'head'), may hold values from -0.046875 to 0.046875
- key_weight: bfloat16 [16384, 128], P('seq'), may hold values from -0.375 to 0.375
- value_weight: bfloat16 [16384, 128], P('seq'), may hold values from -0.046875 to 0.046875
- out_weight: bfloat16 [2048, 16384], P('head', 'seq'), may hold values from -0.125 to 0.125
- key_cache: bfloat16 [131072, 128], P(('seq', 'cand')), may hold values from -60 to 60
- value_cache: bfloat16 [131072, 128], P(('seq', 'cand')), may hold values from -6 to 6
- cand_group: int32 [32], replicated, may hold values from 0 to 7
Outputs:
- attn_out: bfloat16 [256, 16384], P('cand', ('seq', 'head'))
Inputs may be any that keep to these rules, and one draw needn't show every extreme that they name: `cand_group`: each candidate's question.
All inputs are finite; a program needn't handle non-finite values.
Results may differ from a plain program's by a relative error of at most 0.02.
Values may be sent and summed in bfloat16 or wider, within the bound.
No kernel may reach another device: no remote copies, remote signals or barrier semaphores. Data moves between devices by JAX's collectives and lax.ppermute only.
A program may use at most 64 MiB of HBM per device.

v0:
```python
import math

import jax
import jax.numpy as jnp
from jax import lax
from jax.sharding import PartitionSpec as P

HD = 128
GROUPS = 8
ANS_LEN = 8


NEGATIVE = -1e30


def joined(part, axis, combine):
    gathered = jax.tree.map(lambda a: lax.all_gather(a, axis), part)

    def take(source):
        return jax.tree.map(lambda a: lax.dynamic_index_in_dim(a, source, 0, False), gathered)

    return lax.fori_loop(
        1, lax.axis_size(axis), lambda source, state: combine(state, take(source)), take(0)
    )


def combine(first, second):
    top = jnp.maximum(first[0], second[0])
    one = jnp.exp(first[0] - top)
    two = jnp.exp(second[0] - top)
    return (
        top,
        first[1] * one + second[1] * two,
        first[2] * one[..., None] + second[2] * two[..., None],
    )


def body(
    hidden, query_weight, key_weight, value_weight, out_weight, key_cache, value_cache, cand_group
):
    tok_dev = hidden.shape[0]
    heads_dev = query_weight.shape[1] // HD
    shard_len = key_cache.shape[0]
    prefix_len = shard_len * lax.axis_size("seq") * lax.axis_size("cand")
    scale = HD ** (-0.5)
    partial_terms = (
        jnp.dot(hidden, query_weight, preferred_element_type=jnp.float32),
        jnp.dot(hidden, key_weight, preferred_element_type=jnp.float32),
        jnp.dot(hidden, value_weight, preferred_element_type=jnp.float32),
    )
    query_sum, key_sum, value_sum = lax.psum(
        (partial_terms[0], partial_terms[1], partial_terms[2]), "seq"
    )
    queries = query_sum.astype(jnp.bfloat16)
    keys = key_sum.astype(jnp.bfloat16)
    values = value_sum.astype(jnp.bfloat16)
    every_query = lax.all_gather(queries, "cand", axis=0, tiled=True).reshape(-1, heads_dev, HD)
    rows = every_query.shape[0]
    limits = (jnp.repeat(cand_group, ANS_LEN) + 1) * (prefix_len // GROUPS)
    width = math.gcd(shard_len, 1024)
    count = shard_len // width
    base = lax.axis_index(("seq", "cand")) * shard_len

    def update(carry, block):
        top, total, acc = carry
        key_block, value_block, start = block
        scores = (
            jnp.einsum("thd,kd->thk", every_query, key_block, preferred_element_type=jnp.float32)
            * scale
        )
        places = start + jnp.arange(width, dtype=jnp.int32)
        visible = (places[None, :] < limits[:, None])[:, None, :]
        scores = jnp.where(visible, scores, NEGATIVE)
        new_top = jnp.maximum(top, jnp.max(scores, axis=2))
        weights = jnp.where(visible, jnp.exp(scores - new_top[..., None]), 0.0)
        shrink = jnp.exp(top - new_top)
        total = total * shrink + jnp.sum(weights, axis=2)
        acc = acc * shrink[..., None] + jnp.einsum(
            "thk,kd->thd",
            weights.astype(jnp.bfloat16),
            value_block,
            preferred_element_type=jnp.float32,
        )
        return ((new_top, total, acc), None)

    start_state = (
        jnp.full((rows, heads_dev), NEGATIVE, jnp.float32),
        jnp.zeros((rows, heads_dev), jnp.float32),
        jnp.zeros((rows, heads_dev, HD), jnp.float32),
    )
    block_starts = jnp.arange(count, dtype=jnp.int32) * width + base
    (top, total, acc), _ = lax.scan(
        update,
        start_state,
        (key_cache.reshape(count, width, HD), value_cache.reshape(count, width, HD), block_starts),
    )
    own_start = lax.axis_index("cand") * tok_dev
    merged = joined((top, total, acc), ("seq", "cand"), combine)
    prefix_top = lax.dynamic_slice_in_dim(merged[0], own_start, tok_dev, 0)
    prefix_total = lax.dynamic_slice_in_dim(merged[1], own_start, tok_dev, 0)
    prefix_acc = lax.dynamic_slice_in_dim(merged[2], own_start, tok_dev, 0)
    cand_dev = tok_dev // ANS_LEN
    query_four = queries.reshape(cand_dev, ANS_LEN, heads_dev, HD)
    key_four = keys.reshape(cand_dev, ANS_LEN, HD)
    value_four = values.reshape(cand_dev, ANS_LEN, HD)
    own = (
        jnp.einsum("cthd,cud->cthu", query_four, key_four, preferred_element_type=jnp.float32)
        * scale
    )
    causal = (jnp.arange(ANS_LEN)[None, :] <= jnp.arange(ANS_LEN)[:, None])[None, :, None, :]
    own = jnp.where(causal, own, NEGATIVE)
    own_top = jnp.max(own, axis=3)
    own_weights = jnp.where(causal, jnp.exp(own - own_top[..., None]), 0.0)
    own_total = jnp.sum(own_weights, axis=3).reshape(tok_dev, heads_dev)
    own_acc = jnp.einsum(
        "cthu,cud->cthd",
        own_weights.astype(jnp.bfloat16),
        value_four,
        preferred_element_type=jnp.float32,
    ).reshape(tok_dev, heads_dev, HD)
    own_top = own_top.reshape(tok_dev, heads_dev)
    best = jnp.maximum(prefix_top, own_top)
    first = jnp.exp(prefix_top - best)
    second = jnp.exp(own_top - best)
    denominator = prefix_total * first + own_total * second
    numerator = prefix_acc * first[..., None] + own_acc * second[..., None]
    attention = (
        (numerator / denominator[..., None]).astype(jnp.bfloat16).reshape(tok_dev, heads_dev * HD)
    )
    projected = jnp.dot(attention, out_weight, preferred_element_type=jnp.float32)
    return lax.psum_scatter(projected.astype(jnp.bfloat16), "head", scatter_dimension=1, tiled=True)


def solution(mesh):
    in_specs = (
        P("cand", "seq"),
        P("seq", "head"),
        P("seq", None),
        P("seq", None),
        P("head", "seq"),
        P(("seq", "cand"), None),
        P(("seq", "cand"), None),
        P(),
    )
    out_specs = P("cand", ("seq", "head"))
    return jax.shard_map(body, mesh=mesh, in_specs=in_specs, out_specs=out_specs, check_vma=False)
```

profile of v0, /device:TPU:6, one launch (start us, length us, event | category | flops | bytes accessed | tf_op | source)
XLA Modules:
  0.0 447.7 jit_solution(13566244566003365230)
XLA Ops:
  7.4 1.2 fusion.49
  8.6 1.2 fusion.50
  9.8 1.3 fusion.48
  11.1 82.6 %all-reduce.2 = (bf16[64,256]{1,0:T(8,128)(2,1)S(1)}, bf16[64,128]{1,0:T(8,128)(2,1)S(1)}, bf16[64,128]{1,0:T(8,128)(2,1)S(1)}) all-reduce(f32[64,256]{1,0:T(8,128)S(1)} %fusion.48, f32[64,128]{1,0:T(8,128)S(1)} %fusion.49, f32[64,128]{1,0:T(8,128)S(1)} %fusion.50), channel_id=1, replica_groups=mesh['seq'=16,'head'=8,'cand'=4] {'seq'}, use_global_device_ids=true, to_apply=%region_0.0 | all-reduce | flops 32768 | bytes 196608 | tf_op jit(solution)/shard_map/psum | solution.py:51
  93.7 5.4 %all_gather.21 = bf16[256,256]{1,0:T(8,128)(2,1)S(1)} all-gather(bf16[64,256]{1,0:T(8,128)(2,1)S(1)} %get-tuple-element.367), channel_id=1, replica_groups=mesh['seq'=16,'head'=8,'cand'=4] {'cand'}, dimensions={0}, use_global_device_ids=true | all-gather | bytes 163840 | tf_op jit(solution)/shard_map/all_gather | solution.py:57
  99.1 7.2 %while.35 = (s32[]{:T(128)}, f32[256,2]{0,1:T(2,128)S(1)}, f32[256,2]{0,1:T(2,128)S(1)}, f32[256,2,128]{2,0,1:T(8,128)S(1)}, s32[2]{0:T(128)S(1)}, /*index=5*/bf...) while((s32[]{:T(128)}, f32[256,2]{0,1:T(2,128)S(1)}, ...), condition=%wide.region_4.5_spmd.clone, body=%wide.region_1.4_spmd.clone.sunk | while | flops 275713536 | bytes 8565017 | solution.py:92
  107.6 60.9 %all-gather = f32[16384,2]{0,1:T(2,128)S(1)} all-gather(f32[256,2]{0,1:T(2,128)S(1)} %get-tuple-element.232), channel_id=2, replica_groups=mesh['seq'=16,'head'=8,'cand'=4] {'seq','cand'}, dimensions={0}, use_global_device_ids=true | all-gather | bytes 133120 | tf_op jit(solution)/shard_map/all_gather | solution.py:17
  168.5 62.3 %all-gather.1 = f32[16384,2]{0,1:T(2,128)S(1)} all-gather(f32[256,2]{0,1:T(2,128)S(1)} %get-tuple-element.233), channel_id=3, replica_groups=mesh['seq'=16,'head'=8,'cand'=4] {'seq','cand'}, dimensions={0}, use_global_device_ids=true | all-gather | bytes 133120 | tf_op jit(solution)/shard_map/all_gather | solution.py:17
  230.8 6.1 %all-gather.5.cloned.1.call-done = f32[16384,2,128]{2,0,1:T(8,128)} async-done(((f32[256,2,128]{2,0,1:T(8,128)}), f32[16384,2,128]{2,0,1:T(8,128)}) %all-gather.5.cloned.1.call-update) | async-done | bytes 16777232 | tf_op jit(solution)/shard_map/all_gather | solution.py:17
  238.1 154.3 %while.34 = (s32[]{:T(128)}, f32[256,2]{0,1:T(2,128)S(1)}, f32[256,2]{0,1:T(2,128)S(1)}, f32[256,2,128]{2,1,0:T(2,128)S(1)}, f32[64,256,2]{1,2,0:T(2,128)S(1)}, ...) while((s32[]{:T(128)}, f32[256,2]{0,1:T(2,128)S(1)}, ...), condition=%wide.region_6.7_spmd, body=%wide.region_5.6_spmd.sunk | while | flops 199685 | bytes 1339535 | solution.py:22
  239.4 1.1 fusion.70
  241.8 1.1 fusion.70
  244.3 1.1 fusion.70
  246.7 1.1 fusion.70
  249.2 1.1 fusion.70
  251.6 1.1 fusion.70
  254.1 1.1 fusion.70
  256.5 1.1 fusion.70
  259.0 1.1 fusion.70
  261.4 1.1 fusion.70
  263.9 1.1 fusion.70
  266.3 1.1 fusion.70
  268.8 1.1 fusion.70
  271.2 1.1 fusion.70
  273.7 1.1 fusion.70
  276.1 1.1 fusion.70
  278.6 1.1 fusion.70
  281.0 1.1 fusion.70
  283.5 1.1 fusion.70
  285.9 1.1 fusion.70
  288.4 1.1 fusion.70
  290.8 1.1 fusion.70
  293.3 1.1 fusion.70
  295.7 1.1 fusion.70
  298.2 1.1 fusion.70
  300.6 1.1 fusion.70
  303.1 1.1 fusion.70
  305.5 1.1 fusion.70
  308.0 1.1 fusion.70
  310.4 1.1 fusion.70
  312.9 1.1 fusion.70
  325.1 1.1 fusion.70
  344.7 1.1 fusion.70
  352.0 1.1 fusion.70
  371.6 1.1 fusion.70
  391.2 1.1 fusion.70
  393.8 45.7 %reduce-scatter.4.cloned.1.call-done = bf16[128,64]{1,0:T(8,128)(2,1)} async-done(((bf16[1024,64]{1,0:T(8,128)(2,1)}), bf16[128,64]{1,0:T(8,128)(2,1)}) %reduce-scatter.4.cloned.1.call-update) | async-done | bytes 16400
  439.4 1.4 copy.67
  (335 shorter events, 122.5 us)
Async XLA Ops:
  6.5 386.2 %copy-start = (bf16[256,1024]{1,0:T(8,128)(2,1)S(1)}, bf16[256,1024]{1,0:T(8,128)(2,1)}, u32[]{:S(2)}) copy-start(bf16[256,1024]{1,0:T(8,128)(2,1)} %param.16) | copy-start | bytes 1572868
  6.5 92.6 %copy-start.3 = (bf16[2048,128]{1,0:T(8,128)(2,1)S(1)}, bf16[2048,128]{1,0:T(8,128)(2,1)}, u32[]{:S(2)}) copy-start(bf16[2048,128]{1,0:T(8,128)(2,1)} %param.18) | copy-start | bytes 1572868
  6.5 92.6 %copy-start.1 = (bf16[2048,128]{1,0:T(8,128)(2,1)S(1)}, bf16[2048,128]{1,0:T(8,128)(2,1)}, u32[]{:S(2)}) copy-start(bf16[2048,128]{1,0:T(8,128)(2,1)} %param.17) | copy-start | bytes 1572868
  6.5 230.3 %all-gather.5.cloned.1.call-start = ((), (), s32[]{:S(2)}) async-start(), calls=%async_computation.1 | async-start | bytes 17039360 | tf_op jit(solution)/shard_map/all_gather | solution.py:17
  106.3 0.7 copy-start.2
  107.0 332.4 %reduce-scatter.4.cloned.1.call-start = ((), (), s32[]{:S(2)}) async-start(), calls=%async_computation.2 | async-start | bytes 294912
Sparse Core Ops, SparseCore 0:
  107.2 129.6 all-gather.4
  393.9 45.5 reduce-scatter.3
where the time goes:
time: 450 us; the launch traced here: 448 us
  blocking collectives  211 us (47%)
  local copies, waits for them, and re-layouts  84.6 us (19%)
  other arithmetic  76.4 us (17%)
  waiting for transfers between devices  51.8 us (12%)
  between operations  13.6 us (3%)
  matrix products  7.03 us (2%)
    all_gather x2, blocking collectives, joined(): gathered = jax.tree.map(lambda a: lax.all_gather(a, axis), part)  123 us
    psum x1, blocking collectives, body(): lax.psum((partial_terms[0], partial_terms[1], partial_terms[2]), 'seq')  82.6 us
    add x63, other arithmetic, combine(): first[2] * one[..., None] + second[2] * two[..., None]  70.9 us
    dynamic_slice x66, local copies, waits for them, and re-layouts, take(): lax.dynamic_index_in_dim(a, source, 0, False)  62.6 us
    unnamed x3, waiting for transfers between devices  45.7 us
  transfers between devices with their start and end apart: 2, of which 2 were waited for; matrix products, arithmetic and copies ran while one was open for 0% of the time, Pallas kernels for 0%

commit v1 on v0

v1 whole, which is shorter than its diff:
```python
import math

import jax
import jax.numpy as jnp
from jax import lax
from jax.experimental import pallas as pl
from jax.experimental.pallas import tpu as pltpu
from jax.sharding import PartitionSpec as P

HD = 128
GROUPS = 8
ANS_LEN = 8
ROW_BLOCK = 128

NEGATIVE = -1e30
LOG2E = math.log2(math.e)
SMALL_SCALE = 16.0
KEY_SCALE = 2.0

VMEM = pl.BlockSpec(memory_space=pltpu.VMEM)
HBM = pl.BlockSpec(memory_space=pltpu.HBM)

SEQ = ("far", "pair", "side")
CAND = ("lo", "core")


def call(kernel, out_shape, in_specs, **cost):
    return pl.pallas_call(
        kernel,
        out_shape=out_shape,
        in_specs=in_specs,
        out_specs=jax.tree.map(lambda _: VMEM, out_shape),
        compiler_params=pltpu.CompilerParams(vmem_limit_bytes=40 * 1024 * 1024),
        cost_estimate=pl.CostEstimate(**cost),
    )


def dot(a, b):
    return jnp.dot(a, b, preferred_element_type=jnp.float32)


def dot_transposed(a, b):
    return lax.dot_general(a, b, (((1,), (1,)), ((), ())), preferred_element_type=jnp.float32)


def project_kernel(
    hidden_hbm, query_hbm, key_hbm, value_hbm, group_hbm, key_cache, value_cache,
    out_ref, bias_ref, cache_hbm, hidden_ref, weight_ref, group_smem, sems,
):
    far, pairs, side = (lax.axis_size(name) for name in SEQ)
    features = hidden_ref.shape[1]
    width = query_hbm.shape[1]
    halves = [pl.ds(i * (features // 2), features // 2) for i in range(2)]
    copies = []

    def start(source, target):
        copies.append(pltpu.make_async_copy(source, target, sems.at[len(copies)]))
        copies[-1].start()

    for half in halves:
        start(query_hbm.at[half, :], weight_ref.at[half, pl.ds(0, width)])
        start(hidden_hbm.at[:, half], hidden_ref.at[:, half])
        start(key_hbm.at[half, :], weight_ref.at[half, pl.ds(width, HD)])
        start(value_hbm.at[half, :], weight_ref.at[half, pl.ds(width + HD, HD)])
    start(group_hbm, group_smem)
    start(key_cache, cache_hbm.at[0])
    start(value_cache, cache_hbm.at[1])
    total = None
    for i, half in enumerate(halves):
        for copy in copies[4 * i : 4 * i + 4]:
            copy.wait()
        part = dot(hidden_ref[:, half], weight_ref[half, :])
        total = part if total is None else total + part
    ring = SMALL_SCALE * lax.axis_size("pair") * side
    tokens = total.shape[0]
    for h in range(side):
        for p in range(pairs):
            out_ref[p * side + h, :tokens] = total[:, h * HD : (h + 1) * HD] * ring
    for s, scale in ((0, ring * KEY_SCALE / SMALL_SCALE), (1, ring)):
        part = total[:, width + s * HD : width + (s + 1) * HD] * scale
        for p in range(pairs):
            for f in range(far):
                place = slice((f * pairs + p) * ANS_LEN, (f * pairs + p + 1) * ANS_LEN)
                out_ref[p * side + s, tokens + f * ANS_LEN : tokens + (f + 1) * ANS_LEN] = part[place]
    copies[-3].wait()
    chunk = lax.axis_index(SEQ) // (lax.axis_size(SEQ) // GROUPS)
    lane = lax.broadcasted_iota(jnp.int32, bias_ref.shape, 1)
    bias = jnp.zeros(bias_ref.shape, jnp.float32)
    for c in range(group_smem.shape[0]):
        hidden_by = jnp.where(group_smem[c] >= chunk, 0.0, NEGATIVE)
        bias = jnp.where(lane == c, hidden_by, bias)
    bias_ref[...] = bias
    copies[-2].wait()
    copies[-1].wait()


def reduce_kernel(part_ref, out_ref):
    total = jnp.sum(part_ref[...], axis=0) * (1 / part_ref.shape[0])
    out_ref[...] = jnp.broadcast_to(total[None], out_ref.shape)


def packed(mean, level):
    high = level.astype(jnp.bfloat16).astype(jnp.float32)
    middle = (level - high).astype(jnp.bfloat16).astype(jnp.float32)
    row = lax.broadcasted_iota(jnp.int32, mean.shape, 0)
    lane = lax.broadcasted_iota(jnp.int32, mean.shape, 1)
    line = lax.broadcasted_iota(jnp.int32, (ANS_LEN, HD), 0)
    lines = jnp.zeros((ANS_LEN, HD), jnp.float32)
    for place, term in enumerate((high, middle, level - high - middle)):
        spread = jnp.sum(jnp.where(lane == row, term, 0.0), axis=0, keepdims=True)
        lines = jnp.where(line == place, spread, lines)
    return jnp.concatenate([mean, lines], axis=0).astype(jnp.bfloat16)


def unpacked(state):
    state = state.astype(jnp.float32)
    rows = state.shape[-2] - ANS_LEN
    mean = state[..., :rows, :]
    line = jnp.sum(state[..., rows:, :], axis=-2, keepdims=True)
    row = lax.broadcasted_iota(jnp.int32, mean.shape, mean.ndim - 2)
    lane = lax.broadcasted_iota(jnp.int32, mean.shape, mean.ndim - 1)
    return mean, jnp.sum(jnp.where(lane == row, line, 0.0), axis=-1, keepdims=True)


def merged(mean, level):
    best = jnp.max(level, axis=0)
    factor = jnp.exp(level - best[None])
    total = jnp.sum(factor, axis=0)
    return jnp.sum(mean * factor, axis=0) / total, best + jnp.log(total)


def attend_kernel(query_ref, cache_ref, other_ref, bias_ref, out_ref):
    scale = HD ** (-0.5)
    far, side, lo, rows, _ = out_ref.shape
    rows -= ANS_LEN
    halves = far
    sources = ROW_BLOCK // rows * halves
    cores = lax.axis_size("core")
    cands = rows // ANS_LEN
    row = lax.broadcasted_iota(jnp.int32, (ROW_BLOCK, HD), 0)
    lane = lax.broadcasted_iota(jnp.int32, (ROW_BLOCK, HD), 1)
    caches = (cache_ref, other_ref)
    steps = [(r, cache) for r in range(query_ref.shape[0] // sources) for cache in caches]

    def scored(step):
        r, cache = step
        parts = query_ref[r * sources : (r + 1) * sources, :rows]
        query = jnp.sum(parts.reshape(-1, halves, rows, HD), axis=1).reshape(ROW_BLOCK, HD)
        query = (query * (1 / SMALL_SCALE)).astype(jnp.bfloat16)
        return dot_transposed(query, cache[0])

    ahead = scored(steps[0])
    held = []
    for i, (r, cache) in enumerate(steps):
        scores = ahead
        if i + 1 < len(steps):
            ahead = scored(steps[i + 1])
        top = jnp.max(scores, axis=1, keepdims=True)
        weights = jnp.exp2((scores - top) * (scale * LOG2E))
        total = jnp.sum(weights, axis=1, keepdims=True)
        held.append((top * scale, total, dot(weights.astype(jnp.bfloat16), cache[1])))
        if len(held) < len(caches):
            continue
        top = jnp.maximum(held[0][0], held[1][0])
        factors = [jnp.exp(part[0] - top) for part in held]
        total = held[0][1] * factors[0] + held[1][1] * factors[1]
        mean = (held[0][2] * factors[0] + held[1][2] * factors[1]) / total
        held = []
        place = (row + r * ROW_BLOCK) // ANS_LEN
        cand = place // cands % lo * cores + lax.axis_index("core")
        candidate = cand * cands + place % cands
        bias = jnp.sum(jnp.where(lane == candidate, bias_ref[0:1, :], 0.0), axis=1, keepdims=True)
        level = top + jnp.log(total) + bias
        for j in range(ROW_BLOCK // rows):
            part = slice(j * rows, (j + 1) * rows)
            state = packed(mean[part], level[part])
            block = r * (ROW_BLOCK // rows) + j
            for f in range(far):
                out_ref[f, block // lo, block % lo] = state


def merge_kernel(state_ref, own_ref, out_ref):
    mean, level = merged(*unpacked(state_ref[...]))
    halves, pairs, _ = (lax.axis_size(name) for name in SEQ)
    rows = pairs * ANS_LEN
    tokens = mean.shape[0]

    def own(s, part, scale):
        place = (s * lax.axis_size("lo") + lax.axis_index("lo")) * halves
        total = own_ref[place, part]
        for half in range(1, halves):
            total = total + own_ref[place + half, part]
        return (total * (1 / scale)).astype(jnp.bfloat16)

    query = own(lax.axis_index("side"), slice(0, tokens), SMALL_SCALE)
    key = own(0, slice(tokens, None), KEY_SCALE)
    value = own(1, slice(tokens, None), SMALL_SCALE)
    scores = dot_transposed(query, key) * HD ** (-0.5)
    row = lax.broadcasted_iota(jnp.int32, scores.shape, 0)
    column = lax.broadcasted_iota(jnp.int32, scores.shape, 1)
    shown = (row // rows == column // ANS_LEN) & (column % ANS_LEN <= row % ANS_LEN)
    scores = jnp.where(shown, scores, NEGATIVE)
    top = jnp.max(scores, axis=1, keepdims=True)
    weights = jnp.where(shown, jnp.exp(scores - top), 0.0)
    total = jnp.sum(weights, axis=1, keepdims=True)
    own_mean = dot(weights.astype(jnp.bfloat16), value) / total
    own_level = top + jnp.log(total)
    row = lax.broadcasted_iota(jnp.int32, level.shape, 0)
    mine = row // ANS_LEN % pairs == lax.axis_index("pair")
    own_level = jnp.where(mine, own_level, NEGATIVE)
    mean, level = merged(jnp.stack([mean, own_mean]), jnp.stack([level, own_level]))
    out_ref[...] = jnp.broadcast_to(packed(mean, level)[None], out_ref.shape)


def output_kernel(state_ref, weight_ref, out_ref):
    blocks, _, width = out_ref.shape
    columns = [merged(*unpacked(state_ref[s]))[0] for s in range(state_ref.shape[0])]
    attention = jnp.concatenate(columns, axis=1).astype(jnp.bfloat16)
    out = dot(attention, weight_ref[...])
    for block in range(blocks):
        out_ref[block] = out[:, block * width : (block + 1) * width].astype(jnp.bfloat16)


def sum_kernel(part_ref, out_ref):
    out_ref[...] = jnp.sum(part_ref[...].astype(jnp.float32), axis=0).astype(out_ref.dtype)


def body(
    hidden, query_weight, key_weight, value_weight, out_weight, key_cache, value_cache, cand_group
):
    tok_dev, feat_dev = hidden.shape
    heads_dev = query_weight.shape[1] // HD
    head, lo = lax.axis_size("head"), lax.axis_size("lo")
    far, pairs, side = (lax.axis_size(name) for name in SEQ)
    shard_len = key_cache.shape[0]
    bf16, f32 = jnp.bfloat16, jnp.float32
    rows = tok_dev * heads_dev * lo
    columns = out_weight.shape[1] // head

    inputs = (hidden, query_weight, key_weight, value_weight, cand_group, key_cache, value_cache)
    inputs = [pltpu.with_memory_space_constraint(x, pltpu.HBM) for x in inputs]
    partial, bias, cache = pl.pallas_call(
        project_kernel,
        out_shape=(
            jax.ShapeDtypeStruct((pairs * side, tok_dev + far * ANS_LEN, HD), f32),
            jax.ShapeDtypeStruct((ANS_LEN, HD), f32),
            jax.ShapeDtypeStruct((2, *key_cache.shape), bf16),
        ),
        in_specs=[HBM] * 7,
        out_specs=(VMEM, VMEM, HBM),
        scratch_shapes=[
            pltpu.VMEM(hidden.shape, bf16),
            pltpu.VMEM((feat_dev, (heads_dev + 2) * HD), bf16),
            pltpu.SMEM(cand_group.shape, jnp.int32),
            pltpu.SemaphoreType.DMA((11,)),
        ],
        compiler_params=pltpu.CompilerParams(vmem_limit_bytes=40 * 1024 * 1024),
        cost_estimate=pl.CostEstimate(
            flops=2 * tok_dev * feat_dev * (heads_dev + 2) * HD,
            bytes_accessed=2 * feat_dev * (tok_dev + (heads_dev + 2) * HD),
            transcendentals=0,
        ),
    )(*inputs)
    other = lax.ppermute(cache, "core", [(0, 1), (1, 0)])
    partial = lax.all_to_all(partial.astype(jnp.float16), ("pair", "side"), 0, 0, tiled=True)
    near = far * side * lo
    queries = call(
        reduce_kernel,
        jax.ShapeDtypeStruct((near, *partial.shape[1:]), f32),
        [VMEM],
        flops=partial.size,
        bytes_accessed=partial.size * 4,
        transcendentals=0,
    )(partial.astype(f32))
    queries = queries.astype(jnp.float16)
    queries = lax.all_to_all(queries, ("side", "lo", "far"), 0, 0, tiled=True).astype(f32)
    state = call(
        attend_kernel,
        jax.ShapeDtypeStruct((far, side, lo, tok_dev + ANS_LEN, HD), bf16),
        [VMEM] * 4,
        flops=8 * rows * shard_len * HD,
        bytes_accessed=8 * shard_len * HD,
        transcendentals=2 * rows * shard_len,
    )(queries, cache, other, bias)
    state = state.reshape(near, tok_dev + ANS_LEN, HD)
    state = lax.all_to_all(state, ("far", "side", "lo"), 0, 0, tiled=True)
    state = call(
        merge_kernel,
        jax.ShapeDtypeStruct((side * pairs, tok_dev + ANS_LEN, HD), bf16),
        [VMEM] * 2,
        flops=4 * state.size,
        bytes_accessed=2 * state.size,
        transcendentals=0,
    )(state, queries)
    state = lax.all_to_all(state, ("side", "pair"), 0, 0, tiled=True)
    projected = call(
        output_kernel,
        jax.ShapeDtypeStruct((head, tok_dev, columns), bf16),
        [VMEM] * 2,
        flops=2 * tok_dev * out_weight.size,
        bytes_accessed=2 * out_weight.size,
        transcendentals=0,
    )(state.reshape(side, pairs, tok_dev + ANS_LEN, HD), out_weight)
    projected = lax.all_to_all(projected, "head", 0, 0, tiled=True)
    return call(
        sum_kernel,
        jax.ShapeDtypeStruct((tok_dev, columns), bf16),
        [VMEM],
        flops=projected.size,
        bytes_accessed=2 * projected.size,
        transcendentals=0,
    )(projected)


def solution(mesh):
    seq, head, cand = (mesh.shape[name] for name in ("seq", "head", "cand"))
    parts = jax.sharding.Mesh(
        mesh.devices.reshape(2, seq // 4, 2, head, cand // 2, 2), (*SEQ, "head", *CAND)
    )
    in_specs = (
        P(CAND, SEQ),
        P(SEQ, "head"),
        P(SEQ, None),
        P(SEQ, None),
        P("head", SEQ),
        P((*SEQ, *CAND), None),
        P((*SEQ, *CAND), None),
        P(),
    )
    out_specs = P(CAND, (*SEQ, "head"))
    return jax.shard_map(body, mesh=parts, in_specs=in_specs, out_specs=out_specs, check_vma=False)
```

time: 450 us -> 74.1 us (0.16)
  the two profiles are of different devices: /device:TPU:6 before, /device:TPU:8 now
where the time goes in v1:
time: 74.1 us; the launch traced here: 73.4 us
  blocking collectives  66.3 us (89%)
  Pallas kernels  4.98 us (7%)
  starting transfers between devices  1.92 us (3%)
    all_to_all x1, blocking collectives, body(): lax.all_to_all(partial.astype(jnp.float16), ('pair', 'side'), 0, 0, tiled...  20.5 us
    all_to_all x1, blocking collectives, body(): projected = lax.all_to_all(projected, 'head', 0, 0, tiled=True)  15 us
    all_to_all x1, blocking collectives, body(): lax.all_to_all(queries, ('side', 'lo', 'far'), 0, 0, tiled=True).astype(f32)  10.7 us
    all_to_all x1, blocking collectives, body(): state = lax.all_to_all(state, ('side', 'pair'), 0, 0, tiled=True)  10.5 us
    all_to_all x1, blocking collectives, body(): state = lax.all_to_all(state, ('far', 'side', 'lo'), 0, 0, tiled=True)  9.64 us
    ppermute x1, starting transfers between devices, body(): other = lax.ppermute(cache, 'core', [(0, 1), (1, 0)])  1.92 us
    pallas_call x1, Pallas kernels, body(): call(attend_kernel, jax.ShapeDtypeStruct((far, side, lo, tok_dev + ANS_LE...  1.82 us
    pallas_call x1, Pallas kernels, body(): pl.pallas_call(project_kernel, out_shape=(jax.ShapeDtypeStruct((pairs * s...  1.74 us
  transfers between devices with their start and end apart: 1, of which 0 were waited for; matrix products, arithmetic and copies ran while one was open for 0% of the time, Pallas kernels for 0%

profile of v1, /device:TPU:8, one launch (start us, length us, event | category | flops | bytes accessed | tf_op | source)
XLA Modules:
  0.0 73.4 jit_solution(16977260938650607436)
XLA Ops:
  0.0 1.7 %shard_map.82 = (f32[8,80,128]{2,1,0:T(8,128)S(1)}, f32[8,128]{1,0:T(8,128)S(1)}, bf16[2,2048,128]{2,1,0:T(8,128)(2,1)S(1)}) custom-call(bf16[64,1024]{1,0:T(8,128)(2,1)} %hidden_hbm.1, bf16[1024,256]{1,0:T(8,128)(2,1)} %query_hbm.1, bf16[1024,128]{1,0:T(8,128)(2,1)} %key_hbm.1, bf16[1024,128]{1,0:T(8,128)(2,1)} %value_hbm.1, s32[32]{0:T(128)} %group_hbm.1, ...), custom_call_target="tpu_custom_call" | custom-call | flops 67108864 | bytes 1179648 | tf_op jit(solution)/shard_map/pallas_call | solution.py:242
  1.7 1.9 %collective-permute-start = (bf16[2,2048,128]{2,1,0:T(8,128)(2,1)S(1)}, bf16[2,2048,128]{2,1,0:T(8,128)(2,1)S(1)}, u32[]{:S(2)}, u32[]{:S(2)}) collective-permute-start(bf16[2,2048,128]{2,1,0:T(8,128)(2,1)S(1)} %get-tuple-element.9.cache_ref), channel_id=1, source_target_pairs={{0,1},{1,0},{2,3},{3,2},{4,5},{5,4},{6,7},{7,6},{8,9},{9,8},{10,11... | collective-permute-start | bytes 3145736 | tf_op jit(solution)/shard_map/ppermute | solution.py:264
  3.7 20.5 %all_to_all.25 = f16[8,80,128]{2,1,0:T(8,128)(2,1)S(1)} all-to-all(f16[8,80,128]{2,1,0:T(8,128)(2,1)S(1)} %convert_element_type.12), channel_id=1, replica_groups=mesh['far'=2,'pair'=4,'side'=2,'head'=8,'lo'=2,'core'=2] {'pair','side'}, dimensions={0} | all-to-all | bytes 327680 | tf_op jit(solution)/shard_map/all_to_all | solution.py:265
  24.4 10.7 %all_to_all.26 = f16[8,80,128]{2,1,0:T(8,128)(2,1)S(1)} all-to-all(f16[8,80,128]{2,1,0:T(8,128)(2,1)S(1)} %convert_element_type.14), channel_id=1, replica_groups=mesh['far'=2,'pair'=4,'side'=2,'head'=8,'lo'=2,'core'=2] {'side','lo','f..., dimensions={0} | all-to-all | bytes 327680 | tf_op jit(solution)/shard_map/all_to_all | solution.py:276
  35.1 0.0 collective-permute-done.other_ref
  35.1 1.8 %shard_map.84 = bf16[2,2,2,72,128]{4,3,2,1,0:T(8,128)(2,1)S(1)} custom-call(f32[8,80,128]{2,1,0:T(8,128)S(1)} %convert_element_type.15.query_ref.own_ref, bf16[2,2048,128]{2,1,0:T(8,128)(2,1)S(1)} %get-tuple-element.9.cache_ref, bf16[2,2048,128]{2,1,0:T(8,128)(2,1)S(1)} %collective-permute-done.other_ref, f32[8,128]{1,0:T(8,128)S(1)} %get-tuple-element.10.bias_ref), custom_call_target="tpu_custom_call" | custom-call | flops 536870912 | bytes 2097152 | tf_op jit(solution)/shard_map/pallas_call | solution.py:277
  36.9 9.6 %all_to_all.27.state_ref = bf16[8,72,128]{2,1,0:T(8,128)(2,1)S(1)} all-to-all(bf16[8,72,128]{2,1,0:T(8,128)(2,1)S(1)} %bitcast.2), channel_id=1, replica_groups=mesh['far'=2,'pair'=4,'side'=2,'head'=8,'lo'=2,'core'=2] {'far','side','..., dimensions={0} | all-to-all | bytes 294912 | tf_op jit(solution)/shard_map/all_to_all | solution.py:286
  46.6 0.0 copy-start
  46.6 0.4 shard_map.85
  47.0 10.5 %all_to_all.28 = bf16[8,72,128]{2,1,0:T(8,128)(2,1)S(1)} all-to-all(bf16[8,72,128]{2,1,0:T(8,128)(2,1)S(1)} %shard_map.85), channel_id=1, replica_groups=mesh['far'=2,'pair'=4,'side'=2,'head'=8,'lo'=2,'core'=2] {'side','pair'}, dimensions={0} | all-to-all | bytes 294912 | tf_op jit(solution)/shard_map/all_to_all | solution.py:295
  57.5 0.0 copy-done
  57.5 0.3 shard_map.86
  57.8 15.0 %all_to_all.29.part_ref = bf16[8,64,128]{2,1,0:T(8,128)(2,1)S(1)} all-to-all(bf16[8,64,128]{2,1,0:T(8,128)(2,1)S(1)} %shard_map.86), channel_id=1, replica_groups=mesh['far'=2,'pair'=4,'side'=2,'head'=8,'lo'=2,'core'=2] {'head'}, dimensions={0} | all-to-all | bytes 262144 | tf_op jit(solution)/shard_map/all_to_all | solution.py:304
  72.8 0.6 shard_map.87
  (5 shorter events, 0.1 us)
Async XLA Ops:
  1.7 33.3 %collective-permute-start = (bf16[2,2048,128]{2,1,0:T(8,128)(2,1)S(1)}, bf16[2,2048,128]{2,1,0:T(8,128)(2,1)S(1)}, u32[]{:S(2)}, u32[]{:S(2)}) collective-permute-start(bf16[2,2048,128]{2,1,0:T(8,128)(2,1)S(1)} %get-tuple-element.9.cache_ref), channel_id=1, source_target_pairs={{0,1},{1,0},{2,3},{3,2},{4,5},{5,4},{6,7},{7,6},{8,9},{9,8},{10,11... | collective-permute-start | bytes 3145736 | tf_op jit(solution)/shard_map/ppermute | solution.py:264
  46.6 10.9 %copy-start = (bf16[256,1024]{1,0:T(8,128)(2,1)S(1)}, bf16[256,1024]{1,0:T(8,128)(2,1)}, u32[]{:S(2)}) copy-start(bf16[256,1024]{1,0:T(8,128)(2,1)} %weight_ref.1) | copy-start | bytes 1572868

commit v2 on v1

--- a/solution.py
+++ b/solution.py
@@ -10,7 +10,7 @@
 HD = 128
 GROUPS = 8
 ANS_LEN = 8
-ROW_BLOCK = 128
+KEY_BLOCK = 1024
 
 NEGATIVE = -1e30
 LOG2E = math.log2(math.e)
@@ -134,49 +134,49 @@
     far, side, lo, rows, _ = out_ref.shape
     rows -= ANS_LEN
     halves = far
-    sources = ROW_BLOCK // rows * halves
     cores = lax.axis_size("core")
     cands = rows // ANS_LEN
-    row = lax.broadcasted_iota(jnp.int32, (ROW_BLOCK, HD), 0)
-    lane = lax.broadcasted_iota(jnp.int32, (ROW_BLOCK, HD), 1)
-    caches = (cache_ref, other_ref)
-    steps = [(r, cache) for r in range(query_ref.shape[0] // sources) for cache in caches]
+    query = query_ref[:, :rows].reshape(side * lo, halves, rows, HD)
+    query = jnp.sum(query, axis=1).reshape(side * lo * rows, HD)
+    query = (query * (1 / SMALL_SCALE)).astype(jnp.bfloat16)
+    shard = cache_ref.shape[1]
+    steps = [
+        (cache, slice(start, start + KEY_BLOCK))
+        for cache in (cache_ref, other_ref)
+        for start in range(0, shard, KEY_BLOCK)
+    ]
 
     def scored(step):
-        r, cache = step
-        parts = query_ref[r * sources : (r + 1) * sources, :rows]
-        query = jnp.sum(parts.reshape(-1, halves, rows, HD), axis=1).reshape(ROW_BLOCK, HD)
-        query = (query * (1 / SMALL_SCALE)).astype(jnp.bfloat16)
-        return dot_transposed(query, cache[0])
+        cache, part = step
+        return dot_transposed(query, cache[0, part])
 
     ahead = scored(steps[0])
     held = []
-    for i, (r, cache) in enumerate(steps):
+    for i, (cache, part) in enumerate(steps):
         scores = ahead
         if i + 1 < len(steps):
             ahead = scored(steps[i + 1])
         top = jnp.max(scores, axis=1, keepdims=True)
         weights = jnp.exp2((scores - top) * (scale * LOG2E))
         total = jnp.sum(weights, axis=1, keepdims=True)
-        held.append((top * scale, total, dot(weights.astype(jnp.bfloat16), cache[1])))
-        if len(held) < len(caches):
-            continue
-        top = jnp.maximum(held[0][0], held[1][0])
-        factors = [jnp.exp(part[0] - top) for part in held]
-        total = held[0][1] * factors[0] + held[1][1] * factors[1]
-        mean = (held[0][2] * factors[0] + held[1][2] * factors[1]) / total
-        held = []
-        place = (row + r * ROW_BLOCK) // ANS_LEN
-        cand = place // cands % lo * cores + lax.axis_index("core")
-        candidate = cand * cands + place % cands
-        bias = jnp.sum(jnp.where(lane == candidate, bias_ref[0:1, :], 0.0), axis=1, keepdims=True)
-        level = top + jnp.log(total) + bias
-        for j in range(ROW_BLOCK // rows):
-            part = slice(j * rows, (j + 1) * rows)
-            state = packed(mean[part], level[part])
-            block = r * (ROW_BLOCK // rows) + j
-            for f in range(far):
-                out_ref[f, block // lo, block % lo] = state
+        held.append((top * scale, total, dot(weights.astype(jnp.bfloat16), cache[1, part])))
+    top = held[0][0]
+    for part in held[1:]:
+        top = jnp.maximum(top, part[0])
+    factors = [jnp.exp(part[0] - top) for part in held]
+    total = sum(part[1] * factor for part, factor in zip(held, factors))
+    mean = sum(part[2] * factor for part, factor in zip(held, factors)) / total
+    place = lax.broadcasted_iota(jnp.int32, mean.shape, 0) // ANS_LEN
+    lane = lax.broadcasted_iota(jnp.int32, mean.shape, 1)
+    cand = place // cands % lo * cores + lax.axis_index("core")
+    candidate = cand * cands + place % cands
+    bias = jnp.sum(jnp.where(lane == candidate, bias_ref[0:1, :], 0.0), axis=1, keepdims=True)
+    level = top + jnp.log(total) + bias
+    for block in range(side * lo):
+        part = slice(block * rows, (block + 1) * rows)
+        state = packed(mean[part], level[part])
+        for f in range(far):
+            out_ref[f, block // lo, block % lo] = state
 
 
 def merge_kernel(state_ref, own_ref, out_ref):
@@ -219,10 +219,6 @@
     out = dot(attention, weight_ref[...])
     for block in range(blocks):
         out_ref[block] = out[:, block * width : (block + 1) * width].astype(jnp.bfloat16)
-
-
-def sum_kernel(part_ref, out_ref):
-    out_ref[...] = jnp.sum(part_ref[...].astype(jnp.float32), axis=0).astype(out_ref.dtype)
 
 
 def body(
@@ -302,14 +298,7 @@
         transcendentals=0,
     )(state.reshape(side, pairs, tok_dev + ANS_LEN, HD), out_weight)
     projected = lax.all_to_all(projected, "head", 0, 0, tiled=True)
-    return call(
-        sum_kernel,
-        jax.ShapeDtypeStruct((tok_dev, columns), bf16),
-        [VMEM],
-        flops=projected.size,
-        bytes_accessed=2 * projected.size,
-        transcendentals=0,
-    )(projected)
+    return jnp.sum(projected.astype(f32), axis=0).astype(bf16)
 
 
 def solution(mesh):

time: 74.1 us -> 74.1 us (level)
  the two profiles are of different devices: /device:TPU:8 before, /device:TPU:64 now
where the time goes in v2:
time: 74.1 us; the launch traced here: 73.7 us
  blocking collectives  66.7 us (90%)
  Pallas kernels  4.31 us (6%)
  starting transfers between devices  1.92 us (3%)
    all_to_all x1, blocking collectives, body(): lax.all_to_all(partial.astype(jnp.float16), ('pair', 'side'), 0, 0, tiled...  18.7 us
    all_to_all x1, blocking collectives, body(): projected = lax.all_to_all(projected, 'head', 0, 0, tiled=True)  16 us
    all_to_all x1, blocking collectives, body(): state = lax.all_to_all(state, ('side', 'pair'), 0, 0, tiled=True)  11.6 us
    all_to_all x1, blocking collectives, body(): lax.all_to_all(queries, ('side', 'lo', 'far'), 0, 0, tiled=True).astype(f32)  10.9 us
    all_to_all x1, blocking collectives, body(): state = lax.all_to_all(state, ('far', 'side', 'lo'), 0, 0, tiled=True)  9.43 us
    ppermute x1, starting transfers between devices, body(): other = lax.ppermute(cache, 'core', [(0, 1), (1, 0)])  1.92 us
    pallas_call x1, Pallas kernels, body(): call(attend_kernel, jax.ShapeDtypeStruct((far, side, lo, tok_dev + ANS_LE...  1.78 us
    pallas_call x1, Pallas kernels, body(): pl.pallas_call(project_kernel, out_shape=(jax.ShapeDtypeStruct((pairs * s...  1.74 us
  transfers between devices with their start and end apart: 1, of which 0 were waited for; matrix products, arithmetic and copies ran while one was open for 0% of the time, Pallas kernels for 0%

profile of v2, /device:TPU:64, one launch (start us, length us, event | category | flops | bytes accessed | tf_op | source)
XLA Modules:
  0.0 73.7 jit_solution(4920026196873226291)
XLA Ops:
  0.0 1.7 %shard_map.82 = (f32[8,80,128]{2,1,0:T(8,128)S(1)}, f32[8,128]{1,0:T(8,128)S(1)}, bf16[2,2048,128]{2,1,0:T(8,128)(2,1)S(1)}) custom-call(bf16[64,1024]{1,0:T(8,128)(2,1)} %hidden_hbm.1, bf16[1024,256]{1,0:T(8,128)(2,1)} %query_hbm.1, bf16[1024,128]{1,0:T(8,128)(2,1)} %key_hbm.1, bf16[1024,128]{1,0:T(8,128)(2,1)} %value_hbm.1, s32[32]{0:T(128)} %group_hbm.1, ...), custom_call_target="tpu_custom_call" | custom-call | flops 67108864 | bytes 1179648 | tf_op jit(solution)/shard_map/pallas_call | solution.py:238
  1.7 1.9 %collective-permute-start = (bf16[2,2048,128]{2,1,0:T(8,128)(2,1)S(1)}, bf16[2,2048,128]{2,1,0:T(8,128)(2,1)S(1)}, u32[]{:S(2)}, u32[]{:S(2)}) collective-permute-start(bf16[2,2048,128]{2,1,0:T(8,128)(2,1)S(1)} %get-tuple-element.9.cache_ref), channel_id=1, source_target_pairs={{0,1},{1,0},{2,3},{3,2},{4,5},{5,4},{6,7},{7,6},{8,9},{9,8},{10,11... | collective-permute-start | bytes 3145736 | tf_op jit(solution)/shard_map/ppermute | solution.py:260
  3.7 18.7 %all_to_all.25 = f16[8,80,128]{2,1,0:T(8,128)(2,1)S(1)} all-to-all(f16[8,80,128]{2,1,0:T(8,128)(2,1)S(1)} %convert_element_type.14), channel_id=1, replica_groups=mesh['far'=2,'pair'=4,'side'=2,'head'=8,'lo'=2,'core'=2] {'pair','side'}, dimensions={0} | all-to-all | bytes 327680 | tf_op jit(solution)/shard_map/all_to_all | solution.py:261
  22.5 10.9 %all_to_all.26 = f16[8,80,128]{2,1,0:T(8,128)(2,1)S(1)} all-to-all(f16[8,80,128]{2,1,0:T(8,128)(2,1)S(1)} %convert_element_type.16), channel_id=1, replica_groups=mesh['far'=2,'pair'=4,'side'=2,'head'=8,'lo'=2,'core'=2] {'side','lo','f..., dimensions={0} | all-to-all | bytes 327680 | tf_op jit(solution)/shard_map/all_to_all | solution.py:272
  33.5 0.0 collective-permute-done.other_ref
  33.5 1.8 %shard_map.84 = bf16[2,2,2,72,128]{4,3,2,1,0:T(8,128)(2,1)S(1)} custom-call(f32[8,80,128]{2,1,0:T(8,128)S(1)} %convert_element_type.17.query_ref.own_ref, bf16[2,2048,128]{2,1,0:T(8,128)(2,1)S(1)} %get-tuple-element.9.cache_ref, bf16[2,2048,128]{2,1,0:T(8,128)(2,1)S(1)} %collective-permute-done.other_ref, f32[8,128]{1,0:T(8,128)S(1)} %get-tuple-element.10.bias_ref), custom_call_target="tpu_custom_call" | custom-call | flops 536870912 | bytes 2097152 | tf_op jit(solution)/shard_map/pallas_call | solution.py:273
  35.3 9.4 %all_to_all.27.state_ref = bf16[8,72,128]{2,1,0:T(8,128)(2,1)S(1)} all-to-all(bf16[8,72,128]{2,1,0:T(8,128)(2,1)S(1)} %bitcast.2), channel_id=1, replica_groups=mesh['far'=2,'pair'=4,'side'=2,'head'=8,'lo'=2,'core'=2] {'far','side','..., dimensions={0} | all-to-all | bytes 294912 | tf_op jit(solution)/shard_map/all_to_all | solution.py:282
  44.7 0.0 copy-start
  44.7 0.4 shard_map.85
  45.2 11.6 %all_to_all.28 = bf16[8,72,128]{2,1,0:T(8,128)(2,1)S(1)} all-to-all(bf16[8,72,128]{2,1,0:T(8,128)(2,1)S(1)} %shard_map.85), channel_id=1, replica_groups=mesh['far'=2,'pair'=4,'side'=2,'head'=8,'lo'=2,'core'=2] {'side','pair'}, dimensions={0} | all-to-all | bytes 294912 | tf_op jit(solution)/shard_map/all_to_all | solution.py:291
  56.8 0.0 copy-done
  56.8 0.3 shard_map.86
  57.1 16.0 %all_to_all.29 = bf16[8,64,128]{2,1,0:T(8,128)(2,1)S(1)} all-to-all(bf16[8,64,128]{2,1,0:T(8,128)(2,1)S(1)} %shard_map.86), channel_id=1, replica_groups=mesh['far'=2,'pair'=4,'side'=2,'head'=8,'lo'=2,'core'=2] {'head'}, dimensions={0} | all-to-all | bytes 262144 | tf_op jit(solution)/shard_map/all_to_all | solution.py:300
  73.1 0.6 reduce_sum.12
  (5 shorter events, 0.1 us)
Async XLA Ops:
  1.7 31.8 %collective-permute-start = (bf16[2,2048,128]{2,1,0:T(8,128)(2,1)S(1)}, bf16[2,2048,128]{2,1,0:T(8,128)(2,1)S(1)}, u32[]{:S(2)}, u32[]{:S(2)}) collective-permute-start(bf16[2,2048,128]{2,1,0:T(8,128)(2,1)S(1)} %get-tuple-element.9.cache_ref), channel_id=1, source_target_pairs={{0,1},{1,0},{2,3},{3,2},{4,5},{5,4},{6,7},{7,6},{8,9},{9,8},{10,11... | collective-permute-start | bytes 3145736 | tf_op jit(solution)/shard_map/ppermute | solution.py:260
  44.7 12.1 %copy-start = (bf16[256,1024]{1,0:T(8,128)(2,1)S(1)}, bf16[256,1024]{1,0:T(8,128)(2,1)}, u32[]{:S(2)}) copy-start(bf16[256,1024]{1,0:T(8,128)(2,1)} %weight_ref.1) | copy-start | bytes 1572868

commit v3 on v2

--- a/solution.py
+++ b/solution.py
@@ -24,11 +24,12 @@
 CAND = ("lo", "core")
 
 
-def call(kernel, out_shape, in_specs, **cost):
+def call(kernel, out_shape, in_specs, scratch=(), **cost):
     return pl.pallas_call(
         kernel,
         out_shape=out_shape,
         in_specs=in_specs,
+        scratch_shapes=scratch,
         out_specs=jax.tree.map(lambda _: VMEM, out_shape),
         compiler_params=pltpu.CompilerParams(vmem_limit_bytes=40 * 1024 * 1024),
         cost_estimate=pl.CostEstimate(**cost),
@@ -57,17 +58,25 @@
         copies.append(pltpu.make_async_copy(source, target, sems.at[len(copies)]))
         copies[-1].start()
 
+    start(group_hbm, group_smem)
     for half in halves:
         start(query_hbm.at[half, :], weight_ref.at[half, pl.ds(0, width)])
         start(hidden_hbm.at[:, half], hidden_ref.at[:, half])
         start(key_hbm.at[half, :], weight_ref.at[half, pl.ds(width, HD)])
         start(value_hbm.at[half, :], weight_ref.at[half, pl.ds(width + HD, HD)])
-    start(group_hbm, group_smem)
     start(key_cache, cache_hbm.at[0])
     start(value_cache, cache_hbm.at[1])
+    copies[0].wait()
+    chunk = lax.axis_index(SEQ) // (lax.axis_size(SEQ) // GROUPS)
+    lane = lax.broadcasted_iota(jnp.int32, bias_ref.shape, 1)
+    bias = jnp.zeros(bias_ref.shape, jnp.float32)
+    for c in range(group_smem.shape[0]):
+        hidden_by = jnp.where(group_smem[c] >= chunk, 0.0, NEGATIVE)
+        bias = jnp.where(lane == c, hidden_by, bias)
+    bias_ref[...] = bias
     total = None
     for i, half in enumerate(halves):
-        for copy in copies[4 * i : 4 * i + 4]:
+        for copy in copies[4 * i + 1 : 4 * i + 5]:
             copy.wait()
         part = dot(hidden_ref[:, half], weight_ref[half, :])
         total = part if total is None else total + part
@@ -82,14 +91,6 @@
             for f in range(far):
                 place = slice((f * pairs + p) * ANS_LEN, (f * pairs + p + 1) * ANS_LEN)
                 out_ref[p * side + s, tokens + f * ANS_LEN : tokens + (f + 1) * ANS_LEN] = part[place]
-    copies[-3].wait()
-    chunk = lax.axis_index(SEQ) // (lax.axis_size(SEQ) // GROUPS)
-    lane = lax.broadcasted_iota(jnp.int32, bias_ref.shape, 1)
-    bias = jnp.zeros(bias_ref.shape, jnp.float32)
-    for c in range(group_smem.shape[0]):
-        hidden_by = jnp.where(group_smem[c] >= chunk, 0.0, NEGATIVE)
-        bias = jnp.where(lane == c, hidden_by, bias)
-    bias_ref[...] = bias
     copies[-2].wait()
     copies[-1].wait()
 
@@ -129,7 +130,7 @@
     return jnp.sum(mean * factor, axis=0) / total, best + jnp.log(total)
 
 
-def attend_kernel(query_ref, cache_ref, other_ref, bias_ref, out_ref):
+def attend_kernel(query_ref, cache_ref, other_ref, bias_ref, out_ref, held_ref):
     scale = HD ** (-0.5)
     far, side, lo, rows, _ = out_ref.shape
     rows -= ANS_LEN
@@ -146,32 +147,28 @@
         for start in range(0, shard, KEY_BLOCK)
     ]
 
-    def scored(step):
-        cache, part = step
-        return dot_transposed(query, cache[0, part])
-
-    ahead = scored(steps[0])
-    held = []
+    top = None
     for i, (cache, part) in enumerate(steps):
-        scores = ahead
-        if i + 1 < len(steps):
-            ahead = scored(steps[i + 1])
-        top = jnp.max(scores, axis=1, keepdims=True)
-        weights = jnp.exp2((scores - top) * (scale * LOG2E))
-        total = jnp.sum(weights, axis=1, keepdims=True)
-        held.append((top * scale, total, dot(weights.astype(jnp.bfloat16), cache[1, part])))
-    top = held[0][0]
-    for part in held[1:]:
-        top = jnp.maximum(top, part[0])
-    factors = [jnp.exp(part[0] - top) for part in held]
-    total = sum(part[1] * factor for part, factor in zip(held, factors))
-    mean = sum(part[2] * factor for part, factor in zip(held, factors)) / total
+        scores = dot_transposed(query, cache[0, part])
+        held_ref[i] = scores
+        for lanes in range(0, KEY_BLOCK, HD):
+            piece = scores[:, lanes : lanes + HD]
+            top = piece if top is None else jnp.maximum(top, piece)
+    top = jnp.max(top, axis=1, keepdims=True)
+    total, mean = 0.0, 0.0
+    for i, (cache, part) in enumerate(steps):
+        weights = jnp.exp2((held_ref[i] - top) * (scale * LOG2E))
+        for lanes in range(0, KEY_BLOCK, HD):
+            total = total + weights[:, lanes : lanes + HD]
+        mean = mean + dot(weights.astype(jnp.bfloat16), cache[1, part])
+    total = jnp.sum(total, axis=1, keepdims=True)
+    mean = mean / total
     place = lax.broadcasted_iota(jnp.int32, mean.shape, 0) // ANS_LEN
     lane = lax.broadcasted_iota(jnp.int32, mean.shape, 1)
     cand = place // cands % lo * cores + lax.axis_index("core")
     candidate = cand * cands + place % cands
     bias = jnp.sum(jnp.where(lane == candidate, bias_ref[0:1, :], 0.0), axis=1, keepdims=True)
-    level = top + jnp.log(total) + bias
+    level = top * scale + jnp.log(total) + bias
     for block in range(side * lo):
         part = slice(block * rows, (block + 1) * rows)
         state = packed(mean[part], level[part])
@@ -274,6 +271,7 @@
         attend_kernel,
         jax.ShapeDtypeStruct((far, side, lo, tok_dev + ANS_LEN, HD), bf16),
         [VMEM] * 4,
+        [pltpu.VMEM((2 * shard_len // KEY_BLOCK, rows, KEY_BLOCK), f32)],
         flops=8 * rows * shard_len * HD,
         bytes_accessed=8 * shard_len * HD,
         transcendentals=2 * rows * shard_len,

time: 74.1 us -> 74.2 us (level)
  no operation moved by 1% of the time
where the time goes in v3:
time: 74.2 us; the launch traced here: 73.9 us
  blocking collectives  66.7 us (90%)
  Pallas kernels  4.48 us (6%)
  starting transfers between devices  1.92 us (3%)
    all_to_all x1, blocking collectives, body(): lax.all_to_all(partial.astype(jnp.float16), ('pair', 'side'), 0, 0, tiled...  18.7 us
    all_to_all x1, blocking collectives, body(): projected = lax.all_to_all(projected, 'head', 0, 0, tiled=True)  16 us
    all_to_all x1, blocking collectives, body(): state = lax.all_to_all(state, ('side', 'pair'), 0, 0, tiled=True)  11.6 us
    all_to_all x1, blocking collectives, body(): lax.all_to_all(queries, ('side', 'lo', 'far'), 0, 0, tiled=True).astype(f32)  10.9 us
    all_to_all x1, blocking collectives, body(): state = lax.all_to_all(state, ('far', 'side', 'lo'), 0, 0, tiled=True)  9.43 us
    pallas_call x1, Pallas kernels, body(): call(attend_kernel, jax.ShapeDtypeStruct((far, side, lo, tok_dev + ANS_LE...  1.98 us
    ppermute x1, starting transfers between devices, body(): other = lax.ppermute(cache, 'core', [(0, 1), (1, 0)])  1.92 us
    pallas_call x1, Pallas kernels, body(): pl.pallas_call(project_kernel, out_shape=(jax.ShapeDtypeStruct((pairs * s...  1.71 us
  transfers between devices with their start and end apart: 1, of which 0 were waited for; matrix products, arithmetic and copies ran while one was open for 0% of the time, Pallas kernels for 0%

profile of v3, /device:TPU:64, one launch (start us, length us, event | category | flops | bytes accessed | tf_op | source)
XLA Modules:
  0.0 73.9 jit_solution(13516696899184685482)
XLA Ops:
  0.0 1.7 %shard_map.82 = (f32[8,80,128]{2,1,0:T(8,128)S(1)}, f32[8,128]{1,0:T(8,128)S(1)}, bf16[2,2048,128]{2,1,0:T(8,128)(2,1)S(1)}) custom-call(bf16[64,1024]{1,0:T(8,128)(2,1)} %hidden_hbm.1, bf16[1024,256]{1,0:T(8,128)(2,1)} %query_hbm.1, bf16[1024,128]{1,0:T(8,128)(2,1)} %key_hbm.1, bf16[1024,128]{1,0:T(8,128)(2,1)} %value_hbm.1, s32[32]{0:T(128)} %group_hbm.1, ...), custom_call_target="tpu_custom_call" | custom-call | flops 67108864 | bytes 1179648 | tf_op jit(solution)/shard_map/pallas_call | solution.py:235
  1.7 1.9 %collective-permute-start = (bf16[2,2048,128]{2,1,0:T(8,128)(2,1)S(1)}, bf16[2,2048,128]{2,1,0:T(8,128)(2,1)S(1)}, u32[]{:S(2)}, u32[]{:S(2)}) collective-permute-start(bf16[2,2048,128]{2,1,0:T(8,128)(2,1)S(1)} %get-tuple-element.9.cache_ref), channel_id=1, source_target_pairs={{0,1},{1,0},{2,3},{3,2},{4,5},{5,4},{6,7},{7,6},{8,9},{9,8},{10,11... | collective-permute-start | bytes 3145736 | tf_op jit(solution)/shard_map/ppermute | solution.py:257
  3.7 18.7 %all_to_all.25 = f16[8,80,128]{2,1,0:T(8,128)(2,1)S(1)} all-to-all(f16[8,80,128]{2,1,0:T(8,128)(2,1)S(1)} %convert_element_type.14), channel_id=1, replica_groups=mesh['far'=2,'pair'=4,'side'=2,'head'=8,'lo'=2,'core'=2] {'pair','side'}, dimensions={0} | all-to-all | bytes 327680 | tf_op jit(solution)/shard_map/all_to_all | solution.py:258
  22.5 10.9 %all_to_all.26 = f16[8,80,128]{2,1,0:T(8,128)(2,1)S(1)} all-to-all(f16[8,80,128]{2,1,0:T(8,128)(2,1)S(1)} %convert_element_type.16), channel_id=1, replica_groups=mesh['far'=2,'pair'=4,'side'=2,'head'=8,'lo'=2,'core'=2] {'side','lo','f..., dimensions={0} | all-to-all | bytes 327680 | tf_op jit(solution)/shard_map/all_to_all | solution.py:269
  33.5 0.0 collective-permute-done.other_ref
  33.5 2.0 %shard_map.84 = bf16[2,2,2,72,128]{4,3,2,1,0:T(8,128)(2,1)S(1)} custom-call(f32[8,80,128]{2,1,0:T(8,128)S(1)} %convert_element_type.17.query_ref.own_ref, bf16[2,2048,128]{2,1,0:T(8,128)(2,1)S(1)} %get-tuple-element.9.cache_ref, bf16[2,2048,128]{2,1,0:T(8,128)(2,1)S(1)} %collective-permute-done.other_ref, f32[8,128]{1,0:T(8,128)S(1)} %get-tuple-element.10.bias_ref), custom_call_target="tpu_custom_call" | custom-call | flops 536870912 | bytes 2097152 | tf_op jit(solution)/shard_map/pallas_call | solution.py:270
  35.5 9.4 %all_to_all.27.state_ref = bf16[8,72,128]{2,1,0:T(8,128)(2,1)S(1)} all-to-all(bf16[8,72,128]{2,1,0:T(8,128)(2,1)S(1)} %bitcast.2), channel_id=1, replica_groups=mesh['far'=2,'pair'=4,'side'=2,'head'=8,'lo'=2,'core'=2] {'far','side','..., dimensions={0} | all-to-all | bytes 294912 | tf_op jit(solution)/shard_map/all_to_all | solution.py:280
  44.9 0.0 copy-start
  44.9 0.4 shard_map.85
  45.4 11.6 %all_to_all.28 = bf16[8,72,128]{2,1,0:T(8,128)(2,1)S(1)} all-to-all(bf16[8,72,128]{2,1,0:T(8,128)(2,1)S(1)} %shard_map.85), channel_id=1, replica_groups=mesh['far'=2,'pair'=4,'side'=2,'head'=8,'lo'=2,'core'=2] {'side','pair'}, dimensions={0} | all-to-all | bytes 294912 | tf_op jit(solution)/shard_map/all_to_all | solution.py:289
  57.0 0.0 copy-done
  57.0 0.3 shard_map.86
  57.3 16.0 %all_to_all.29 = bf16[8,64,128]{2,1,0:T(8,128)(2,1)S(1)} all-to-all(bf16[8,64,128]{2,1,0:T(8,128)(2,1)S(1)} %shard_map.86), channel_id=1, replica_groups=mesh['far'=2,'pair'=4,'side'=2,'head'=8,'lo'=2,'core'=2] {'head'}, dimensions={0} | all-to-all | bytes 262144 | tf_op jit(solution)/shard_map/all_to_all | solution.py:298
  73.3 0.6 reduce_sum.12
  (5 shorter events, 0.1 us)
Async XLA Ops:
  1.7 31.8 %collective-permute-start = (bf16[2,2048,128]{2,1,0:T(8,128)(2,1)S(1)}, bf16[2,2048,128]{2,1,0:T(8,128)(2,1)S(1)}, u32[]{:S(2)}, u32[]{:S(2)}) collective-permute-start(bf16[2,2048,128]{2,1,0:T(8,128)(2,1)S(1)} %get-tuple-element.9.cache_ref), channel_id=1, source_target_pairs={{0,1},{1,0},{2,3},{3,2},{4,5},{5,4},{6,7},{7,6},{8,9},{9,8},{10,11... | collective-permute-start | bytes 3145736 | tf_op jit(solution)/shard_map/ppermute | solution.py:257
  44.9 12.1 %copy-start = (bf16[256,1024]{1,0:T(8,128)(2,1)S(1)}, bf16[256,1024]{1,0:T(8,128)(2,1)}, u32[]{:S(2)}) copy-start(bf16[256,1024]{1,0:T(8,128)(2,1)} %weight_ref.1) | copy-start | bytes 1572868

commit v4 on v3

--- a/solution.py
+++ b/solution.py
@@ -10,7 +10,7 @@
 HD = 128
 GROUPS = 8
 ANS_LEN = 8
-KEY_BLOCK = 1024
+ROW_BLOCK = 128
 
 NEGATIVE = -1e30
 LOG2E = math.log2(math.e)
@@ -24,12 +24,11 @@
 CAND = ("lo", "core")
 
 
-def call(kernel, out_shape, in_specs, scratch=(), **cost):
+def call(kernel, out_shape, in_specs, **cost):
     return pl.pallas_call(
         kernel,
         out_shape=out_shape,
         in_specs=in_specs,
-        scratch_shapes=scratch,
         out_specs=jax.tree.map(lambda _: VMEM, out_shape),
         compiler_params=pltpu.CompilerParams(vmem_limit_bytes=40 * 1024 * 1024),
         cost_estimate=pl.CostEstimate(**cost),
@@ -130,57 +129,9 @@
     return jnp.sum(mean * factor, axis=0) / total, best + jnp.log(total)
 
 
-def attend_kernel(query_ref, cache_ref, other_ref, bias_ref, out_ref, held_ref):
-    scale = HD ** (-0.5)
-    far, side, lo, rows, _ = out_ref.shape
-    rows -= ANS_LEN
-    halves = far
-    cores = lax.axis_size("core")
-    cands = rows // ANS_LEN
-    query = query_ref[:, :rows].reshape(side * lo, halves, rows, HD)
-    query = jnp.sum(query, axis=1).reshape(side * lo * rows, HD)
-    query = (query * (1 / SMALL_SCALE)).astype(jnp.bfloat16)
-    shard = cache_ref.shape[1]
-    steps = [
-        (cache, slice(start, start + KEY_BLOCK))
-        for cache in (cache_ref, other_ref)
-        for start in range(0, shard, KEY_BLOCK)
-    ]
-
-    top = None
-    for i, (cache, part) in enumerate(steps):
-        scores = dot_transposed(query, cache[0, part])
-        held_ref[i] = scores
-        for lanes in range(0, KEY_BLOCK, HD):
-            piece = scores[:, lanes : lanes + HD]
-            top = piece if top is None else jnp.maximum(top, piece)
-    top = jnp.max(top, axis=1, keepdims=True)
-    total, mean = 0.0, 0.0
-    for i, (cache, part) in enumerate(steps):
-        weights = jnp.exp2((held_ref[i] - top) * (scale * LOG2E))
-        for lanes in range(0, KEY_BLOCK, HD):
-            total = total + weights[:, lanes : lanes + HD]
-        mean = mean + dot(weights.astype(jnp.bfloat16), cache[1, part])
-    total = jnp.sum(total, axis=1, keepdims=True)
-    mean = mean / total
-    place = lax.broadcasted_iota(jnp.int32, mean.shape, 0) // ANS_LEN
-    lane = lax.broadcasted_iota(jnp.int32, mean.shape, 1)
-    cand = place // cands % lo * cores + lax.axis_index("core")
-    candidate = cand * cands + place % cands
-    bias = jnp.sum(jnp.where(lane == candidate, bias_ref[0:1, :], 0.0), axis=1, keepdims=True)
-    level = top * scale + jnp.log(total) + bias
-    for block in range(side * lo):
-        part = slice(block * rows, (block + 1) * rows)
-        state = packed(mean[part], level[part])
-        for f in range(far):
-            out_ref[f, block // lo, block % lo] = state
-
-
-def merge_kernel(state_ref, own_ref, out_ref):
-    mean, level = merged(*unpacked(state_ref[...]))
-    halves, pairs, _ = (lax.axis_size(name) for name in SEQ)
-    rows = pairs * ANS_LEN
-    tokens = mean.shape[0]
+def own_state(own_ref, halves, pairs):
+    tokens = own_ref.shape[1] - halves * ANS_LEN
+    rows = tokens // halves
 
     def own(s, part, scale):
         place = (s * lax.axis_size("lo") + lax.axis_index("lo")) * halves
@@ -200,13 +151,64 @@
     top = jnp.max(scores, axis=1, keepdims=True)
     weights = jnp.where(shown, jnp.exp(scores - top), 0.0)
     total = jnp.sum(weights, axis=1, keepdims=True)
-    own_mean = dot(weights.astype(jnp.bfloat16), value) / total
-    own_level = top + jnp.log(total)
-    row = lax.broadcasted_iota(jnp.int32, level.shape, 0)
+    mean = dot(weights.astype(jnp.bfloat16), value) / total
+    row = lax.broadcasted_iota(jnp.int32, mean.shape, 0)
     mine = row // ANS_LEN % pairs == lax.axis_index("pair")
-    own_level = jnp.where(mine, own_level, NEGATIVE)
-    mean, level = merged(jnp.stack([mean, own_mean]), jnp.stack([level, own_level]))
-    out_ref[...] = jnp.broadcast_to(packed(mean, level)[None], out_ref.shape)
+    return mean, jnp.where(mine, jnp.broadcast_to(top + jnp.log(total), mean.shape), NEGATIVE)
+
+
+def attend_kernel(query_ref, cache_ref, other_ref, bias_ref, out_ref, own_ref):
+    scale = HD ** (-0.5)
+    far, side, lo, rows, _ = out_ref.shape
+    rows -= ANS_LEN
+    halves = far
+    sources = ROW_BLOCK // rows * halves
+    cores = lax.axis_size("core")
+    cands = rows // ANS_LEN
+    row = lax.broadcasted_iota(jnp.int32, (ROW_BLOCK, HD), 0)
+    lane = lax.broadcasted_iota(jnp.int32, (ROW_BLOCK, HD), 1)
+    caches = (cache_ref, other_ref)
+    blocks = query_ref.shape[0] // sources
+
+    def scored(r):
+        parts = query_ref[r * sources : (r + 1) * sources, :rows]
+        query = jnp.sum(parts.reshape(-1, halves, rows, HD), axis=1).reshape(ROW_BLOCK, HD)
+        query = (query * (1 / SMALL_SCALE)).astype(jnp.bfloat16)
+        return [dot_transposed(query, cache[0]) for cache in caches]
+
+    ahead = scored(0)
+    for r in range(blocks):
+        scores = ahead
+        if r + 1 < blocks:
+            ahead = scored(r + 1)
+        else:
+            own_ref[0], own_ref[1] = own_state(query_ref, halves, cands // halves)
+        top = jnp.maximum(*(jnp.max(part, axis=1, keepdims=True) for part in scores))
+        total, mean = 0.0, 0.0
+        for part, cache in zip(scores, caches):
+            weights = jnp.exp2((part - top) * (scale * LOG2E))
+            total = total + jnp.sum(weights, axis=1, keepdims=True)
+            mean = mean + dot(weights.astype(jnp.bfloat16), cache[1])
+        mean = mean / total
+        place = (row + r * ROW_BLOCK) // ANS_LEN
+        cand = place // cands % lo * cores + lax.axis_index("core")
+        candidate = cand * cands + place % cands
+        bias = jnp.sum(jnp.where(lane == candidate, bias_ref[0:1, :], 0.0), axis=1, keepdims=True)
+        level = top * scale + jnp.log(total) + bias
+        for j in range(ROW_BLOCK // rows):
+            part = slice(j * rows, (j + 1) * rows)
+            state = packed(mean[part], level[part])
+            block = r * (ROW_BLOCK // rows) + j
+            for f in range(far):
+                out_ref[f, block // lo, block % lo] = state
+
+
+def merge_kernel(state_ref, own_ref, out_ref):
+    mean, level = unpacked(state_ref[...])
+    mean = jnp.concatenate([mean, own_ref[0:1]], axis=0)
+    level = jnp.concatenate([level, own_ref[1:2, :, 0:1]], axis=0)
+    state = packed(*merged(mean, level))
+    out_ref[...] = jnp.broadcast_to(state[None], out_ref.shape)
 
 
 def output_kernel(state_ref, weight_ref, out_ref):
@@ -267,11 +269,13 @@
     )(partial.astype(f32))
     queries = queries.astype(jnp.float16)
     queries = lax.all_to_all(queries, ("side", "lo", "far"), 0, 0, tiled=True).astype(f32)
-    state = call(
+    state, own = call(
         attend_kernel,
-        jax.ShapeDtypeStruct((far, side, lo, tok_dev + ANS_LEN, HD), bf16),
+        (
+            jax.ShapeDtypeStruct((far, side, lo, tok_dev + ANS_LEN, HD), bf16),
+            jax.ShapeDtypeStruct((2, tok_dev, HD), f32),
+        ),
         [VMEM] * 4,
-        [pltpu.VMEM((2 * shard_len // KEY_BLOCK, rows, KEY_BLOCK), f32)],
         flops=8 * rows * shard_len * HD,
         bytes_accessed=8 * shard_len * HD,
         transcendentals=2 * rows * shard_len,
@@ -285,7 +289,7 @@
         flops=4 * state.size,
         bytes_accessed=2 * state.size,
         transcendentals=0,
-    )(state, queries)
+    )(state, own)
     state = lax.all_to_all(state, ("side", "pair"), 0, 0, tiled=True)
     projected = call(
         output_kernel,

time: 74.2 us -> 74.5 us (level)
  no operation moved by 1% of the time
where the time goes in v4:
time: 74.5 us; the launch traced here: 74.2 us
  blocking collectives  66.8 us (90%)
  Pallas kernels  4.63 us (6%)
  starting transfers between devices  1.92 us (3%)
    all_to_all x1, blocking collectives, body(): lax.all_to_all(partial.astype(jnp.float16), ('pair', 'side'), 0, 0, tiled...  18.7 us
    all_to_all x1, blocking collectives, body(): projected = lax.all_to_all(projected, 'head', 0, 0, tiled=True)  16 us
    all_to_all x1, blocking collectives, body(): state = lax.all_to_all(state, ('side', 'pair'), 0, 0, tiled=True)  11.6 us
    all_to_all x1, blocking collectives, body(): lax.all_to_all(queries, ('side', 'lo', 'far'), 0, 0, tiled=True).astype(f32)  10.9 us
    all_to_all x1, blocking collectives, body(): state = lax.all_to_all(state, ('far', 'side', 'lo'), 0, 0, tiled=True)  9.56 us
    pallas_call x1, Pallas kernels, body(): call(attend_kernel, (jax.ShapeDtypeStruct((far, side, lo, tok_dev + ANS_L...  2.19 us
    ppermute x1, starting transfers between devices, body(): other = lax.ppermute(cache, 'core', [(0, 1), (1, 0)])  1.92 us
    pallas_call x1, Pallas kernels, body(): pl.pallas_call(project_kernel, out_shape=(jax.ShapeDtypeStruct((pairs * s...  1.71 us
  transfers between devices with their start and end apart: 1, of which 0 were waited for; matrix products, arithmetic and copies ran while one was open for 0% of the time, Pallas kernels for 0%

profile of v4, /device:TPU:64, one launch (start us, length us, event | category | flops | bytes accessed | tf_op | source)
XLA Modules:
  0.0 74.2 jit_solution(14241934053103302157)
XLA Ops:
  0.0 1.7 %shard_map.82 = (f32[8,80,128]{2,1,0:T(8,128)S(1)}, f32[8,128]{1,0:T(8,128)S(1)}, bf16[2,2048,128]{2,1,0:T(8,128)(2,1)S(1)}) custom-call(bf16[64,1024]{1,0:T(8,128)(2,1)} %hidden_hbm.1, bf16[1024,256]{1,0:T(8,128)(2,1)} %query_hbm.1, bf16[1024,128]{1,0:T(8,128)(2,1)} %key_hbm.1, bf16[1024,128]{1,0:T(8,128)(2,1)} %value_hbm.1, s32[32]{0:T(128)} %group_hbm.1, ...), custom_call_target="tpu_custom_call" | custom-call | flops 67108864 | bytes 1179648 | tf_op jit(solution)/shard_map/pallas_call | solution.py:237
  1.7 1.9 %collective-permute-start = (bf16[2,2048,128]{2,1,0:T(8,128)(2,1)S(1)}, bf16[2,2048,128]{2,1,0:T(8,128)(2,1)S(1)}, u32[]{:S(2)}, u32[]{:S(2)}) collective-permute-start(bf16[2,2048,128]{2,1,0:T(8,128)(2,1)S(1)} %get-tuple-element.11.cache_ref), channel_id=1, source_target_pairs={{0,1},{1,0},{2,3},{3,2},{4,5},{5,4},{6,7},{7,6},{8,9},{9,8},{10,11... | collective-permute-start | bytes 3145736 | tf_op jit(solution)/shard_map/ppermute | solution.py:259
  3.7 18.7 %all_to_all.25 = f16[8,80,128]{2,1,0:T(8,128)(2,1)S(1)} all-to-all(f16[8,80,128]{2,1,0:T(8,128)(2,1)S(1)} %convert_element_type.14), channel_id=1, replica_groups=mesh['far'=2,'pair'=4,'side'=2,'head'=8,'lo'=2,'core'=2] {'pair','side'}, dimensions={0} | all-to-all | bytes 327680 | tf_op jit(solution)/shard_map/all_to_all | solution.py:260
  22.5 10.9 %all_to_all.26 = f16[8,80,128]{2,1,0:T(8,128)(2,1)S(1)} all-to-all(f16[8,80,128]{2,1,0:T(8,128)(2,1)S(1)} %convert_element_type.16), channel_id=1, replica_groups=mesh['far'=2,'pair'=4,'side'=2,'head'=8,'lo'=2,'core'=2] {'side','lo','f..., dimensions={0} | all-to-all | bytes 327680 | tf_op jit(solution)/shard_map/all_to_all | solution.py:271
  33.5 0.0 collective-permute-done.other_ref
  33.5 2.2 %shard_map.84 = (bf16[2,2,2,72,128]{4,3,2,1,0:T(8,128)(2,1)S(1)}, f32[2,64,128]{2,1,0:T(8,128)S(1)}) custom-call(f32[8,80,128]{2,1,0:T(8,128)S(1)} %convert_element_type.17.query_ref, bf16[2,2048,128]{2,1,0:T(8,128)(2,1)S(1)} %get-tuple-element.11.cache_ref, bf16[2,2048,128]{2,1,0:T(8,128)(2,1)S(1)} %collective-permute-done.other_ref, ...), custom_call_target="tpu_custom_call" | custom-call | flops 536870912 | bytes 2097152 | tf_op jit(solution)/shard_map/pallas_call | solution.py:272
  35.7 0.0 copy-start
  35.7 9.6 %all_to_all.27.state_ref = bf16[8,72,128]{2,1,0:T(8,128)(2,1)S(1)} all-to-all(bf16[8,72,128]{2,1,0:T(8,128)(2,1)S(1)} %bitcast.3), channel_id=1, replica_groups=mesh['far'=2,'pair'=4,'side'=2,'head'=8,'lo'=2,'core'=2] {'far','side','..., dimensions={0} | all-to-all | bytes 294912 | tf_op jit(solution)/shard_map/all_to_all | solution.py:284
  45.3 0.4 shard_map.85
  45.6 11.6 %all_to_all.28 = bf16[8,72,128]{2,1,0:T(8,128)(2,1)S(1)} all-to-all(bf16[8,72,128]{2,1,0:T(8,128)(2,1)S(1)} %shard_map.85), channel_id=1, replica_groups=mesh['far'=2,'pair'=4,'side'=2,'head'=8,'lo'=2,'core'=2] {'side','pair'}, dimensions={0} | all-to-all | bytes 294912 | tf_op jit(solution)/shard_map/all_to_all | solution.py:293
  57.3 0.0 copy-done
  57.3 0.3 shard_map.86
  57.6 16.0 %all_to_all.29 = bf16[8,64,128]{2,1,0:T(8,128)(2,1)S(1)} all-to-all(bf16[8,64,128]{2,1,0:T(8,128)(2,1)S(1)} %shard_map.86), channel_id=1, replica_groups=mesh['far'=2,'pair'=4,'side'=2,'head'=8,'lo'=2,'core'=2] {'head'}, dimensions={0} | all-to-all | bytes 262144 | tf_op jit(solution)/shard_map/all_to_all | solution.py:302
  73.6 0.6 reduce_sum.12
  (5 shorter events, 0.1 us)
Async XLA Ops:
  1.7 31.8 %collective-permute-start = (bf16[2,2048,128]{2,1,0:T(8,128)(2,1)S(1)}, bf16[2,2048,128]{2,1,0:T(8,128)(2,1)S(1)}, u32[]{:S(2)}, u32[]{:S(2)}) collective-permute-start(bf16[2,2048,128]{2,1,0:T(8,128)(2,1)S(1)} %get-tuple-element.11.cache_ref), channel_id=1, source_target_pairs={{0,1},{1,0},{2,3},{3,2},{4,5},{5,4},{6,7},{7,6},{8,9},{9,8},{10,11... | collective-permute-start | bytes 3145736 | tf_op jit(solution)/shard_map/ppermute | solution.py:259
  35.7 21.6 %copy-start = (bf16[256,1024]{1,0:T(8,128)(2,1)S(1)}, bf16[256,1024]{1,0:T(8,128)(2,1)}, u32[]{:S(2)}) copy-start(bf16[256,1024]{1,0:T(8,128)(2,1)} %weight_ref.1) | copy-start | bytes 1572868

commit v5 on v1

--- a/solution.py
+++ b/solution.py
@@ -131,21 +131,21 @@
 
 def attend_kernel(query_ref, cache_ref, other_ref, bias_ref, out_ref):
     scale = HD ** (-0.5)
-    far, side, lo, rows, _ = out_ref.shape
+    side, far, lo, rows, _ = out_ref.shape
     rows -= ANS_LEN
     halves = far
-    sources = ROW_BLOCK // rows * halves
+    assert ROW_BLOCK == lo * rows
     cores = lax.axis_size("core")
     cands = rows // ANS_LEN
     row = lax.broadcasted_iota(jnp.int32, (ROW_BLOCK, HD), 0)
     lane = lax.broadcasted_iota(jnp.int32, (ROW_BLOCK, HD), 1)
     caches = (cache_ref, other_ref)
-    steps = [(r, cache) for r in range(query_ref.shape[0] // sources) for cache in caches]
+    steps = [(r, cache) for r in range(side) for cache in caches]
 
     def scored(step):
         r, cache = step
-        parts = query_ref[r * sources : (r + 1) * sources, :rows]
-        query = jnp.sum(parts.reshape(-1, halves, rows, HD), axis=1).reshape(ROW_BLOCK, HD)
+        parts = query_ref[r * halves * lo : (r + 1) * halves * lo, :rows]
+        query = jnp.sum(parts.reshape(halves, lo, rows, HD), axis=0).reshape(ROW_BLOCK, HD)
         query = (query * (1 / SMALL_SCALE)).astype(jnp.bfloat16)
         return dot_transposed(query, cache[0])
 
@@ -171,12 +171,11 @@
         candidate = cand * cands + place % cands
         bias = jnp.sum(jnp.where(lane == candidate, bias_ref[0:1, :], 0.0), axis=1, keepdims=True)
         level = top + jnp.log(total) + bias
-        for j in range(ROW_BLOCK // rows):
+        for j in range(lo):
             part = slice(j * rows, (j + 1) * rows)
             state = packed(mean[part], level[part])
-            block = r * (ROW_BLOCK // rows) + j
             for f in range(far):
-                out_ref[f, block // lo, block % lo] = state
+                out_ref[r, f, j] = state
 
 
 def merge_kernel(state_ref, own_ref, out_ref):
@@ -186,10 +185,11 @@
     tokens = mean.shape[0]
 
     def own(s, part, scale):
-        place = (s * lax.axis_size("lo") + lax.axis_index("lo")) * halves
+        lo = lax.axis_size("lo")
+        place = s * halves * lo + lax.axis_index("lo")
         total = own_ref[place, part]
         for half in range(1, halves):
-            total = total + own_ref[place + half, part]
+            total = total + own_ref[place + half * lo, part]
         return (total * (1 / scale)).astype(jnp.bfloat16)
 
     query = own(lax.axis_index("side"), slice(0, tokens), SMALL_SCALE)
@@ -214,7 +214,7 @@
 
 def output_kernel(state_ref, weight_ref, out_ref):
     blocks, _, width = out_ref.shape
-    columns = [merged(*unpacked(state_ref[s]))[0] for s in range(state_ref.shape[0])]
+    columns = [merged(*unpacked(state_ref[:, s]))[0] for s in range(state_ref.shape[1])]
     attention = jnp.concatenate(columns, axis=1).astype(jnp.bfloat16)
     out = dot(attention, weight_ref[...])
     for block in range(blocks):
@@ -273,17 +273,17 @@
         transcendentals=0,
     )(partial.astype(f32))
     queries = queries.astype(jnp.float16)
-    queries = lax.all_to_all(queries, ("side", "lo", "far"), 0, 0, tiled=True).astype(f32)
+    queries = lax.all_to_all(queries, ("side", "far", "lo"), 0, 0, tiled=True).astype(f32)
     state = call(
         attend_kernel,
-        jax.ShapeDtypeStruct((far, side, lo, tok_dev + ANS_LEN, HD), bf16),
+        jax.ShapeDtypeStruct((side, far, lo, tok_dev + ANS_LEN, HD), bf16),
         [VMEM] * 4,
         flops=8 * rows * shard_len * HD,
         bytes_accessed=8 * shard_len * HD,
         transcendentals=2 * rows * shard_len,
     )(queries, cache, other, bias)
     state = state.reshape(near, tok_dev + ANS_LEN, HD)
-    state = lax.all_to_all(state, ("far", "side", "lo"), 0, 0, tiled=True)
+    state = lax.all_to_all(state, ("side", "far", "lo"), 0, 0, tiled=True)
     state = call(
         merge_kernel,
         jax.ShapeDtypeStruct((side * pairs, tok_dev + ANS_LEN, HD), bf16),
@@ -292,7 +292,7 @@
         bytes_accessed=2 * state.size,
         transcendentals=0,
     )(state, queries)
-    state = lax.all_to_all(state, ("side", "pair"), 0, 0, tiled=True)
+    state = lax.all_to_all(state, ("pair", "side"), 0, 0, tiled=True)
     projected = call(
         output_kernel,
         jax.ShapeDtypeStruct((head, tok_dev, columns), bf16),
@@ -300,7 +300,7 @@
         flops=2 * tok_dev * out_weight.size,
         bytes_accessed=2 * out_weight.size,
         transcendentals=0,
-    )(state.reshape(side, pairs, tok_dev + ANS_LEN, HD), out_weight)
+    )(state.reshape(pairs, side, tok_dev + ANS_LEN, HD), out_weight)
     projected = lax.all_to_all(projected, "head", 0, 0, tiled=True)
     return call(
         sum_kernel,

time: 74.1 us -> 74.6 us (level)
  blocking collectives: 66.3 us -> 67.2 us
    all_to_all x3, blocking collectives: 30.8 us -> 31.7 us  [the longest x1 11.6 us: body(): state = lax.all_to_all(state, ('pair', 'side'), 0, 0, tiled=True)]
where the time goes in v5:
time: 74.6 us; the launch traced here: 74.3 us
  blocking collectives  67.2 us (90%)
  Pallas kernels  4.99 us (7%)
  starting transfers between devices  1.92 us (3%)
    all_to_all x1, blocking collectives, body(): lax.all_to_all(partial.astype(jnp.float16), ('pair', 'side'), 0, 0, tiled...  20.5 us
    all_to_all x1, blocking collectives, body(): projected = lax.all_to_all(projected, 'head', 0, 0, tiled=True)  15 us
    all_to_all x1, blocking collectives, body(): state = lax.all_to_all(state, ('pair', 'side'), 0, 0, tiled=True)  11.6 us
    all_to_all x1, blocking collectives, body(): lax.all_to_all(queries, ('side', 'far', 'lo'), 0, 0, tiled=True).astype(f32)  10.9 us
    all_to_all x1, blocking collectives, body(): state = lax.all_to_all(state, ('side', 'far', 'lo'), 0, 0, tiled=True)  9.19 us
    ppermute x1, starting transfers between devices, body(): other = lax.ppermute(cache, 'core', [(0, 1), (1, 0)])  1.92 us
    pallas_call x1, Pallas kernels, body(): call(attend_kernel, jax.ShapeDtypeStruct((side, far, lo, tok_dev + ANS_LE...  1.82 us
    pallas_call x1, Pallas kernels, body(): pl.pallas_call(project_kernel, out_shape=(jax.ShapeDtypeStruct((pairs * s...  1.74 us
  transfers between devices with their start and end apart: 1, of which 0 were waited for; matrix products, arithmetic and copies ran while one was open for 0% of the time, Pallas kernels for 0%

profile of v5, /device:TPU:8, one launch (start us, length us, event | category | flops | bytes accessed | tf_op | source)
XLA Modules:
  0.0 74.3 jit_solution(1694522587488518754)
XLA Ops:
  0.0 1.7 %shard_map.82 = (f32[8,80,128]{2,1,0:T(8,128)S(1)}, f32[8,128]{1,0:T(8,128)S(1)}, bf16[2,2048,128]{2,1,0:T(8,128)(2,1)S(1)}) custom-call(bf16[64,1024]{1,0:T(8,128)(2,1)} %hidden_hbm.1, bf16[1024,256]{1,0:T(8,128)(2,1)} %query_hbm.1, bf16[1024,128]{1,0:T(8,128)(2,1)} %key_hbm.1, bf16[1024,128]{1,0:T(8,128)(2,1)} %value_hbm.1, s32[32]{0:T(128)} %group_hbm.1, ...), custom_call_target="tpu_custom_call" | custom-call | flops 67108864 | bytes 1179648 | tf_op jit(solution)/shard_map/pallas_call | solution.py:242
  1.7 1.9 %collective-permute-start = (bf16[2,2048,128]{2,1,0:T(8,128)(2,1)S(1)}, bf16[2,2048,128]{2,1,0:T(8,128)(2,1)S(1)}, u32[]{:S(2)}, u32[]{:S(2)}) collective-permute-start(bf16[2,2048,128]{2,1,0:T(8,128)(2,1)S(1)} %get-tuple-element.9.cache_ref), channel_id=1, source_target_pairs={{0,1},{1,0},{2,3},{3,2},{4,5},{5,4},{6,7},{7,6},{8,9},{9,8},{10,11... | collective-permute-start | bytes 3145736 | tf_op jit(solution)/shard_map/ppermute | solution.py:264
  3.7 20.5 %all_to_all.25 = f16[8,80,128]{2,1,0:T(8,128)(2,1)S(1)} all-to-all(f16[8,80,128]{2,1,0:T(8,128)(2,1)S(1)} %convert_element_type.12), channel_id=1, replica_groups=mesh['far'=2,'pair'=4,'side'=2,'head'=8,'lo'=2,'core'=2] {'pair','side'}, dimensions={0} | all-to-all | bytes 327680 | tf_op jit(solution)/shard_map/all_to_all | solution.py:265
  24.4 10.9 %all_to_all.26 = f16[8,80,128]{2,1,0:T(8,128)(2,1)S(1)} all-to-all(f16[8,80,128]{2,1,0:T(8,128)(2,1)S(1)} %convert_element_type.14), channel_id=1, replica_groups=mesh['far'=2,'pair'=4,'side'=2,'head'=8,'lo'=2,'core'=2] {'side','far','..., dimensions={0} | all-to-all | bytes 327680 | tf_op jit(solution)/shard_map/all_to_all | solution.py:276
  35.2 0.0 collective-permute-done.other_ref
  35.2 1.8 %shard_map.84 = bf16[2,2,2,72,128]{4,3,2,1,0:T(8,128)(2,1)S(1)} custom-call(f32[8,80,128]{2,1,0:T(8,128)S(1)} %convert_element_type.15.query_ref.own_ref, bf16[2,2048,128]{2,1,0:T(8,128)(2,1)S(1)} %get-tuple-element.9.cache_ref, bf16[2,2048,128]{2,1,0:T(8,128)(2,1)S(1)} %collective-permute-done.other_ref, f32[8,128]{1,0:T(8,128)S(1)} %get-tuple-element.10.bias_ref), custom_call_target="tpu_custom_call" | custom-call | flops 536870912 | bytes 2097152 | tf_op jit(solution)/shard_map/pallas_call | solution.py:277
  37.1 9.2 %all_to_all.27.state_ref = bf16[8,72,128]{2,1,0:T(8,128)(2,1)S(1)} all-to-all(bf16[8,72,128]{2,1,0:T(8,128)(2,1)S(1)} %bitcast.2), channel_id=1, replica_groups=mesh['far'=2,'pair'=4,'side'=2,'head'=8,'lo'=2,'core'=2] {'side','far','..., dimensions={0} | all-to-all | bytes 294912 | tf_op jit(solution)/shard_map/all_to_all | solution.py:286
  46.3 0.0 copy-start
  46.3 0.4 shard_map.85
  46.7 11.6 %all_to_all.28 = bf16[8,72,128]{2,1,0:T(8,128)(2,1)S(1)} all-to-all(bf16[8,72,128]{2,1,0:T(8,128)(2,1)S(1)} %shard_map.85), channel_id=1, replica_groups=mesh['far'=2,'pair'=4,'side'=2,'head'=8,'lo'=2,'core'=2] {'pair','side'}, dimensions={0} | all-to-all | bytes 294912 | tf_op jit(solution)/shard_map/all_to_all | solution.py:295
  58.4 0.0 copy-done
  58.4 0.3 shard_map.86
  58.7 15.0 %all_to_all.29.part_ref = bf16[8,64,128]{2,1,0:T(8,128)(2,1)S(1)} all-to-all(bf16[8,64,128]{2,1,0:T(8,128)(2,1)S(1)} %shard_map.86), channel_id=1, replica_groups=mesh['far'=2,'pair'=4,'side'=2,'head'=8,'lo'=2,'core'=2] {'head'}, dimensions={0} | all-to-all | bytes 262144 | tf_op jit(solution)/shard_map/all_to_all | solution.py:304
  73.7 0.6 shard_map.87
  (5 shorter events, 0.1 us)
Async XLA Ops:
  1.7 33.5 %collective-permute-start = (bf16[2,2048,128]{2,1,0:T(8,128)(2,1)S(1)}, bf16[2,2048,128]{2,1,0:T(8,128)(2,1)S(1)}, u32[]{:S(2)}, u32[]{:S(2)}) collective-permute-start(bf16[2,2048,128]{2,1,0:T(8,128)(2,1)S(1)} %get-tuple-element.9.cache_ref), channel_id=1, source_target_pairs={{0,1},{1,0},{2,3},{3,2},{4,5},{5,4},{6,7},{7,6},{8,9},{9,8},{10,11... | collective-permute-start | bytes 3145736 | tf_op jit(solution)/shard_map/ppermute | solution.py:264
  46.3 12.1 %copy-start = (bf16[256,1024]{1,0:T(8,128)(2,1)S(1)}, bf16[256,1024]{1,0:T(8,128)(2,1)}, u32[]{:S(2)}) copy-start(bf16[256,1024]{1,0:T(8,128)(2,1)} %weight_ref.1) | copy-start | bytes 1572868

commit v6 on v5

--- a/solution.py
+++ b/solution.py
@@ -20,7 +20,10 @@
 VMEM = pl.BlockSpec(memory_space=pltpu.VMEM)
 HBM = pl.BlockSpec(memory_space=pltpu.HBM)
 
-SEQ = ("far", "pair", "side")
+PAIR = ("high", "low")
+SEQ = ("far", *PAIR, "side")
+RING = ("side", *PAIR[::-1])
+HEAD = ("head2", "head1", "head0")
 CAND = ("lo", "core")
 
 
@@ -35,6 +38,13 @@
     )
 
 
+def reverse(place, count):
+    out = 0
+    while count > 1:
+        out, place, count = 2 * out + place % 2, place // 2, count // 2
+    return out
+
+
 def dot(a, b):
     return jnp.dot(a, b, preferred_element_type=jnp.float32)
 
@@ -47,7 +57,7 @@
     hidden_hbm, query_hbm, key_hbm, value_hbm, group_hbm, key_cache, value_cache,
     out_ref, bias_ref, cache_hbm, hidden_ref, weight_ref, group_smem, sems,
 ):
-    far, pairs, side = (lax.axis_size(name) for name in SEQ)
+    far, pairs, side = (lax.axis_size(name) for name in ("far", PAIR, "side"))
     features = hidden_ref.shape[1]
     width = query_hbm.shape[1]
     halves = [pl.ds(i * (features // 2), features // 2) for i in range(2)]
@@ -71,17 +81,18 @@
             copy.wait()
         part = dot(hidden_ref[:, half], weight_ref[half, :])
         total = part if total is None else total + part
-    ring = SMALL_SCALE * lax.axis_size("pair") * side
+    ring = SMALL_SCALE * lax.axis_size(PAIR) * side
     tokens = total.shape[0]
     for h in range(side):
         for p in range(pairs):
-            out_ref[p * side + h, :tokens] = total[:, h * HD : (h + 1) * HD] * ring
+            out_ref[h * pairs + p, :tokens] = total[:, h * HD : (h + 1) * HD] * ring
     for s, scale in ((0, ring * KEY_SCALE / SMALL_SCALE), (1, ring)):
         part = total[:, width + s * HD : width + (s + 1) * HD] * scale
         for p in range(pairs):
             for f in range(far):
                 place = slice((f * pairs + p) * ANS_LEN, (f * pairs + p + 1) * ANS_LEN)
-                out_ref[p * side + s, tokens + f * ANS_LEN : tokens + (f + 1) * ANS_LEN] = part[place]
+                target = s * pairs + reverse(p, pairs)
+                out_ref[target, tokens + f * ANS_LEN : tokens + (f + 1) * ANS_LEN] = part[place]
     copies[-3].wait()
     chunk = lax.axis_index(SEQ) // (lax.axis_size(SEQ) // GROUPS)
     lane = lax.broadcasted_iota(jnp.int32, bias_ref.shape, 1)
@@ -180,7 +191,7 @@
 
 def merge_kernel(state_ref, own_ref, out_ref):
     mean, level = merged(*unpacked(state_ref[...]))
-    halves, pairs, _ = (lax.axis_size(name) for name in SEQ)
+    halves, pairs = lax.axis_size("far"), lax.axis_size(PAIR)
     rows = pairs * ANS_LEN
     tokens = mean.shape[0]
 
@@ -206,7 +217,7 @@
     own_mean = dot(weights.astype(jnp.bfloat16), value) / total
     own_level = top + jnp.log(total)
     row = lax.broadcasted_iota(jnp.int32, level.shape, 0)
-    mine = row // ANS_LEN % pairs == lax.axis_index("pair")
+    mine = row // ANS_LEN % pairs == lax.axis_index(PAIR)
     own_level = jnp.where(mine, own_level, NEGATIVE)
     mean, level = merged(jnp.stack([mean, own_mean]), jnp.stack([level, own_level]))
     out_ref[...] = jnp.broadcast_to(packed(mean, level)[None], out_ref.shape)
@@ -214,11 +225,12 @@
 
 def output_kernel(state_ref, weight_ref, out_ref):
     blocks, _, width = out_ref.shape
-    columns = [merged(*unpacked(state_ref[:, s]))[0] for s in range(state_ref.shape[1])]
+    columns = [merged(*unpacked(state_ref[s]))[0] for s in range(state_ref.shape[0])]
     attention = jnp.concatenate(columns, axis=1).astype(jnp.bfloat16)
     out = dot(attention, weight_ref[...])
     for block in range(blocks):
-        out_ref[block] = out[:, block * width : (block + 1) * width].astype(jnp.bfloat16)
+        place = reverse(block, blocks)
+        out_ref[block] = out[:, place * width : (place + 1) * width].astype(jnp.bfloat16)
 
 
 def sum_kernel(part_ref, out_ref):
@@ -230,8 +242,8 @@
 ):
     tok_dev, feat_dev = hidden.shape
     heads_dev = query_weight.shape[1] // HD
-    head, lo = lax.axis_size("head"), lax.axis_size("lo")
-    far, pairs, side = (lax.axis_size(name) for name in SEQ)
+    head, lo = lax.axis_size(HEAD), lax.axis_size("lo")
+    far, pairs, side = (lax.axis_size(name) for name in ("far", PAIR, "side"))
     shard_len = key_cache.shape[0]
     bf16, f32 = jnp.bfloat16, jnp.float32
     rows = tok_dev * heads_dev * lo
@@ -262,7 +274,7 @@
         ),
     )(*inputs)
     other = lax.ppermute(cache, "core", [(0, 1), (1, 0)])
-    partial = lax.all_to_all(partial.astype(jnp.float16), ("pair", "side"), 0, 0, tiled=True)
+    partial = lax.all_to_all(partial.astype(jnp.float16), RING, 0, 0, tiled=True)
     near = far * side * lo
     queries = call(
         reduce_kernel,
@@ -292,7 +304,7 @@
         bytes_accessed=2 * state.size,
         transcendentals=0,
     )(state, queries)
-    state = lax.all_to_all(state, ("pair", "side"), 0, 0, tiled=True)
+    state = lax.all_to_all(state, RING, 0, 0, tiled=True)
     projected = call(
         output_kernel,
         jax.ShapeDtypeStruct((head, tok_dev, columns), bf16),
@@ -300,8 +312,8 @@
         flops=2 * tok_dev * out_weight.size,
         bytes_accessed=2 * out_weight.size,
         transcendentals=0,
-    )(state.reshape(pairs, side, tok_dev + ANS_LEN, HD), out_weight)
-    projected = lax.all_to_all(projected, "head", 0, 0, tiled=True)
+    )(state.reshape(side, pairs, tok_dev + ANS_LEN, HD), out_weight)
+    projected = lax.all_to_all(projected, HEAD[::-1], 0, 0, tiled=True)
     return call(
         sum_kernel,
         jax.ShapeDtypeStruct((tok_dev, columns), bf16),
@@ -315,17 +327,18 @@
 def solution(mesh):
     seq, head, cand = (mesh.shape[name] for name in ("seq", "head", "cand"))
     parts = jax.sharding.Mesh(
-        mesh.devices.reshape(2, seq // 4, 2, head, cand // 2, 2), (*SEQ, "head", *CAND)
+        mesh.devices.reshape(2, seq // 8, 2, 2, head // 4, 2, 2, cand // 2, 2),
+        (*SEQ, *HEAD, *CAND),
     )
     in_specs = (
         P(CAND, SEQ),
-        P(SEQ, "head"),
+        P(SEQ, HEAD),
         P(SEQ, None),
         P(SEQ, None),
-        P("head", SEQ),
+        P(HEAD, SEQ),
         P((*SEQ, *CAND), None),
         P((*SEQ, *CAND), None),
         P(),
     )
-    out_specs = P(CAND, (*SEQ, "head"))
+    out_specs = P(CAND, (*SEQ, *HEAD))
     return jax.shard_map(body, mesh=parts, in_specs=in_specs, out_specs=out_specs, check_vma=False)

time: 74.6 us -> 72.4 us (0.971)
  blocking collectives: 67.2 us -> 65 us
    all_to_all x3, blocking collectives: 47.2 us -> 43.7 us  [the longest x1 18.4 us: body(): lax.all_to_all(partial.astype(jnp.float16), RING, 0, 0, tiled=True)]
    all_to_all x1, blocking collectives: 10.9 us -> 12.1 us  [body(): lax.all_to_all(queries, ('side', 'far', 'lo'), 0, 0, tiled=True).astype(f32)]
where the time goes in v6:
time: 72.4 us; the launch traced here: 72.1 us
  blocking collectives  65 us (90%)
  Pallas kernels  4.98 us (7%)
  starting transfers between devices  1.92 us (3%)
    all_to_all x1, blocking collectives, body(): lax.all_to_all(partial.astype(jnp.float16), RING, 0, 0, tiled=True)  18.4 us
    all_to_all x1, blocking collectives, body(): projected = lax.all_to_all(projected, HEAD[::-1], 0, 0, tiled=True)  14.2 us
    all_to_all x1, blocking collectives, body(): lax.all_to_all(queries, ('side', 'far', 'lo'), 0, 0, tiled=True).astype(f32)  12.1 us
    all_to_all x1, blocking collectives, body(): state = lax.all_to_all(state, RING, 0, 0, tiled=True)  11.1 us
    all_to_all x1, blocking collectives, body(): state = lax.all_to_all(state, ('side', 'far', 'lo'), 0, 0, tiled=True)  9.2 us
    ppermute x1, starting transfers between devices, body(): other = lax.ppermute(cache, 'core', [(0, 1), (1, 0)])  1.92 us
    pallas_call x1, Pallas kernels, body(): call(attend_kernel, jax.ShapeDtypeStruct((side, far, lo, tok_dev + ANS_LE...  1.82 us
    pallas_call x1, Pallas kernels, body(): pl.pallas_call(project_kernel, out_shape=(jax.ShapeDtypeStruct((pairs * s...  1.74 us
  transfers between devices with their start and end apart: 1, of which 0 were waited for; matrix products, arithmetic and copies ran while one was open for 0% of the time, Pallas kernels for 0%

profile of v6, /device:TPU:8, one launch (start us, length us, event | category | flops | bytes accessed | tf_op | source)
XLA Modules:
  0.0 72.1 jit_solution(3310752313132678683)
XLA Ops:
  0.0 1.7 %shard_map.82 = (f32[8,80,128]{2,1,0:T(8,128)S(1)}, f32[8,128]{1,0:T(8,128)S(1)}, bf16[2,2048,128]{2,1,0:T(8,128)(2,1)S(1)}) custom-call(bf16[64,1024]{1,0:T(8,128)(2,1)} %hidden_hbm.1, bf16[1024,256]{1,0:T(8,128)(2,1)} %query_hbm.1, bf16[1024,128]{1,0:T(8,128)(2,1)} %key_hbm.1, bf16[1024,128]{1,0:T(8,128)(2,1)} %value_hbm.1, s32[32]{0:T(128)} %group_hbm.1, ...), custom_call_target="tpu_custom_call" | custom-call | flops 67108864 | bytes 1179648 | tf_op jit(solution)/shard_map/pallas_call | solution.py:254
  1.8 1.9 %collective-permute-start = (bf16[2,2048,128]{2,1,0:T(8,128)(2,1)S(1)}, bf16[2,2048,128]{2,1,0:T(8,128)(2,1)S(1)}, u32[]{:S(2)}, u32[]{:S(2)}) collective-permute-start(bf16[2,2048,128]{2,1,0:T(8,128)(2,1)S(1)} %get-tuple-element.9.cache_ref), channel_id=1, source_target_pairs={{0,1},{1,0},{2,3},{3,2},{4,5},{5,4},{6,7},{7,6},{8,9},{9,8},{10,11... | collective-permute-start | bytes 3145736 | tf_op jit(solution)/shard_map/ppermute | solution.py:276
  3.7 18.4 %all_to_all.25 = f16[8,80,128]{2,1,0:T(8,128)(2,1)S(1)} all-to-all(f16[8,80,128]{2,1,0:T(8,128)(2,1)S(1)} %convert_element_type.12), channel_id=1, replica_groups=mesh['far'=2,'high'=2,'low'=2,'side'=2,'head2'=2,'head1'=2,'head0'=2,'lo..., dimensions={0} | all-to-all | bytes 327680 | tf_op jit(solution)/shard_map/all_to_all | solution.py:277
  22.2 12.1 %all_to_all.26 = f16[8,80,128]{2,1,0:T(8,128)(2,1)S(1)} all-to-all(f16[8,80,128]{2,1,0:T(8,128)(2,1)S(1)} %convert_element_type.14), channel_id=1, replica_groups=mesh['far'=2,'high'=2,'low'=2,'side'=2,'head2'=2,'head1'=2,'head0'=2,'lo..., dimensions={0} | all-to-all | bytes 327680 | tf_op jit(solution)/shard_map/all_to_all | solution.py:288
  34.3 0.0 collective-permute-done.other_ref
  34.3 1.8 %shard_map.84 = bf16[2,2,2,72,128]{4,3,2,1,0:T(8,128)(2,1)S(1)} custom-call(f32[8,80,128]{2,1,0:T(8,128)S(1)} %convert_element_type.15.query_ref.own_ref, bf16[2,2048,128]{2,1,0:T(8,128)(2,1)S(1)} %get-tuple-element.9.cache_ref, bf16[2,2048,128]{2,1,0:T(8,128)(2,1)S(1)} %collective-permute-done.other_ref, f32[8,128]{1,0:T(8,128)S(1)} %get-tuple-element.10.bias_ref), custom_call_target="tpu_custom_call" | custom-call | flops 536870912 | bytes 2097152 | tf_op jit(solution)/shard_map/pallas_call | solution.py:289
  36.1 9.2 %all_to_all.27.state_ref = bf16[8,72,128]{2,1,0:T(8,128)(2,1)S(1)} all-to-all(bf16[8,72,128]{2,1,0:T(8,128)(2,1)S(1)} %bitcast.2), channel_id=1, replica_groups=mesh['far'=2,'high'=2,'low'=2,'side'=2,'head2'=2,'head1'=2,'head0'=2,'lo..., dimensions={0} | all-to-all | bytes 294912 | tf_op jit(solution)/shard_map/all_to_all | solution.py:298
  45.3 0.0 copy-start
  45.3 0.4 shard_map.85
  45.8 11.1 %all_to_all.28 = bf16[8,72,128]{2,1,0:T(8,128)(2,1)S(1)} all-to-all(bf16[8,72,128]{2,1,0:T(8,128)(2,1)S(1)} %shard_map.85), channel_id=1, replica_groups=mesh['far'=2,'high'=2,'low'=2,'side'=2,'head2'=2,'head1'=2,'head0'=2,'lo..., dimensions={0} | all-to-all | bytes 294912 | tf_op jit(solution)/shard_map/all_to_all | solution.py:307
  56.9 0.0 copy-done
  56.9 0.3 shard_map.86
  57.2 14.2 %all_to_all.29.part_ref = bf16[8,64,128]{2,1,0:T(8,128)(2,1)S(1)} all-to-all(bf16[8,64,128]{2,1,0:T(8,128)(2,1)S(1)} %shard_map.86), channel_id=1, replica_groups=mesh['far'=2,'high'=2,'low'=2,'side'=2,'head2'=2,'head1'=2,'head0'=2,'lo..., dimensions={0} | all-to-all | bytes 262144 | tf_op jit(solution)/shard_map/all_to_all | solution.py:316
  71.4 0.6 shard_map.87
  (5 shorter events, 0.1 us)
Async XLA Ops:
  1.8 32.6 %collective-permute-start = (bf16[2,2048,128]{2,1,0:T(8,128)(2,1)S(1)}, bf16[2,2048,128]{2,1,0:T(8,128)(2,1)S(1)}, u32[]{:S(2)}, u32[]{:S(2)}) collective-permute-start(bf16[2,2048,128]{2,1,0:T(8,128)(2,1)S(1)} %get-tuple-element.9.cache_ref), channel_id=1, source_target_pairs={{0,1},{1,0},{2,3},{3,2},{4,5},{5,4},{6,7},{7,6},{8,9},{9,8},{10,11... | collective-permute-start | bytes 3145736 | tf_op jit(solution)/shard_map/ppermute | solution.py:276
  45.3 11.6 %copy-start = (bf16[256,1024]{1,0:T(8,128)(2,1)S(1)}, bf16[256,1024]{1,0:T(8,128)(2,1)}, u32[]{:S(2)}) copy-start(bf16[256,1024]{1,0:T(8,128)(2,1)} %weight_ref.1) | copy-start | bytes 1572868

commit v7 on v6

--- a/solution.py
+++ b/solution.py
@@ -22,9 +22,11 @@
 
 PAIR = ("high", "low")
 SEQ = ("far", *PAIR, "side")
-RING = ("side", *PAIR[::-1])
 HEAD = ("head2", "head1", "head0")
 CAND = ("lo", "core")
+RING = ("low", "side", "high")
+HEAD_RING = ("head1", "head0", "head2")
+NEAR = ("lo", "side", "far")
 
 
 def call(kernel, out_shape, in_specs, **cost):
@@ -38,11 +40,19 @@
     )
 
 
-def reverse(place, count):
-    out = 0
-    while count > 1:
-        out, place, count = 2 * out + place % 2, place // 2, count // 2
-    return out
+def counted(order, **at):
+    place = 0
+    for name in order:
+        place = place * lax.axis_size(name) + at[name]
+    return place
+
+
+def coordinates(names, place):
+    at = {}
+    for name in reversed(names):
+        at[name] = place % lax.axis_size(name)
+        place //= lax.axis_size(name)
+    return at
 
 
 def dot(a, b):
@@ -85,13 +95,14 @@
     tokens = total.shape[0]
     for h in range(side):
         for p in range(pairs):
-            out_ref[h * pairs + p, :tokens] = total[:, h * HD : (h + 1) * HD] * ring
+            target = counted(RING, side=h, **coordinates(PAIR, p))
+            out_ref[target, :tokens] = total[:, h * HD : (h + 1) * HD] * ring
     for s, scale in ((0, ring * KEY_SCALE / SMALL_SCALE), (1, ring)):
         part = total[:, width + s * HD : width + (s + 1) * HD] * scale
         for p in range(pairs):
             for f in range(far):
                 place = slice((f * pairs + p) * ANS_LEN, (f * pairs + p + 1) * ANS_LEN)
-                target = s * pairs + reverse(p, pairs)
+                target = counted(RING, side=s, **coordinates(PAIR, p))
                 out_ref[target, tokens + f * ANS_LEN : tokens + (f + 1) * ANS_LEN] = part[place]
     copies[-3].wait()
     chunk = lax.axis_index(SEQ) // (lax.axis_size(SEQ) // GROUPS)
@@ -142,9 +153,8 @@
 
 def attend_kernel(query_ref, cache_ref, other_ref, bias_ref, out_ref):
     scale = HD ** (-0.5)
-    side, far, lo, rows, _ = out_ref.shape
-    rows -= ANS_LEN
-    halves = far
+    rows = out_ref.shape[1] - ANS_LEN
+    far, side, lo = (lax.axis_size(name) for name in ("far", "side", "lo"))
     assert ROW_BLOCK == lo * rows
     cores = lax.axis_size("core")
     cands = rows // ANS_LEN
@@ -155,9 +165,11 @@
 
     def scored(step):
         r, cache = step
-        parts = query_ref[r * halves * lo : (r + 1) * halves * lo, :rows]
-        query = jnp.sum(parts.reshape(halves, lo, rows, HD), axis=0).reshape(ROW_BLOCK, HD)
-        query = (query * (1 / SMALL_SCALE)).astype(jnp.bfloat16)
+        parts = [
+            sum(query_ref[counted(NEAR, side=r, lo=j, far=half), :rows] for half in range(far))
+            for j in range(lo)
+        ]
+        query = (jnp.concatenate(parts, axis=0) * (1 / SMALL_SCALE)).astype(jnp.bfloat16)
         return dot_transposed(query, cache[0])
 
     ahead = scored(steps[0])
@@ -186,7 +198,7 @@
             part = slice(j * rows, (j + 1) * rows)
             state = packed(mean[part], level[part])
             for f in range(far):
-                out_ref[r, f, j] = state
+                out_ref[counted(NEAR, side=r, lo=j, far=f)] = state
 
 
 def merge_kernel(state_ref, own_ref, out_ref):
@@ -196,11 +208,8 @@
     tokens = mean.shape[0]
 
     def own(s, part, scale):
-        lo = lax.axis_size("lo")
-        place = s * halves * lo + lax.axis_index("lo")
-        total = own_ref[place, part]
-        for half in range(1, halves):
-            total = total + own_ref[place + half * lo, part]
+        lo = lax.axis_index("lo")
+        total = sum(own_ref[counted(NEAR, side=s, lo=lo, far=half), part] for half in range(halves))
         return (total * (1 / scale)).astype(jnp.bfloat16)
 
     query = own(lax.axis_index("side"), slice(0, tokens), SMALL_SCALE)
@@ -225,12 +234,16 @@
 
 def output_kernel(state_ref, weight_ref, out_ref):
     blocks, _, width = out_ref.shape
-    columns = [merged(*unpacked(state_ref[s]))[0] for s in range(state_ref.shape[0])]
+    pairs, side = lax.axis_size(PAIR), lax.axis_size("side")
+    columns = []
+    for h in range(side):
+        sources = [counted(RING, side=h, **coordinates(PAIR, p)) for p in range(pairs)]
+        columns.append(merged(*unpacked(jnp.stack([state_ref[place] for place in sources])))[0])
     attention = jnp.concatenate(columns, axis=1).astype(jnp.bfloat16)
     out = dot(attention, weight_ref[...])
     for block in range(blocks):
-        place = reverse(block, blocks)
-        out_ref[block] = out[:, place * width : (place + 1) * width].astype(jnp.bfloat16)
+        place = counted(HEAD_RING, **coordinates(HEAD, block))
+        out_ref[place] = out[:, block * width : (block + 1) * width].astype(jnp.bfloat16)
 
 
 def sum_kernel(part_ref, out_ref):
@@ -285,17 +298,16 @@
         transcendentals=0,
     )(partial.astype(f32))
     queries = queries.astype(jnp.float16)
-    queries = lax.all_to_all(queries, ("side", "far", "lo"), 0, 0, tiled=True).astype(f32)
+    queries = lax.all_to_all(queries, NEAR, 0, 0, tiled=True).astype(f32)
     state = call(
         attend_kernel,
-        jax.ShapeDtypeStruct((side, far, lo, tok_dev + ANS_LEN, HD), bf16),
+        jax.ShapeDtypeStruct((near, tok_dev + ANS_LEN, HD), bf16),
         [VMEM] * 4,
         flops=8 * rows * shard_len * HD,
         bytes_accessed=8 * shard_len * HD,
         transcendentals=2 * rows * shard_len,
     )(queries, cache, other, bias)
-    state = state.reshape(near, tok_dev + ANS_LEN, HD)
-    state = lax.all_to_all(state, ("side", "far", "lo"), 0, 0, tiled=True)
+    state = lax.all_to_all(state, NEAR, 0, 0, tiled=True)
     state = call(
         merge_kernel,
         jax.ShapeDtypeStruct((side * pairs, tok_dev + ANS_LEN, HD), bf16),
@@ -312,8 +324,8 @@
         flops=2 * tok_dev * out_weight.size,
         bytes_accessed=2 * out_weight.size,
         transcendentals=0,
-    )(state.reshape(side, pairs, tok_dev + ANS_LEN, HD), out_weight)
-    projected = lax.all_to_all(projected, HEAD[::-1], 0, 0, tiled=True)
+    )(state, out_weight)
+    projected = lax.all_to_all(projected, HEAD_RING, 0, 0, tiled=True)
     return call(
         sum_kernel,
         jax.ShapeDtypeStruct((tok_dev, columns), bf16),

time: 72.4 us -> 73.5 us (1.015)
  blocking collectives: 65 us -> 66.1 us
    all_to_all x3, blocking collectives: 35.5 us -> 36.8 us  [the longest x1 14.8 us: body(): projected = lax.all_to_all(projected, HEAD_RING, 0, 0, tiled=True)]
where the time goes in v7:
time: 73.5 us; the launch traced here: 73.2 us
  blocking collectives  66.1 us (90%)
  Pallas kernels  4.99 us (7%)
  starting transfers between devices  1.92 us (3%)
    all_to_all x1, blocking collectives, body(): lax.all_to_all(partial.astype(jnp.float16), RING, 0, 0, tiled=True)  18.6 us
    all_to_all x1, blocking collectives, body(): projected = lax.all_to_all(projected, HEAD_RING, 0, 0, tiled=True)  14.8 us
    all_to_all x1, blocking collectives, body(): queries = lax.all_to_all(queries, NEAR, 0, 0, tiled=True).astype(f32)  12.8 us
    all_to_all x1, blocking collectives, body(): state = lax.all_to_all(state, RING, 0, 0, tiled=True)  10.7 us
    all_to_all x1, blocking collectives, body(): state = lax.all_to_all(state, NEAR, 0, 0, tiled=True)  9.26 us
    ppermute x1, starting transfers between devices, body(): other = lax.ppermute(cache, 'core', [(0, 1), (1, 0)])  1.92 us
    pallas_call x1, Pallas kernels, body(): call(attend_kernel, jax.ShapeDtypeStruct((near, tok_dev + ANS_LEN, HD), b...  1.83 us
    pallas_call x1, Pallas kernels, body(): pl.pallas_call(project_kernel, out_shape=(jax.ShapeDtypeStruct((pairs * s...  1.74 us
  transfers between devices with their start and end apart: 1, of which 0 were waited for; matrix products, arithmetic and copies ran while one was open for 0% of the time, Pallas kernels for 0%

profile of v7, /device:TPU:8, one launch (start us, length us, event | category | flops | bytes accessed | tf_op | source)
XLA Modules:
  0.0 73.2 jit_solution(3525502201570276539)
XLA Ops:
  0.0 1.7 %shard_map.82 = (f32[8,80,128]{2,1,0:T(8,128)S(1)}, f32[8,128]{1,0:T(8,128)S(1)}, bf16[2,2048,128]{2,1,0:T(8,128)(2,1)S(1)}) custom-call(bf16[64,1024]{1,0:T(8,128)(2,1)} %hidden_hbm.1, bf16[1024,256]{1,0:T(8,128)(2,1)} %query_hbm.1, bf16[1024,128]{1,0:T(8,128)(2,1)} %key_hbm.1, bf16[1024,128]{1,0:T(8,128)(2,1)} %value_hbm.1, s32[32]{0:T(128)} %group_hbm.1, ...), custom_call_target="tpu_custom_call" | custom-call | flops 67108864 | bytes 1179648 | tf_op jit(solution)/shard_map/pallas_call | solution.py:267
  1.8 1.9 %collective-permute-start = (bf16[2,2048,128]{2,1,0:T(8,128)(2,1)S(1)}, bf16[2,2048,128]{2,1,0:T(8,128)(2,1)S(1)}, u32[]{:S(2)}, u32[]{:S(2)}) collective-permute-start(bf16[2,2048,128]{2,1,0:T(8,128)(2,1)S(1)} %get-tuple-element.9.cache_ref), channel_id=1, source_target_pairs={{0,1},{1,0},{2,3},{3,2},{4,5},{5,4},{6,7},{7,6},{8,9},{9,8},{10,11... | collective-permute-start | bytes 3145736 | tf_op jit(solution)/shard_map/ppermute | solution.py:289
  3.7 18.6 %all_to_all.25 = f16[8,80,128]{2,1,0:T(8,128)(2,1)S(1)} all-to-all(f16[8,80,128]{2,1,0:T(8,128)(2,1)S(1)} %convert_element_type.12), channel_id=1, replica_groups=mesh['far'=2,'high'=2,'low'=2,'side'=2,'head2'=2,'head1'=2,'head0'=2,'lo..., dimensions={0} | all-to-all | bytes 327680 | tf_op jit(solution)/shard_map/all_to_all | solution.py:290
  22.4 12.8 %all_to_all.26 = f16[8,80,128]{2,1,0:T(8,128)(2,1)S(1)} all-to-all(f16[8,80,128]{2,1,0:T(8,128)(2,1)S(1)} %convert_element_type.14), channel_id=1, replica_groups=mesh['far'=2,'high'=2,'low'=2,'side'=2,'head2'=2,'head1'=2,'head0'=2,'lo..., dimensions={0} | all-to-all | bytes 327680 | tf_op jit(solution)/shard_map/all_to_all | solution.py:301
  35.2 0.0 collective-permute-done.other_ref
  35.2 1.8 %shard_map.84 = bf16[8,72,128]{2,1,0:T(8,128)(2,1)S(1)} custom-call(f32[8,80,128]{2,1,0:T(8,128)S(1)} %convert_element_type.15.query_ref.own_ref, bf16[2,2048,128]{2,1,0:T(8,128)(2,1)S(1)} %get-tuple-element.9.cache_ref, bf16[2,2048,128]{2,1,0:T(8,128)(2,1)S(1)} %collective-permute-done.other_ref, f32[8,128]{1,0:T(8,128)S(1)} %get-tuple-element.10.bias_ref), custom_call_target="tpu_custom_call" | custom-call | flops 536870912 | bytes 2097152 | tf_op jit(solution)/shard_map/pallas_call | solution.py:302
  37.1 9.3 %all_to_all.27.state_ref = bf16[8,72,128]{2,1,0:T(8,128)(2,1)S(1)} all-to-all(bf16[8,72,128]{2,1,0:T(8,128)(2,1)S(1)} %shard_map.84), channel_id=1, replica_groups=mesh['far'=2,'high'=2,'low'=2,'side'=2,'head2'=2,'head1'=2,'head0'=2,'lo..., dimensions={0} | all-to-all | bytes 294912 | tf_op jit(solution)/shard_map/all_to_all | solution.py:310
  46.3 0.0 copy-start
  46.3 0.4 shard_map.85
  46.8 10.7 %all_to_all.28.state_ref = bf16[8,72,128]{2,1,0:T(8,128)(2,1)S(1)} all-to-all(bf16[8,72,128]{2,1,0:T(8,128)(2,1)S(1)} %shard_map.85), channel_id=1, replica_groups=mesh['far'=2,'high'=2,'low'=2,'side'=2,'head2'=2,'head1'=2,'head0'=2,'lo..., dimensions={0} | all-to-all | bytes 294912 | tf_op jit(solution)/shard_map/all_to_all | solution.py:319
  57.5 0.0 copy-done
  57.5 0.3 shard_map.86
  57.8 14.8 %all_to_all.29.part_ref = bf16[8,64,128]{2,1,0:T(8,128)(2,1)S(1)} all-to-all(bf16[8,64,128]{2,1,0:T(8,128)(2,1)S(1)} %shard_map.86), channel_id=1, replica_groups=mesh['far'=2,'high'=2,'low'=2,'side'=2,'head2'=2,'head1'=2,'head0'=2,'lo..., dimensions={0} | all-to-all | bytes 262144 | tf_op jit(solution)/shard_map/all_to_all | solution.py:328
  72.6 0.6 shard_map.87
  (5 shorter events, 0.1 us)
Async XLA Ops:
  1.8 33.5 %collective-permute-start = (bf16[2,2048,128]{2,1,0:T(8,128)(2,1)S(1)}, bf16[2,2048,128]{2,1,0:T(8,128)(2,1)S(1)}, u32[]{:S(2)}, u32[]{:S(2)}) collective-permute-start(bf16[2,2048,128]{2,1,0:T(8,128)(2,1)S(1)} %get-tuple-element.9.cache_ref), channel_id=1, source_target_pairs={{0,1},{1,0},{2,3},{3,2},{4,5},{5,4},{6,7},{7,6},{8,9},{9,8},{10,11... | collective-permute-start | bytes 3145736 | tf_op jit(solution)/shard_map/ppermute | solution.py:289
  46.3 11.1 %copy-start = (bf16[256,1024]{1,0:T(8,128)(2,1)S(1)}, bf16[256,1024]{1,0:T(8,128)(2,1)}, u32[]{:S(2)}) copy-start(bf16[256,1024]{1,0:T(8,128)(2,1)} %weight_ref.1) | copy-start | bytes 1572868

commit v8 on v7

--- a/solution.py
+++ b/solution.py
@@ -24,9 +24,10 @@
 SEQ = ("far", *PAIR, "side")
 HEAD = ("head2", "head1", "head0")
 CAND = ("lo", "core")
-RING = ("low", "side", "high")
-HEAD_RING = ("head1", "head0", "head2")
-NEAR = ("lo", "side", "far")
+RING = ("side", "low", "high")
+RING_OUT = ("low", "high", "side")
+HEAD_RING = ("head1", "head2", "head0")
+NEAR = ("far", "lo", "side")
 
 
 def call(kernel, out_shape, in_specs, **cost):
@@ -237,7 +238,7 @@
     pairs, side = lax.axis_size(PAIR), lax.axis_size("side")
     columns = []
     for h in range(side):
-        sources = [counted(RING, side=h, **coordinates(PAIR, p)) for p in range(pairs)]
+        sources = [counted(RING_OUT, side=h, **coordinates(PAIR, p)) for p in range(pairs)]
         columns.append(merged(*unpacked(jnp.stack([state_ref[place] for place in sources])))[0])
     attention = jnp.concatenate(columns, axis=1).astype(jnp.bfloat16)
     out = dot(attention, weight_ref[...])
@@ -316,7 +317,7 @@
         bytes_accessed=2 * state.size,
         transcendentals=0,
     )(state, queries)
-    state = lax.all_to_all(state, RING, 0, 0, tiled=True)
+    state = lax.all_to_all(state, RING_OUT, 0, 0, tiled=True)
     projected = call(
         output_kernel,
         jax.ShapeDtypeStruct((head, tok_dev, columns), bf16),

time: 73.5 us -> 73 us (level)
  no operation moved by 1% of the time
where the time goes in v8:
time: 73 us; the launch traced here: 72.6 us
  blocking collectives  65.6 us (90%)
  Pallas kernels  4.99 us (7%)
  starting transfers between devices  1.92 us (3%)
    all_to_all x1, blocking collectives, body(): lax.all_to_all(partial.astype(jnp.float16), RING, 0, 0, tiled=True)  18.4 us
    all_to_all x1, blocking collectives, body(): projected = lax.all_to_all(projected, HEAD_RING, 0, 0, tiled=True)  14.4 us
    all_to_all x1, blocking collectives, body(): queries = lax.all_to_all(queries, NEAR, 0, 0, tiled=True).astype(f32)  12.2 us
    all_to_all x1, blocking collectives, body(): state = lax.all_to_all(state, RING_OUT, 0, 0, tiled=True)  11.3 us
    all_to_all x1, blocking collectives, body(): state = lax.all_to_all(state, NEAR, 0, 0, tiled=True)  9.23 us
    ppermute x1, starting transfers between devices, body(): other = lax.ppermute(cache, 'core', [(0, 1), (1, 0)])  1.92 us
    pallas_call x1, Pallas kernels, body(): call(attend_kernel, jax.ShapeDtypeStruct((near, tok_dev + ANS_LEN, HD), b...  1.83 us
    pallas_call x1, Pallas kernels, body(): pl.pallas_call(project_kernel, out_shape=(jax.ShapeDtypeStruct((pairs * s...  1.74 us
  transfers between devices with their start and end apart: 1, of which 0 were waited for; matrix products, arithmetic and copies ran while one was open for 0% of the time, Pallas kernels for 0%

profile of v8, /device:TPU:8, one launch (start us, length us, event | category | flops | bytes accessed | tf_op | source)
XLA Modules:
  0.0 72.6 jit_solution(1815381591355854125)
XLA Ops:
  0.0 1.7 %shard_map.82 = (f32[8,80,128]{2,1,0:T(8,128)S(1)}, f32[8,128]{1,0:T(8,128)S(1)}, bf16[2,2048,128]{2,1,0:T(8,128)(2,1)S(1)}) custom-call(bf16[64,1024]{1,0:T(8,128)(2,1)} %hidden_hbm.1, bf16[1024,256]{1,0:T(8,128)(2,1)} %query_hbm.1, bf16[1024,128]{1,0:T(8,128)(2,1)} %key_hbm.1, bf16[1024,128]{1,0:T(8,128)(2,1)} %value_hbm.1, s32[32]{0:T(128)} %group_hbm.1, ...), custom_call_target="tpu_custom_call" | custom-call | flops 67108864 | bytes 1179648 | tf_op jit(solution)/shard_map/pallas_call | solution.py:268
  1.8 1.9 %collective-permute-start = (bf16[2,2048,128]{2,1,0:T(8,128)(2,1)S(1)}, bf16[2,2048,128]{2,1,0:T(8,128)(2,1)S(1)}, u32[]{:S(2)}, u32[]{:S(2)}) collective-permute-start(bf16[2,2048,128]{2,1,0:T(8,128)(2,1)S(1)} %get-tuple-element.9.cache_ref), channel_id=1, source_target_pairs={{0,1},{1,0},{2,3},{3,2},{4,5},{5,4},{6,7},{7,6},{8,9},{9,8},{10,11... | collective-permute-start | bytes 3145736 | tf_op jit(solution)/shard_map/ppermute | solution.py:290
  3.7 18.4 %all_to_all.25 = f16[8,80,128]{2,1,0:T(8,128)(2,1)S(1)} all-to-all(f16[8,80,128]{2,1,0:T(8,128)(2,1)S(1)} %convert_element_type.12), channel_id=1, replica_groups=mesh['far'=2,'high'=2,'low'=2,'side'=2,'head2'=2,'head1'=2,'head0'=2,'lo..., dimensions={0} | all-to-all | bytes 327680 | tf_op jit(solution)/shard_map/all_to_all | solution.py:291
  22.2 12.2 %all_to_all.26 = f16[8,80,128]{2,1,0:T(8,128)(2,1)S(1)} all-to-all(f16[8,80,128]{2,1,0:T(8,128)(2,1)S(1)} %convert_element_type.14), channel_id=1, replica_groups=mesh['far'=2,'high'=2,'low'=2,'side'=2,'head2'=2,'head1'=2,'head0'=2,'lo..., dimensions={0} | all-to-all | bytes 327680 | tf_op jit(solution)/shard_map/all_to_all | solution.py:302
  34.4 0.0 collective-permute-done.other_ref
  34.4 1.8 %shard_map.84 = bf16[8,72,128]{2,1,0:T(8,128)(2,1)S(1)} custom-call(f32[8,80,128]{2,1,0:T(8,128)S(1)} %convert_element_type.15.query_ref.own_ref, bf16[2,2048,128]{2,1,0:T(8,128)(2,1)S(1)} %get-tuple-element.9.cache_ref, bf16[2,2048,128]{2,1,0:T(8,128)(2,1)S(1)} %collective-permute-done.other_ref, f32[8,128]{1,0:T(8,128)S(1)} %get-tuple-element.10.bias_ref), custom_call_target="tpu_custom_call" | custom-call | flops 536870912 | bytes 2097152 | tf_op jit(solution)/shard_map/pallas_call | solution.py:303
  36.2 9.2 %all_to_all.27.state_ref = bf16[8,72,128]{2,1,0:T(8,128)(2,1)S(1)} all-to-all(bf16[8,72,128]{2,1,0:T(8,128)(2,1)S(1)} %shard_map.84), channel_id=1, replica_groups=mesh['far'=2,'high'=2,'low'=2,'side'=2,'head2'=2,'head1'=2,'head0'=2,'lo..., dimensions={0} | all-to-all | bytes 294912 | tf_op jit(solution)/shard_map/all_to_all | solution.py:311
  45.4 0.0 copy-start
  45.4 0.4 shard_map.85
  45.9 11.3 %all_to_all.28.state_ref = bf16[8,72,128]{2,1,0:T(8,128)(2,1)S(1)} all-to-all(bf16[8,72,128]{2,1,0:T(8,128)(2,1)S(1)} %shard_map.85), channel_id=1, replica_groups=mesh['far'=2,'high'=2,'low'=2,'side'=2,'head2'=2,'head1'=2,'head0'=2,'lo..., dimensions={0} | all-to-all | bytes 294912 | tf_op jit(solution)/shard_map/all_to_all | solution.py:320
  57.2 0.0 copy-done
  57.3 0.3 shard_map.86
  57.6 14.4 %all_to_all.29.part_ref = bf16[8,64,128]{2,1,0:T(8,128)(2,1)S(1)} all-to-all(bf16[8,64,128]{2,1,0:T(8,128)(2,1)S(1)} %shard_map.86), channel_id=1, replica_groups=mesh['far'=2,'high'=2,'low'=2,'side'=2,'head2'=2,'head1'=2,'head0'=2,'lo..., dimensions={0} | all-to-all | bytes 262144 | tf_op jit(solution)/shard_map/all_to_all | solution.py:329
  72.0 0.6 shard_map.87
  (5 shorter events, 0.1 us)
Async XLA Ops:
  1.8 32.6 %collective-permute-start = (bf16[2,2048,128]{2,1,0:T(8,128)(2,1)S(1)}, bf16[2,2048,128]{2,1,0:T(8,128)(2,1)S(1)}, u32[]{:S(2)}, u32[]{:S(2)}) collective-permute-start(bf16[2,2048,128]{2,1,0:T(8,128)(2,1)S(1)} %get-tuple-element.9.cache_ref), channel_id=1, source_target_pairs={{0,1},{1,0},{2,3},{3,2},{4,5},{5,4},{6,7},{7,6},{8,9},{9,8},{10,11... | collective-permute-start | bytes 3145736 | tf_op jit(solution)/shard_map/ppermute | solution.py:290
  45.4 11.8 %copy-start = (bf16[256,1024]{1,0:T(8,128)(2,1)S(1)}, bf16[256,1024]{1,0:T(8,128)(2,1)}, u32[]{:S(2)}) copy-start(bf16[256,1024]{1,0:T(8,128)(2,1)} %weight_ref.1) | copy-start | bytes 1572868

commit v9 on v6

--- a/solution.py
+++ b/solution.py
@@ -105,7 +105,7 @@
     copies[-1].wait()
 
 
-def reduce_kernel(part_ref, out_ref):
+def reduce_kernel(part_ref, _, out_ref, __):
     total = jnp.sum(part_ref[...], axis=0) * (1 / part_ref.shape[0])
     out_ref[...] = jnp.broadcast_to(total[None], out_ref.shape)
 
@@ -273,17 +273,23 @@
             transcendentals=0,
         ),
     )(*inputs)
-    other = lax.ppermute(cache, "core", [(0, 1), (1, 0)])
     partial = lax.all_to_all(partial.astype(jnp.float16), RING, 0, 0, tiled=True)
     near = far * side * lo
-    queries = call(
+    queries, cache = pl.pallas_call(
         reduce_kernel,
-        jax.ShapeDtypeStruct((near, *partial.shape[1:]), f32),
-        [VMEM],
-        flops=partial.size,
-        bytes_accessed=partial.size * 4,
-        transcendentals=0,
-    )(partial.astype(f32))
+        out_shape=(
+            jax.ShapeDtypeStruct((near, *partial.shape[1:]), f32),
+            jax.ShapeDtypeStruct(cache.shape, cache.dtype),
+        ),
+        in_specs=[VMEM, pl.BlockSpec(memory_space=pl.ANY)],
+        out_specs=(VMEM, pl.BlockSpec(memory_space=pl.ANY)),
+        input_output_aliases={1: 1},
+        compiler_params=pltpu.CompilerParams(vmem_limit_bytes=40 * 1024 * 1024),
+        cost_estimate=pl.CostEstimate(
+            flops=partial.size, bytes_accessed=partial.size * 4, transcendentals=0
+        ),
+    )(partial.astype(f32), cache)
+    other = lax.ppermute(cache, "core", [(0, 1), (1, 0)])
     queries = queries.astype(jnp.float16)
     queries = lax.all_to_all(queries, ("side", "far", "lo"), 0, 0, tiled=True).astype(f32)
     state = call(

time: 72.4 us -> 71.9 us (level)
  no operation moved by 1% of the time
where the time goes in v9:
time: 71.9 us; the launch traced here: 71.5 us
  blocking collectives  64.5 us (90%)
  Pallas kernels  4.98 us (7%)
  starting transfers between devices  1.92 us (3%)
    all_to_all x1, blocking collectives, body(): lax.all_to_all(partial.astype(jnp.float16), RING, 0, 0, tiled=True)  18.1 us
    all_to_all x1, blocking collectives, body(): projected = lax.all_to_all(projected, HEAD[::-1], 0, 0, tiled=True)  14.2 us
    all_to_all x1, blocking collectives, body(): lax.all_to_all(queries, ('side', 'far', 'lo'), 0, 0, tiled=True).astype(f32)  12.1 us
    all_to_all x1, blocking collectives, body(): state = lax.all_to_all(state, RING, 0, 0, tiled=True)  10.9 us
    all_to_all x1, blocking collectives, body(): state = lax.all_to_all(state, ('side', 'far', 'lo'), 0, 0, tiled=True)  9.2 us
    ppermute x1, starting transfers between devices, body(): other = lax.ppermute(cache, 'core', [(0, 1), (1, 0)])  1.92 us
    pallas_call x1, Pallas kernels, body(): call(attend_kernel, jax.ShapeDtypeStruct((side, far, lo, tok_dev + ANS_LE...  1.82 us
    pallas_call x1, Pallas kernels, body(): pl.pallas_call(project_kernel, out_shape=(jax.ShapeDtypeStruct((pairs * s...  1.74 us
  transfers between devices with their start and end apart: 1, of which 0 were waited for; matrix products, arithmetic and copies ran while one was open for 0% of the time, Pallas kernels for 0%

profile of v9, /device:TPU:8, one launch (start us, length us, event | category | flops | bytes accessed | tf_op | source)
XLA Modules:
  0.0 71.5 jit_solution(12446479440222040201)
XLA Ops:
  0.0 1.7 %shard_map.82 = (f32[8,80,128]{2,1,0:T(8,128)S(1)}, f32[8,128]{1,0:T(8,128)S(1)}, bf16[2,2048,128]{2,1,0:T(8,128)(2,1)S(1)}) custom-call(bf16[64,1024]{1,0:T(8,128)(2,1)} %hidden_hbm.1, bf16[1024,256]{1,0:T(8,128)(2,1)} %query_hbm.1, bf16[1024,128]{1,0:T(8,128)(2,1)} %key_hbm.1, bf16[1024,128]{1,0:T(8,128)(2,1)} %value_hbm.1, s32[32]{0:T(128)} %group_hbm.1, ...), custom_call_target="tpu_custom_call" | custom-call | flops 67108864 | bytes 1179648 | tf_op jit(solution)/shard_map/pallas_call | solution.py:254
  1.8 18.1 %all_to_all.25 = f16[8,80,128]{2,1,0:T(8,128)(2,1)S(1)} all-to-all(f16[8,80,128]{2,1,0:T(8,128)(2,1)S(1)} %convert_element_type.12), channel_id=1, replica_groups=mesh['far'=2,'high'=2,'low'=2,'side'=2,'head2'=2,'head1'=2,'head0'=2,'lo..., dimensions={0} | all-to-all | bytes 327680 | tf_op jit(solution)/shard_map/all_to_all | solution.py:276
  20.0 1.9 %collective-permute-start = (bf16[2,2048,128]{2,1,0:T(8,128)(2,1)S(1)}, bf16[2,2048,128]{2,1,0:T(8,128)(2,1)S(1)}, u32[]{:S(2)}, u32[]{:S(2)}) collective-permute-start(bf16[2,2048,128]{2,1,0:T(8,128)(2,1)S(1)} %get-tuple-element.13.cache_ref), channel_id=1, source_target_pairs={{0,1},{1,0},{2,3},{3,2},{4,5},{5,4},{6,7},{7,6},{8,9},{9,8},{10,11... | collective-permute-start | bytes 3145736 | tf_op jit(solution)/shard_map/ppermute | solution.py:292
  22.0 12.1 %all_to_all.26 = f16[8,80,128]{2,1,0:T(8,128)(2,1)S(1)} all-to-all(f16[8,80,128]{2,1,0:T(8,128)(2,1)S(1)} %convert_element_type.14), channel_id=1, replica_groups=mesh['far'=2,'high'=2,'low'=2,'side'=2,'head2'=2,'head1'=2,'head0'=2,'lo..., dimensions={0} | all-to-all | bytes 327680 | tf_op jit(solution)/shard_map/all_to_all | solution.py:294
  34.0 0.0 collective-permute-done.other_ref
  34.1 1.8 %shard_map.84 = bf16[2,2,2,72,128]{4,3,2,1,0:T(8,128)(2,1)S(1)} custom-call(f32[8,80,128]{2,1,0:T(8,128)S(1)} %convert_element_type.15.query_ref.own_ref, bf16[2,2048,128]{2,1,0:T(8,128)(2,1)S(1)} %get-tuple-element.13.cache_ref, bf16[2,2048,128]{2,1,0:T(8,128)(2,1)S(1)} %collective-permute-done.other_ref, f32[8,128]{1,0:T(8,128)S(1)} %get-tuple-element.14.bias_ref), custom_call_target="tpu_custom_call" | custom-call | flops 536870912 | bytes 2097152 | tf_op jit(solution)/shard_map/pallas_call | solution.py:295
  35.9 9.2 %all_to_all.27.state_ref = bf16[8,72,128]{2,1,0:T(8,128)(2,1)S(1)} all-to-all(bf16[8,72,128]{2,1,0:T(8,128)(2,1)S(1)} %bitcast.2), channel_id=1, replica_groups=mesh['far'=2,'high'=2,'low'=2,'side'=2,'head2'=2,'head1'=2,'head0'=2,'lo..., dimensions={0} | all-to-all | bytes 294912 | tf_op jit(solution)/shard_map/all_to_all | solution.py:304
  45.1 0.0 copy-start
  45.1 0.4 shard_map.85
  45.5 10.9 %all_to_all.28 = bf16[8,72,128]{2,1,0:T(8,128)(2,1)S(1)} all-to-all(bf16[8,72,128]{2,1,0:T(8,128)(2,1)S(1)} %shard_map.85), channel_id=1, replica_groups=mesh['far'=2,'high'=2,'low'=2,'side'=2,'head2'=2,'head1'=2,'head0'=2,'lo..., dimensions={0} | all-to-all | bytes 294912 | tf_op jit(solution)/shard_map/all_to_all | solution.py:313
  56.4 0.0 copy-done
  56.4 0.3 shard_map.86
  56.7 14.2 %all_to_all.29.part_ref = bf16[8,64,128]{2,1,0:T(8,128)(2,1)S(1)} all-to-all(bf16[8,64,128]{2,1,0:T(8,128)(2,1)S(1)} %shard_map.86), channel_id=1, replica_groups=mesh['far'=2,'high'=2,'low'=2,'side'=2,'head2'=2,'head1'=2,'head0'=2,'lo..., dimensions={0} | all-to-all | bytes 262144 | tf_op jit(solution)/shard_map/all_to_all | solution.py:322
  70.9 0.6 shard_map.87
  (5 shorter events, 0.1 us)
Async XLA Ops:
  20.0 14.0 %collective-permute-start = (bf16[2,2048,128]{2,1,0:T(8,128)(2,1)S(1)}, bf16[2,2048,128]{2,1,0:T(8,128)(2,1)S(1)}, u32[]{:S(2)}, u32[]{:S(2)}) collective-permute-start(bf16[2,2048,128]{2,1,0:T(8,128)(2,1)S(1)} %get-tuple-element.13.cache_ref), channel_id=1, source_target_pairs={{0,1},{1,0},{2,3},{3,2},{4,5},{5,4},{6,7},{7,6},{8,9},{9,8},{10,11... | collective-permute-start | bytes 3145736 | tf_op jit(solution)/shard_map/ppermute | solution.py:292
  45.1 11.3 %copy-start = (bf16[256,1024]{1,0:T(8,128)(2,1)S(1)}, bf16[256,1024]{1,0:T(8,128)(2,1)}, u32[]{:S(2)}) copy-start(bf16[256,1024]{1,0:T(8,128)(2,1)} %weight_ref.1) | copy-start | bytes 1572868

commit v10 on v9

--- a/solution.py
+++ b/solution.py
@@ -67,18 +67,27 @@
         copies.append(pltpu.make_async_copy(source, target, sems.at[len(copies)]))
         copies[-1].start()
 
+    start(group_hbm, group_smem)
     for half in halves:
         start(query_hbm.at[half, :], weight_ref.at[half, pl.ds(0, width)])
         start(hidden_hbm.at[:, half], hidden_ref.at[:, half])
         start(key_hbm.at[half, :], weight_ref.at[half, pl.ds(width, HD)])
         start(value_hbm.at[half, :], weight_ref.at[half, pl.ds(width + HD, HD)])
-    start(group_hbm, group_smem)
-    start(key_cache, cache_hbm.at[0])
-    start(value_cache, cache_hbm.at[1])
+    copies[0].wait()
+    chunk = lax.axis_index(SEQ) // (lax.axis_size(SEQ) // GROUPS)
+    lane = lax.broadcasted_iota(jnp.int32, bias_ref.shape, 1)
+    bias = jnp.zeros(bias_ref.shape, jnp.float32)
+    for c in range(group_smem.shape[0]):
+        hidden_by = jnp.where(group_smem[c] >= chunk, 0.0, NEGATIVE)
+        bias = jnp.where(lane == c, hidden_by, bias)
+    bias_ref[...] = bias
     total = None
     for i, half in enumerate(halves):
-        for copy in copies[4 * i : 4 * i + 4]:
+        for copy in copies[4 * i + 1 : 4 * i + 5]:
             copy.wait()
+        if i == 0:
+            start(key_cache, cache_hbm.at[0])
+            start(value_cache, cache_hbm.at[1])
         part = dot(hidden_ref[:, half], weight_ref[half, :])
         total = part if total is None else total + part
     ring = SMALL_SCALE * lax.axis_size(PAIR) * side
@@ -93,14 +102,6 @@
                 place = slice((f * pairs + p) * ANS_LEN, (f * pairs + p + 1) * ANS_LEN)
                 target = s * pairs + reverse(p, pairs)
                 out_ref[target, tokens + f * ANS_LEN : tokens + (f + 1) * ANS_LEN] = part[place]
-    copies[-3].wait()
-    chunk = lax.axis_index(SEQ) // (lax.axis_size(SEQ) // GROUPS)
-    lane = lax.broadcasted_iota(jnp.int32, bias_ref.shape, 1)
-    bias = jnp.zeros(bias_ref.shape, jnp.float32)
-    for c in range(group_smem.shape[0]):
-        hidden_by = jnp.where(group_smem[c] >= chunk, 0.0, NEGATIVE)
-        bias = jnp.where(lane == c, hidden_by, bias)
-    bias_ref[...] = bias
     copies[-2].wait()
     copies[-1].wait()
 

time: 71.9 us -> 72.5 us (level)
  no operation moved by 1% of the time
where the time goes in v10:
time: 72.5 us; the launch traced here: 72.2 us
  blocking collectives  64.5 us (89%)
  Pallas kernels  5.66 us (8%)
  starting transfers between devices  1.92 us (3%)
    all_to_all x1, blocking collectives, body(): lax.all_to_all(partial.astype(jnp.float16), RING, 0, 0, tiled=True)  18.1 us
    all_to_all x1, blocking collectives, body(): projected = lax.all_to_all(projected, HEAD[::-1], 0, 0, tiled=True)  14.2 us
    all_to_all x1, blocking collectives, body(): lax.all_to_all(queries, ('side', 'far', 'lo'), 0, 0, tiled=True).astype(f32)  12.1 us
    all_to_all x1, blocking collectives, body(): state = lax.all_to_all(state, RING, 0, 0, tiled=True)  10.9 us
    all_to_all x1, blocking collectives, body(): state = lax.all_to_all(state, ('side', 'far', 'lo'), 0, 0, tiled=True)  9.2 us
    pallas_call x1, Pallas kernels, body(): pl.pallas_call(project_kernel, out_shape=(jax.ShapeDtypeStruct((pairs * s...  2.42 us
    ppermute x1, starting transfers between devices, body(): other = lax.ppermute(cache, 'core', [(0, 1), (1, 0)])  1.92 us
    pallas_call x1, Pallas kernels, body(): call(attend_kernel, jax.ShapeDtypeStruct((side, far, lo, tok_dev + ANS_LE...  1.82 us
  transfers between devices with their start and end apart: 1, of which 0 were waited for; matrix products, arithmetic and copies ran while one was open for 0% of the time, Pallas kernels for 0%

profile of v10, /device:TPU:8, one launch (start us, length us, event | category | flops | bytes accessed | tf_op | source)
XLA Modules:
  0.0 72.2 jit_solution(2654341513466908731)
XLA Ops:
  0.0 2.4 %shard_map.82 = (f32[8,80,128]{2,1,0:T(8,128)S(1)}, f32[8,128]{1,0:T(8,128)S(1)}, bf16[2,2048,128]{2,1,0:T(8,128)(2,1)S(1)}) custom-call(bf16[64,1024]{1,0:T(8,128)(2,1)} %hidden_hbm.1, bf16[1024,256]{1,0:T(8,128)(2,1)} %query_hbm.1, bf16[1024,128]{1,0:T(8,128)(2,1)} %key_hbm.1, bf16[1024,128]{1,0:T(8,128)(2,1)} %value_hbm.1, s32[32]{0:T(128)} %group_hbm.1, ...), custom_call_target="tpu_custom_call" | custom-call | flops 67108864 | bytes 1179648 | tf_op jit(solution)/shard_map/pallas_call | solution.py:255
  2.5 18.1 %all_to_all.25 = f16[8,80,128]{2,1,0:T(8,128)(2,1)S(1)} all-to-all(f16[8,80,128]{2,1,0:T(8,128)(2,1)S(1)} %convert_element_type.12), channel_id=1, replica_groups=mesh['far'=2,'high'=2,'low'=2,'side'=2,'head2'=2,'head1'=2,'head0'=2,'lo..., dimensions={0} | all-to-all | bytes 327680 | tf_op jit(solution)/shard_map/all_to_all | solution.py:277
  20.7 1.9 %collective-permute-start = (bf16[2,2048,128]{2,1,0:T(8,128)(2,1)S(1)}, bf16[2,2048,128]{2,1,0:T(8,128)(2,1)S(1)}, u32[]{:S(2)}, u32[]{:S(2)}) collective-permute-start(bf16[2,2048,128]{2,1,0:T(8,128)(2,1)S(1)} %get-tuple-element.13.cache_ref), channel_id=1, source_target_pairs={{0,1},{1,0},{2,3},{3,2},{4,5},{5,4},{6,7},{7,6},{8,9},{9,8},{10,11... | collective-permute-start | bytes 3145736 | tf_op jit(solution)/shard_map/ppermute | solution.py:293
  22.6 12.1 %all_to_all.26 = f16[8,80,128]{2,1,0:T(8,128)(2,1)S(1)} all-to-all(f16[8,80,128]{2,1,0:T(8,128)(2,1)S(1)} %convert_element_type.14), channel_id=1, replica_groups=mesh['far'=2,'high'=2,'low'=2,'side'=2,'head2'=2,'head1'=2,'head0'=2,'lo..., dimensions={0} | all-to-all | bytes 327680 | tf_op jit(solution)/shard_map/all_to_all | solution.py:295
  34.7 0.0 collective-permute-done.other_ref
  34.7 1.8 %shard_map.84 = bf16[2,2,2,72,128]{4,3,2,1,0:T(8,128)(2,1)S(1)} custom-call(f32[8,80,128]{2,1,0:T(8,128)S(1)} %convert_element_type.15.query_ref.own_ref, bf16[2,2048,128]{2,1,0:T(8,128)(2,1)S(1)} %get-tuple-element.13.cache_ref, bf16[2,2048,128]{2,1,0:T(8,128)(2,1)S(1)} %collective-permute-done.other_ref, f32[8,128]{1,0:T(8,128)S(1)} %get-tuple-element.14.bias_ref), custom_call_target="tpu_custom_call" | custom-call | flops 536870912 | bytes 2097152 | tf_op jit(solution)/shard_map/pallas_call | solution.py:296
  36.6 9.2 %all_to_all.27.state_ref = bf16[8,72,128]{2,1,0:T(8,128)(2,1)S(1)} all-to-all(bf16[8,72,128]{2,1,0:T(8,128)(2,1)S(1)} %bitcast.2), channel_id=1, replica_groups=mesh['far'=2,'high'=2,'low'=2,'side'=2,'head2'=2,'head1'=2,'head0'=2,'lo..., dimensions={0} | all-to-all | bytes 294912 | tf_op jit(solution)/shard_map/all_to_all | solution.py:305
  45.7 0.0 copy-start
  45.8 0.4 shard_map.85
  46.2 10.9 %all_to_all.28 = bf16[8,72,128]{2,1,0:T(8,128)(2,1)S(1)} all-to-all(bf16[8,72,128]{2,1,0:T(8,128)(2,1)S(1)} %shard_map.85), channel_id=1, replica_groups=mesh['far'=2,'high'=2,'low'=2,'side'=2,'head2'=2,'head1'=2,'head0'=2,'lo..., dimensions={0} | all-to-all | bytes 294912 | tf_op jit(solution)/shard_map/all_to_all | solution.py:314
  57.1 0.0 copy-done
  57.1 0.3 shard_map.86
  57.4 14.2 %all_to_all.29.part_ref = bf16[8,64,128]{2,1,0:T(8,128)(2,1)S(1)} all-to-all(bf16[8,64,128]{2,1,0:T(8,128)(2,1)S(1)} %shard_map.86), channel_id=1, replica_groups=mesh['far'=2,'high'=2,'low'=2,'side'=2,'head2'=2,'head1'=2,'head0'=2,'lo..., dimensions={0} | all-to-all | bytes 262144 | tf_op jit(solution)/shard_map/all_to_all | solution.py:323
  71.6 0.6 shard_map.87
  (5 shorter events, 0.1 us)
Async XLA Ops:
  20.7 14.0 %collective-permute-start = (bf16[2,2048,128]{2,1,0:T(8,128)(2,1)S(1)}, bf16[2,2048,128]{2,1,0:T(8,128)(2,1)S(1)}, u32[]{:S(2)}, u32[]{:S(2)}) collective-permute-start(bf16[2,2048,128]{2,1,0:T(8,128)(2,1)S(1)} %get-tuple-element.13.cache_ref), channel_id=1, source_target_pairs={{0,1},{1,0},{2,3},{3,2},{4,5},{5,4},{6,7},{7,6},{8,9},{9,8},{10,11... | collective-permute-start | bytes 3145736 | tf_op jit(solution)/shard_map/ppermute | solution.py:293
  45.7 11.3 %copy-start = (bf16[256,1024]{1,0:T(8,128)(2,1)S(1)}, bf16[256,1024]{1,0:T(8,128)(2,1)}, u32[]{:S(2)}) copy-start(bf16[256,1024]{1,0:T(8,128)(2,1)} %weight_ref.1) | copy-start | bytes 1572868

commit v11 on v9

--- a/solution.py
+++ b/solution.py
@@ -229,7 +229,7 @@
     attention = jnp.concatenate(columns, axis=1).astype(jnp.bfloat16)
     out = dot(attention, weight_ref[...])
     for block in range(blocks):
-        place = reverse(block, blocks)
+        place = 2 * (block % (blocks // 2)) + block // (blocks // 2)
         out_ref[block] = out[:, place * width : (place + 1) * width].astype(jnp.bfloat16)
 
 
@@ -310,7 +310,7 @@
         bytes_accessed=2 * state.size,
         transcendentals=0,
     )(state, queries)
-    state = lax.all_to_all(state, RING, 0, 0, tiled=True)
+    state = lax.all_to_all(state, ("side", *PAIR), 0, 0, tiled=True)
     projected = call(
         output_kernel,
         jax.ShapeDtypeStruct((head, tok_dev, columns), bf16),
@@ -319,7 +319,7 @@
         bytes_accessed=2 * out_weight.size,
         transcendentals=0,
     )(state.reshape(side, pairs, tok_dev + ANS_LEN, HD), out_weight)
-    projected = lax.all_to_all(projected, HEAD[::-1], 0, 0, tiled=True)
+    projected = lax.all_to_all(projected, (HEAD[2], *HEAD[:2]), 0, 0, tiled=True)
     return call(
         sum_kernel,
         jax.ShapeDtypeStruct((tok_dev, columns), bf16),

time: 71.9 us -> 73.1 us (1.017)
  blocking collectives: 64.5 us -> 65.7 us
    all_to_all x2, blocking collectives: 25.1 us -> 26.3 us  [the longest x1 15 us: body(): lax.all_to_all(projected, (HEAD[2], *HEAD[:2]), 0, 0, tiled=True)]
where the time goes in v11:
time: 73.1 us; the launch traced here: 72.7 us
  blocking collectives  65.7 us (90%)
  Pallas kernels  4.99 us (7%)
  starting transfers between devices  1.92 us (3%)
    all_to_all x1, blocking collectives, body(): lax.all_to_all(partial.astype(jnp.float16), RING, 0, 0, tiled=True)  18.1 us
    all_to_all x1, blocking collectives, body(): lax.all_to_all(projected, (HEAD[2], *HEAD[:2]), 0, 0, tiled=True)  15 us
    all_to_all x1, blocking collectives, body(): lax.all_to_all(queries, ('side', 'far', 'lo'), 0, 0, tiled=True).astype(f32)  12.1 us
    all_to_all x1, blocking collectives, body(): state = lax.all_to_all(state, ('side', *PAIR), 0, 0, tiled=True)  11.3 us
    all_to_all x1, blocking collectives, body(): state = lax.all_to_all(state, ('side', 'far', 'lo'), 0, 0, tiled=True)  9.2 us
    ppermute x1, starting transfers between devices, body(): other = lax.ppermute(cache, 'core', [(0, 1), (1, 0)])  1.92 us
    pallas_call x1, Pallas kernels, body(): call(attend_kernel, jax.ShapeDtypeStruct((side, far, lo, tok_dev + ANS_LE...  1.82 us
    pallas_call x1, Pallas kernels, body(): pl.pallas_call(project_kernel, out_shape=(jax.ShapeDtypeStruct((pairs * s...  1.74 us
  transfers between devices with their start and end apart: 1, of which 0 were waited for; matrix products, arithmetic and copies ran while one was open for 0% of the time, Pallas kernels for 0%

profile of v11, /device:TPU:8, one launch (start us, length us, event | category | flops | bytes accessed | tf_op | source)
XLA Modules:
  0.0 72.7 jit_solution(7329774345827779335)
XLA Ops:
  0.0 1.7 %shard_map.82 = (f32[8,80,128]{2,1,0:T(8,128)S(1)}, f32[8,128]{1,0:T(8,128)S(1)}, bf16[2,2048,128]{2,1,0:T(8,128)(2,1)S(1)}) custom-call(bf16[64,1024]{1,0:T(8,128)(2,1)} %hidden_hbm.1, bf16[1024,256]{1,0:T(8,128)(2,1)} %query_hbm.1, bf16[1024,128]{1,0:T(8,128)(2,1)} %key_hbm.1, bf16[1024,128]{1,0:T(8,128)(2,1)} %value_hbm.1, s32[32]{0:T(128)} %group_hbm.1, ...), custom_call_target="tpu_custom_call" | custom-call | flops 67108864 | bytes 1179648 | tf_op jit(solution)/shard_map/pallas_call | solution.py:254
  1.8 18.1 %all_to_all.25 = f16[8,80,128]{2,1,0:T(8,128)(2,1)S(1)} all-to-all(f16[8,80,128]{2,1,0:T(8,128)(2,1)S(1)} %convert_element_type.12), channel_id=1, replica_groups=mesh['far'=2,'high'=2,'low'=2,'side'=2,'head2'=2,'head1'=2,'head0'=2,'lo..., dimensions={0} | all-to-all | bytes 327680 | tf_op jit(solution)/shard_map/all_to_all | solution.py:276
  20.0 1.9 %collective-permute-start = (bf16[2,2048,128]{2,1,0:T(8,128)(2,1)S(1)}, bf16[2,2048,128]{2,1,0:T(8,128)(2,1)S(1)}, u32[]{:S(2)}, u32[]{:S(2)}) collective-permute-start(bf16[2,2048,128]{2,1,0:T(8,128)(2,1)S(1)} %get-tuple-element.13.cache_ref), channel_id=1, source_target_pairs={{0,1},{1,0},{2,3},{3,2},{4,5},{5,4},{6,7},{7,6},{8,9},{9,8},{10,11... | collective-permute-start | bytes 3145736 | tf_op jit(solution)/shard_map/ppermute | solution.py:292
  22.0 12.1 %all_to_all.26 = f16[8,80,128]{2,1,0:T(8,128)(2,1)S(1)} all-to-all(f16[8,80,128]{2,1,0:T(8,128)(2,1)S(1)} %convert_element_type.14), channel_id=1, replica_groups=mesh['far'=2,'high'=2,'low'=2,'side'=2,'head2'=2,'head1'=2,'head0'=2,'lo..., dimensions={0} | all-to-all | bytes 327680 | tf_op jit(solution)/shard_map/all_to_all | solution.py:294
  34.0 0.0 collective-permute-done.other_ref
  34.1 1.8 %shard_map.84 = bf16[2,2,2,72,128]{4,3,2,1,0:T(8,128)(2,1)S(1)} custom-call(f32[8,80,128]{2,1,0:T(8,128)S(1)} %convert_element_type.15.query_ref.own_ref, bf16[2,2048,128]{2,1,0:T(8,128)(2,1)S(1)} %get-tuple-element.13.cache_ref, bf16[2,2048,128]{2,1,0:T(8,128)(2,1)S(1)} %collective-permute-done.other_ref, f32[8,128]{1,0:T(8,128)S(1)} %get-tuple-element.14.bias_ref), custom_call_target="tpu_custom_call" | custom-call | flops 536870912 | bytes 2097152 | tf_op jit(solution)/shard_map/pallas_call | solution.py:295
  35.9 9.2 %all_to_all.27.state_ref = bf16[8,72,128]{2,1,0:T(8,128)(2,1)S(1)} all-to-all(bf16[8,72,128]{2,1,0:T(8,128)(2,1)S(1)} %bitcast.2), channel_id=1, replica_groups=mesh['far'=2,'high'=2,'low'=2,'side'=2,'head2'=2,'head1'=2,'head0'=2,'lo..., dimensions={0} | all-to-all | bytes 294912 | tf_op jit(solution)/shard_map/all_to_all | solution.py:304
  45.1 0.0 copy-start
  45.1 0.4 shard_map.85
  45.5 11.3 %all_to_all.28 = bf16[8,72,128]{2,1,0:T(8,128)(2,1)S(1)} all-to-all(bf16[8,72,128]{2,1,0:T(8,128)(2,1)S(1)} %shard_map.85), channel_id=1, replica_groups=mesh['far'=2,'high'=2,'low'=2,'side'=2,'head2'=2,'head1'=2,'head0'=2,'lo..., dimensions={0} | all-to-all | bytes 294912 | tf_op jit(solution)/shard_map/all_to_all | solution.py:313
  56.8 0.0 copy-done
  56.8 0.3 shard_map.86
  57.2 15.0 %all_to_all.29.part_ref = bf16[8,64,128]{2,1,0:T(8,128)(2,1)S(1)} all-to-all(bf16[8,64,128]{2,1,0:T(8,128)(2,1)S(1)} %shard_map.86), channel_id=1, replica_groups=mesh['far'=2,'high'=2,'low'=2,'side'=2,'head2'=2,'head1'=2,'head0'=2,'lo..., dimensions={0} | all-to-all | bytes 262144 | tf_op jit(solution)/shard_map/all_to_all | solution.py:322
  72.1 0.6 shard_map.87
  (5 shorter events, 0.1 us)
Async XLA Ops:
  20.0 14.0 %collective-permute-start = (bf16[2,2048,128]{2,1,0:T(8,128)(2,1)S(1)}, bf16[2,2048,128]{2,1,0:T(8,128)(2,1)S(1)}, u32[]{:S(2)}, u32[]{:S(2)}) collective-permute-start(bf16[2,2048,128]{2,1,0:T(8,128)(2,1)S(1)} %get-tuple-element.13.cache_ref), channel_id=1, source_target_pairs={{0,1},{1,0},{2,3},{3,2},{4,5},{5,4},{6,7},{7,6},{8,9},{9,8},{10,11... | collective-permute-start | bytes 3145736 | tf_op jit(solution)/shard_map/ppermute | solution.py:292
  45.1 11.8 %copy-start = (bf16[256,1024]{1,0:T(8,128)(2,1)S(1)}, bf16[256,1024]{1,0:T(8,128)(2,1)}, u32[]{:S(2)}) copy-start(bf16[256,1024]{1,0:T(8,128)(2,1)} %weight_ref.1) | copy-start | bytes 1572868

commit v12 on v9

--- a/solution.py
+++ b/solution.py
@@ -143,7 +143,7 @@
 def attend_kernel(query_ref, cache_ref, other_ref, bias_ref, out_ref):
     scale = HD ** (-0.5)
     side, far, lo, rows, _ = out_ref.shape
-    rows -= ANS_LEN
+    rows = (rows - ANS_LEN) // side
     halves = far
     assert ROW_BLOCK == lo * rows
     cores = lax.axis_size("core")
@@ -161,7 +161,7 @@
         return dot_transposed(query, cache[0])
 
     ahead = scored(steps[0])
-    held = []
+    held, heads = [], []
     for i, (r, cache) in enumerate(steps):
         scores = ahead
         if i + 1 < len(steps):
@@ -182,9 +182,12 @@
         candidate = cand * cands + place % cands
         bias = jnp.sum(jnp.where(lane == candidate, bias_ref[0:1, :], 0.0), axis=1, keepdims=True)
         level = top + jnp.log(total) + bias
-        for j in range(lo):
-            part = slice(j * rows, (j + 1) * rows)
-            state = packed(mean[part], level[part])
+        heads.append((mean, level))
+    for j in range(lo):
+        part = slice(j * rows, (j + 1) * rows)
+        mean, level = (jnp.concatenate([head[k][part] for head in heads], axis=0) for k in (0, 1))
+        state = packed(mean, level)
+        for r in range(side):
             for f in range(far):
                 out_ref[r, f, j] = state
 
@@ -203,13 +206,16 @@
             total = total + own_ref[place + half * lo, part]
         return (total * (1 / scale)).astype(jnp.bfloat16)
 
-    query = own(lax.axis_index("side"), slice(0, tokens), SMALL_SCALE)
+    heads = lax.axis_size("side")
+    tokens //= heads
+    query = [own(s, slice(0, tokens), SMALL_SCALE) for s in range(heads)]
+    query = jnp.concatenate(query, axis=0)
     key = own(0, slice(tokens, None), KEY_SCALE)
     value = own(1, slice(tokens, None), SMALL_SCALE)
     scores = dot_transposed(query, key) * HD ** (-0.5)
     row = lax.broadcasted_iota(jnp.int32, scores.shape, 0)
     column = lax.broadcasted_iota(jnp.int32, scores.shape, 1)
-    shown = (row // rows == column // ANS_LEN) & (column % ANS_LEN <= row % ANS_LEN)
+    shown = (row % tokens // rows == column // ANS_LEN) & (column % ANS_LEN <= row % ANS_LEN)
     scores = jnp.where(shown, scores, NEGATIVE)
     top = jnp.max(scores, axis=1, keepdims=True)
     weights = jnp.where(shown, jnp.exp(scores - top), 0.0)
@@ -224,8 +230,9 @@
 
 
 def output_kernel(state_ref, weight_ref, out_ref):
-    blocks, _, width = out_ref.shape
-    columns = [merged(*unpacked(state_ref[s]))[0] for s in range(state_ref.shape[0])]
+    blocks, tokens, width = out_ref.shape
+    attention = merged(*unpacked(state_ref[...]))[0]
+    columns = [attention[at : at + tokens] for at in range(0, attention.shape[0], tokens)]
     attention = jnp.concatenate(columns, axis=1).astype(jnp.bfloat16)
     out = dot(attention, weight_ref[...])
     for block in range(blocks):
@@ -294,23 +301,23 @@
     queries = lax.all_to_all(queries, ("side", "far", "lo"), 0, 0, tiled=True).astype(f32)
     state = call(
         attend_kernel,
-        jax.ShapeDtypeStruct((side, far, lo, tok_dev + ANS_LEN, HD), bf16),
+        jax.ShapeDtypeStruct((side, far, lo, side * tok_dev + ANS_LEN, HD), bf16),
         [VMEM] * 4,
         flops=8 * rows * shard_len * HD,
         bytes_accessed=8 * shard_len * HD,
         transcendentals=2 * rows * shard_len,
     )(queries, cache, other, bias)
-    state = state.reshape(near, tok_dev + ANS_LEN, HD)
+    state = state.reshape(near, side * tok_dev + ANS_LEN, HD)
     state = lax.all_to_all(state, ("side", "far", "lo"), 0, 0, tiled=True)
     state = call(
         merge_kernel,
-        jax.ShapeDtypeStruct((side * pairs, tok_dev + ANS_LEN, HD), bf16),
+        jax.ShapeDtypeStruct((pairs, side * tok_dev + ANS_LEN, HD), bf16),
         [VMEM] * 2,
         flops=4 * state.size,
         bytes_accessed=2 * state.size,
         transcendentals=0,
     )(state, queries)
-    state = lax.all_to_all(state, RING, 0, 0, tiled=True)
+    state = lax.all_to_all(state, PAIR[::-1], 0, 0, tiled=True)
     projected = call(
         output_kernel,
         jax.ShapeDtypeStruct((head, tok_dev, columns), bf16),
@@ -318,7 +325,7 @@
         flops=2 * tok_dev * out_weight.size,
         bytes_accessed=2 * out_weight.size,
         transcendentals=0,
-    )(state.reshape(side, pairs, tok_dev + ANS_LEN, HD), out_weight)
+    )(state, out_weight)
     projected = lax.all_to_all(projected, HEAD[::-1], 0, 0, tiled=True)
     return call(
         sum_kernel,

time: 71.9 us -> 73.8 us (1.026)
  blocking collectives: 64.5 us -> 66.3 us
    all_to_all x1, blocking collectives: 9.2 us -> 10.2 us  [body(): state = lax.all_to_all(state, ('side', 'far', 'lo'), 0, 0, tiled=True)]
    all_to_all x1, blocking collectives: 10.9 us -> 11.8 us  [body(): state = lax.all_to_all(state, PAIR[::-1], 0, 0, tiled=True)]
where the time goes in v12:
time: 73.8 us; the launch traced here: 73.4 us
  blocking collectives  66.3 us (90%)
  Pallas kernels  5.05 us (7%)
  starting transfers between devices  1.92 us (3%)
    all_to_all x1, blocking collectives, body(): lax.all_to_all(partial.astype(jnp.float16), RING, 0, 0, tiled=True)  18.1 us
    all_to_all x1, blocking collectives, body(): projected = lax.all_to_all(projected, HEAD[::-1], 0, 0, tiled=True)  14.2 us
    all_to_all x1, blocking collectives, body(): lax.all_to_all(queries, ('side', 'far', 'lo'), 0, 0, tiled=True).astype(f32)  12.1 us
    all_to_all x1, blocking collectives, body(): state = lax.all_to_all(state, PAIR[::-1], 0, 0, tiled=True)  11.8 us
    all_to_all x1, blocking collectives, body(): state = lax.all_to_all(state, ('side', 'far', 'lo'), 0, 0, tiled=True)  10.2 us
    ppermute x1, starting transfers between devices, body(): other = lax.ppermute(cache, 'core', [(0, 1), (1, 0)])  1.92 us
    pallas_call x1, Pallas kernels, body(): call(attend_kernel, jax.ShapeDtypeStruct((side, far, lo, side * tok_dev +...  1.82 us
    pallas_call x1, Pallas kernels, body(): pl.pallas_call(project_kernel, out_shape=(jax.ShapeDtypeStruct((pairs * s...  1.74 us
  transfers between devices with their start and end apart: 1, of which 0 were waited for; matrix products, arithmetic and copies ran while one was open for 0% of the time, Pallas kernels for 0%

profile of v12, /device:TPU:8, one launch (start us, length us, event | category | flops | bytes accessed | tf_op | source)
XLA Modules:
  0.0 73.4 jit_solution(16958658584432010055)
XLA Ops:
  0.0 1.7 %shard_map.82 = (f32[8,80,128]{2,1,0:T(8,128)S(1)}, f32[8,128]{1,0:T(8,128)S(1)}, bf16[2,2048,128]{2,1,0:T(8,128)(2,1)S(1)}) custom-call(bf16[64,1024]{1,0:T(8,128)(2,1)} %hidden_hbm.1, bf16[1024,256]{1,0:T(8,128)(2,1)} %query_hbm.1, bf16[1024,128]{1,0:T(8,128)(2,1)} %key_hbm.1, bf16[1024,128]{1,0:T(8,128)(2,1)} %value_hbm.1, s32[32]{0:T(128)} %group_hbm.1, ...), custom_call_target="tpu_custom_call" | custom-call | flops 67108864 | bytes 1179648 | tf_op jit(solution)/shard_map/pallas_call | solution.py:261
  1.8 18.1 %all_to_all.25 = f16[8,80,128]{2,1,0:T(8,128)(2,1)S(1)} all-to-all(f16[8,80,128]{2,1,0:T(8,128)(2,1)S(1)} %convert_element_type.12), channel_id=1, replica_groups=mesh['far'=2,'high'=2,'low'=2,'side'=2,'head2'=2,'head1'=2,'head0'=2,'lo..., dimensions={0} | all-to-all | bytes 327680 | tf_op jit(solution)/shard_map/all_to_all | solution.py:283
  20.0 1.9 %collective-permute-start = (bf16[2,2048,128]{2,1,0:T(8,128)(2,1)S(1)}, bf16[2,2048,128]{2,1,0:T(8,128)(2,1)S(1)}, u32[]{:S(2)}, u32[]{:S(2)}) collective-permute-start(bf16[2,2048,128]{2,1,0:T(8,128)(2,1)S(1)} %get-tuple-element.13.cache_ref), channel_id=1, source_target_pairs={{0,1},{1,0},{2,3},{3,2},{4,5},{5,4},{6,7},{7,6},{8,9},{9,8},{10,11... | collective-permute-start | bytes 3145736 | tf_op jit(solution)/shard_map/ppermute | solution.py:299
  22.0 12.1 %all_to_all.26 = f16[8,80,128]{2,1,0:T(8,128)(2,1)S(1)} all-to-all(f16[8,80,128]{2,1,0:T(8,128)(2,1)S(1)} %convert_element_type.14), channel_id=1, replica_groups=mesh['far'=2,'high'=2,'low'=2,'side'=2,'head2'=2,'head1'=2,'head0'=2,'lo..., dimensions={0} | all-to-all | bytes 327680 | tf_op jit(solution)/shard_map/all_to_all | solution.py:301
  34.0 0.0 collective-permute-done.other_ref
  34.1 1.8 %shard_map.84 = bf16[2,2,2,136,128]{4,3,2,1,0:T(8,128)(2,1)S(1)} custom-call(f32[8,80,128]{2,1,0:T(8,128)S(1)} %convert_element_type.15.query_ref.own_ref, bf16[2,2048,128]{2,1,0:T(8,128)(2,1)S(1)} %get-tuple-element.13.cache_ref, bf16[2,2048,128]{2,1,0:T(8,128)(2,1)S(1)} %collective-permute-done.other_ref, f32[8,128]{1,0:T(8,128)S(1)} %get-tuple-element.14.bias_ref), custom_call_target="tpu_custom_call" | custom-call | flops 536870912 | bytes 2097152 | tf_op jit(solution)/shard_map/pallas_call | solution.py:302
  35.9 10.2 %all_to_all.27.state_ref = bf16[8,136,128]{2,1,0:T(8,128)(2,1)S(1)} all-to-all(bf16[8,136,128]{2,1,0:T(8,128)(2,1)S(1)} %bitcast.1), channel_id=1, replica_groups=mesh['far'=2,'high'=2,'low'=2,'side'=2,'head2'=2,'head1'=2,'head0'=2,'lo..., dimensions={0} | all-to-all | bytes 557056 | tf_op jit(solution)/shard_map/all_to_all | solution.py:311
  46.0 0.0 copy-start
  46.0 0.5 shard_map.85
  46.5 11.8 %all_to_all.28.state_ref = bf16[4,136,128]{2,1,0:T(8,128)(2,1)S(1)} all-to-all(bf16[4,136,128]{2,1,0:T(8,128)(2,1)S(1)} %shard_map.85), channel_id=1, replica_groups=mesh['far'=2,'high'=2,'low'=2,'side'=2,'head2'=2,'head1'=2,'head0'=2,'lo..., dimensions={0} | all-to-all | bytes 278528 | tf_op jit(solution)/shard_map/all_to_all | solution.py:320
  58.3 0.0 copy-done
  58.3 0.3 shard_map.86
  58.6 14.2 %all_to_all.29.part_ref = bf16[8,64,128]{2,1,0:T(8,128)(2,1)S(1)} all-to-all(bf16[8,64,128]{2,1,0:T(8,128)(2,1)S(1)} %shard_map.86), channel_id=1, replica_groups=mesh['far'=2,'high'=2,'low'=2,'side'=2,'head2'=2,'head1'=2,'head0'=2,'lo..., dimensions={0} | all-to-all | bytes 262144 | tf_op jit(solution)/shard_map/all_to_all | solution.py:329
  72.8 0.6 shard_map.87
  (5 shorter events, 0.1 us)
Async XLA Ops:
  20.0 14.0 %collective-permute-start = (bf16[2,2048,128]{2,1,0:T(8,128)(2,1)S(1)}, bf16[2,2048,128]{2,1,0:T(8,128)(2,1)S(1)}, u32[]{:S(2)}, u32[]{:S(2)}) collective-permute-start(bf16[2,2048,128]{2,1,0:T(8,128)(2,1)S(1)} %get-tuple-element.13.cache_ref), channel_id=1, source_target_pairs={{0,1},{1,0},{2,3},{3,2},{4,5},{5,4},{6,7},{7,6},{8,9},{9,8},{10,11... | collective-permute-start | bytes 3145736 | tf_op jit(solution)/shard_map/ppermute | solution.py:299
  46.0 12.3 %copy-start = (bf16[256,1024]{1,0:T(8,128)(2,1)S(1)}, bf16[256,1024]{1,0:T(8,128)(2,1)}, u32[]{:S(2)}) copy-start(bf16[256,1024]{1,0:T(8,128)(2,1)} %weight_ref.1) | copy-start | bytes 1572868

commit v13 on v10

--- a/solution.py
+++ b/solution.py
@@ -10,7 +10,7 @@
 HD = 128
 GROUPS = 8
 ANS_LEN = 8
-ROW_BLOCK = 128
+KEY_BLOCK = 1024
 
 NEGATIVE = -1e30
 LOG2E = math.log2(math.e)
@@ -73,6 +73,8 @@
         start(hidden_hbm.at[:, half], hidden_ref.at[:, half])
         start(key_hbm.at[half, :], weight_ref.at[half, pl.ds(width, HD)])
         start(value_hbm.at[half, :], weight_ref.at[half, pl.ds(width + HD, HD)])
+    start(key_cache, cache_hbm.at[0])
+    start(value_cache, cache_hbm.at[1])
     copies[0].wait()
     chunk = lax.axis_index(SEQ) // (lax.axis_size(SEQ) // GROUPS)
     lane = lax.broadcasted_iota(jnp.int32, bias_ref.shape, 1)
@@ -85,9 +87,6 @@
     for i, half in enumerate(halves):
         for copy in copies[4 * i + 1 : 4 * i + 5]:
             copy.wait()
-        if i == 0:
-            start(key_cache, cache_hbm.at[0])
-            start(value_cache, cache_hbm.at[1])
         part = dot(hidden_ref[:, half], weight_ref[half, :])
         total = part if total is None else total + part
     ring = SMALL_SCALE * lax.axis_size(PAIR) * side
@@ -146,46 +145,47 @@
     side, far, lo, rows, _ = out_ref.shape
     rows -= ANS_LEN
     halves = far
-    assert ROW_BLOCK == lo * rows
     cores = lax.axis_size("core")
     cands = rows // ANS_LEN
-    row = lax.broadcasted_iota(jnp.int32, (ROW_BLOCK, HD), 0)
-    lane = lax.broadcasted_iota(jnp.int32, (ROW_BLOCK, HD), 1)
-    caches = (cache_ref, other_ref)
-    steps = [(r, cache) for r in range(side) for cache in caches]
+    query = query_ref[:, :rows].reshape(side, halves, lo * rows, HD)
+    query = jnp.sum(query, axis=1).reshape(side * lo * rows, HD)
+    query = (query * (1 / SMALL_SCALE)).astype(jnp.bfloat16)
+    steps = [
+        (cache, slice(start, start + KEY_BLOCK))
+        for cache in (cache_ref, other_ref)
+        for start in range(0, cache_ref.shape[1], KEY_BLOCK)
+    ]
 
     def scored(step):
-        r, cache = step
-        parts = query_ref[r * halves * lo : (r + 1) * halves * lo, :rows]
-        query = jnp.sum(parts.reshape(halves, lo, rows, HD), axis=0).reshape(ROW_BLOCK, HD)
-        query = (query * (1 / SMALL_SCALE)).astype(jnp.bfloat16)
-        return dot_transposed(query, cache[0])
+        cache, part = step
+        return dot_transposed(query, cache[0, part])
 
     ahead = scored(steps[0])
     held = []
-    for i, (r, cache) in enumerate(steps):
+    for i, (cache, part) in enumerate(steps):
         scores = ahead
         if i + 1 < len(steps):
             ahead = scored(steps[i + 1])
         top = jnp.max(scores, axis=1, keepdims=True)
         weights = jnp.exp2((scores - top) * (scale * LOG2E))
         total = jnp.sum(weights, axis=1, keepdims=True)
-        held.append((top * scale, total, dot(weights.astype(jnp.bfloat16), cache[1])))
-        if len(held) < len(caches):
-            continue
-        top = jnp.maximum(held[0][0], held[1][0])
-        factors = [jnp.exp(part[0] - top) for part in held]
-        total = held[0][1] * factors[0] + held[1][1] * factors[1]
-        mean = (held[0][2] * factors[0] + held[1][2] * factors[1]) / total
-        held = []
-        place = (row + r * ROW_BLOCK) // ANS_LEN
-        cand = place // cands % lo * cores + lax.axis_index("core")
-        candidate = cand * cands + place % cands
-        bias = jnp.sum(jnp.where(lane == candidate, bias_ref[0:1, :], 0.0), axis=1, keepdims=True)
-        level = top + jnp.log(total) + bias
+        held.append((top * scale, total, dot(weights.astype(jnp.bfloat16), cache[1, part])))
+    top = held[0][0]
+    for part in held[1:]:
+        top = jnp.maximum(top, part[0])
+    factors = [jnp.exp(part[0] - top) for part in held]
+    total = sum(part[1] * factor for part, factor in zip(held, factors))
+    mean = sum(part[2] * factor for part, factor in zip(held, factors)) / total
+    place = lax.broadcasted_iota(jnp.int32, mean.shape, 0) // ANS_LEN
+    lane = lax.broadcasted_iota(jnp.int32, mean.shape, 1)
+    cand = place // cands % lo * cores + lax.axis_index("core")
+    candidate = cand * cands + place % cands
+    bias = jnp.sum(jnp.where(lane == candidate, bias_ref[0:1, :], 0.0), axis=1, keepdims=True)
+    level = top + jnp.log(total) + bias
+    for r in range(side):
         for j in range(lo):
-            part = slice(j * rows, (j + 1) * rows)
-            state = packed(mean[part], level[part])
+            start = (r * lo + j) * rows
+            state = packed(mean[start : start + rows], level[start : start + rows])
             for f in range(far):
                 out_ref[r, f, j] = state
 

time: 72.5 us -> 71.8 us (level)
  Pallas kernels: 5.66 us -> 4.92 us
where the time goes in v13:
time: 71.8 us; the launch traced here: 71.5 us
  blocking collectives  64.5 us (90%)
  Pallas kernels  4.92 us (7%)
  starting transfers between devices  1.92 us (3%)
    all_to_all x1, blocking collectives, body(): lax.all_to_all(partial.astype(jnp.float16), RING, 0, 0, tiled=True)  18.1 us
    all_to_all x1, blocking collectives, body(): projected = lax.all_to_all(projected, HEAD[::-1], 0, 0, tiled=True)  14.2 us
    all_to_all x1, blocking collectives, body(): lax.all_to_all(queries, ('side', 'far', 'lo'), 0, 0, tiled=True).astype(f32)  12.1 us
    all_to_all x1, blocking collectives, body(): state = lax.all_to_all(state, RING, 0, 0, tiled=True)  10.9 us
    all_to_all x1, blocking collectives, body(): state = lax.all_to_all(state, ('side', 'far', 'lo'), 0, 0, tiled=True)  9.2 us
    ppermute x1, starting transfers between devices, body(): other = lax.ppermute(cache, 'core', [(0, 1), (1, 0)])  1.92 us
    pallas_call x1, Pallas kernels, body(): call(attend_kernel, jax.ShapeDtypeStruct((side, far, lo, tok_dev + ANS_LE...  1.79 us
    pallas_call x1, Pallas kernels, body(): pl.pallas_call(project_kernel, out_shape=(jax.ShapeDtypeStruct((pairs * s...  1.71 us
  transfers between devices with their start and end apart: 1, of which 0 were waited for; matrix products, arithmetic and copies ran while one was open for 0% of the time, Pallas kernels for 0%

profile of v13, /device:TPU:8, one launch (start us, length us, event | category | flops | bytes accessed | tf_op | source)
XLA Modules:
  0.0 71.5 jit_solution(17112093150650409626)
XLA Ops:
  0.0 1.7 %shard_map.82 = (f32[8,80,128]{2,1,0:T(8,128)S(1)}, f32[8,128]{1,0:T(8,128)S(1)}, bf16[2,2048,128]{2,1,0:T(8,128)(2,1)S(1)}) custom-call(bf16[64,1024]{1,0:T(8,128)(2,1)} %hidden_hbm.1, bf16[1024,256]{1,0:T(8,128)(2,1)} %query_hbm.1, bf16[1024,128]{1,0:T(8,128)(2,1)} %key_hbm.1, bf16[1024,128]{1,0:T(8,128)(2,1)} %value_hbm.1, s32[32]{0:T(128)} %group_hbm.1, ...), custom_call_target="tpu_custom_call" | custom-call | flops 67108864 | bytes 1179648 | tf_op jit(solution)/shard_map/pallas_call | solution.py:255
  1.8 18.1 %all_to_all.25 = f16[8,80,128]{2,1,0:T(8,128)(2,1)S(1)} all-to-all(f16[8,80,128]{2,1,0:T(8,128)(2,1)S(1)} %convert_element_type.12), channel_id=1, replica_groups=mesh['far'=2,'high'=2,'low'=2,'side'=2,'head2'=2,'head1'=2,'head0'=2,'lo..., dimensions={0} | all-to-all | bytes 327680 | tf_op jit(solution)/shard_map/all_to_all | solution.py:277
  20.0 1.9 %collective-permute-start = (bf16[2,2048,128]{2,1,0:T(8,128)(2,1)S(1)}, bf16[2,2048,128]{2,1,0:T(8,128)(2,1)S(1)}, u32[]{:S(2)}, u32[]{:S(2)}) collective-permute-start(bf16[2,2048,128]{2,1,0:T(8,128)(2,1)S(1)} %get-tuple-element.13.cache_ref), channel_id=1, source_target_pairs={{0,1},{1,0},{2,3},{3,2},{4,5},{5,4},{6,7},{7,6},{8,9},{9,8},{10,11... | collective-permute-start | bytes 3145736 | tf_op jit(solution)/shard_map/ppermute | solution.py:293
  21.9 12.1 %all_to_all.26 = f16[8,80,128]{2,1,0:T(8,128)(2,1)S(1)} all-to-all(f16[8,80,128]{2,1,0:T(8,128)(2,1)S(1)} %convert_element_type.14), channel_id=1, replica_groups=mesh['far'=2,'high'=2,'low'=2,'side'=2,'head2'=2,'head1'=2,'head0'=2,'lo..., dimensions={0} | all-to-all | bytes 327680 | tf_op jit(solution)/shard_map/all_to_all | solution.py:295
  34.0 0.0 collective-permute-done.other_ref
  34.0 1.8 %shard_map.84 = bf16[2,2,2,72,128]{4,3,2,1,0:T(8,128)(2,1)S(1)} custom-call(f32[8,80,128]{2,1,0:T(8,128)S(1)} %convert_element_type.15.query_ref.own_ref, bf16[2,2048,128]{2,1,0:T(8,128)(2,1)S(1)} %get-tuple-element.13.cache_ref, bf16[2,2048,128]{2,1,0:T(8,128)(2,1)S(1)} %collective-permute-done.other_ref, f32[8,128]{1,0:T(8,128)S(1)} %get-tuple-element.14.bias_ref), custom_call_target="tpu_custom_call" | custom-call | flops 536870912 | bytes 2097152 | tf_op jit(solution)/shard_map/pallas_call | solution.py:296
  35.8 9.2 %all_to_all.27.state_ref = bf16[8,72,128]{2,1,0:T(8,128)(2,1)S(1)} all-to-all(bf16[8,72,128]{2,1,0:T(8,128)(2,1)S(1)} %bitcast.2), channel_id=1, replica_groups=mesh['far'=2,'high'=2,'low'=2,'side'=2,'head2'=2,'head1'=2,'head0'=2,'lo..., dimensions={0} | all-to-all | bytes 294912 | tf_op jit(solution)/shard_map/all_to_all | solution.py:305
  45.0 0.0 copy-start
  45.0 0.4 shard_map.85
  45.5 10.9 %all_to_all.28 = bf16[8,72,128]{2,1,0:T(8,128)(2,1)S(1)} all-to-all(bf16[8,72,128]{2,1,0:T(8,128)(2,1)S(1)} %shard_map.85), channel_id=1, replica_groups=mesh['far'=2,'high'=2,'low'=2,'side'=2,'head2'=2,'head1'=2,'head0'=2,'lo..., dimensions={0} | all-to-all | bytes 294912 | tf_op jit(solution)/shard_map/all_to_all | solution.py:314
  56.3 0.0 copy-done
  56.3 0.3 shard_map.86
  56.7 14.2 %all_to_all.29.part_ref = bf16[8,64,128]{2,1,0:T(8,128)(2,1)S(1)} all-to-all(bf16[8,64,128]{2,1,0:T(8,128)(2,1)S(1)} %shard_map.86), channel_id=1, replica_groups=mesh['far'=2,'high'=2,'low'=2,'side'=2,'head2'=2,'head1'=2,'head0'=2,'lo..., dimensions={0} | all-to-all | bytes 262144 | tf_op jit(solution)/shard_map/all_to_all | solution.py:323
  70.8 0.6 shard_map.87
  (5 shorter events, 0.1 us)
Async XLA Ops:
  20.0 14.0 %collective-permute-start = (bf16[2,2048,128]{2,1,0:T(8,128)(2,1)S(1)}, bf16[2,2048,128]{2,1,0:T(8,128)(2,1)S(1)}, u32[]{:S(2)}, u32[]{:S(2)}) collective-permute-start(bf16[2,2048,128]{2,1,0:T(8,128)(2,1)S(1)} %get-tuple-element.13.cache_ref), channel_id=1, source_target_pairs={{0,1},{1,0},{2,3},{3,2},{4,5},{5,4},{6,7},{7,6},{8,9},{9,8},{10,11... | collective-permute-start | bytes 3145736 | tf_op jit(solution)/shard_map/ppermute | solution.py:293
  45.0 11.3 %copy-start = (bf16[256,1024]{1,0:T(8,128)(2,1)S(1)}, bf16[256,1024]{1,0:T(8,128)(2,1)}, u32[]{:S(2)}) copy-start(bf16[256,1024]{1,0:T(8,128)(2,1)} %weight_ref.1) | copy-start | bytes 1572868

commit v14 on v13

--- a/solution.py
+++ b/solution.py
@@ -147,8 +147,8 @@
     halves = far
     cores = lax.axis_size("core")
     cands = rows // ANS_LEN
-    query = query_ref[:, :rows].reshape(side, halves, lo * rows, HD)
-    query = jnp.sum(query, axis=1).reshape(side * lo * rows, HD)
+    query = jnp.sum(query_ref[:, :rows].reshape(halves, lo, side, rows, HD), axis=0)
+    query = jnp.concatenate([query[j, r] for r in range(side) for j in range(lo)], axis=0)
     query = (query * (1 / SMALL_SCALE)).astype(jnp.bfloat16)
     steps = [
         (cache, slice(start, start + KEY_BLOCK))
@@ -198,10 +198,11 @@
 
     def own(s, part, scale):
         lo = lax.axis_size("lo")
-        place = s * halves * lo + lax.axis_index("lo")
+        heads = lax.axis_size("side")
+        place = lax.axis_index("lo") * heads + s
         total = own_ref[place, part]
         for half in range(1, halves):
-            total = total + own_ref[place + half * lo, part]
+            total = total + own_ref[place + half * lo * heads, part]
         return (total * (1 / scale)).astype(jnp.bfloat16)
 
     query = own(lax.axis_index("side"), slice(0, tokens), SMALL_SCALE)
@@ -292,7 +293,7 @@
     )(partial.astype(f32), cache)
     other = lax.ppermute(cache, "core", [(0, 1), (1, 0)])
     queries = queries.astype(jnp.float16)
-    queries = lax.all_to_all(queries, ("side", "far", "lo"), 0, 0, tiled=True).astype(f32)
+    queries = lax.all_to_all(queries, ("far", "lo", "side"), 0, 0, tiled=True).astype(f32)
     state = call(
         attend_kernel,
         jax.ShapeDtypeStruct((side, far, lo, tok_dev + ANS_LEN, HD), bf16),

time: 71.8 us -> 71.8 us (level)
  no operation moved by 1% of the time
where the time goes in v14:
time: 71.8 us; the launch traced here: 71.5 us
  blocking collectives  64.5 us (90%)
  Pallas kernels  4.92 us (7%)
  starting transfers between devices  1.92 us (3%)
    all_to_all x1, blocking collectives, body(): lax.all_to_all(partial.astype(jnp.float16), RING, 0, 0, tiled=True)  18.1 us
    all_to_all x1, blocking collectives, body(): projected = lax.all_to_all(projected, HEAD[::-1], 0, 0, tiled=True)  14.2 us
    all_to_all x1, blocking collectives, body(): lax.all_to_all(queries, ('far', 'lo', 'side'), 0, 0, tiled=True).astype(f32)  12.1 us
    all_to_all x1, blocking collectives, body(): state = lax.all_to_all(state, RING, 0, 0, tiled=True)  10.9 us
    all_to_all x1, blocking collectives, body(): state = lax.all_to_all(state, ('side', 'far', 'lo'), 0, 0, tiled=True)  9.13 us
    ppermute x1, starting transfers between devices, body(): other = lax.ppermute(cache, 'core', [(0, 1), (1, 0)])  1.92 us
    pallas_call x1, Pallas kernels, body(): call(attend_kernel, jax.ShapeDtypeStruct((side, far, lo, tok_dev + ANS_LE...  1.79 us
    pallas_call x1, Pallas kernels, body(): pl.pallas_call(project_kernel, out_shape=(jax.ShapeDtypeStruct((pairs * s...  1.71 us
  transfers between devices with their start and end apart: 1, of which 0 were waited for; matrix products, arithmetic and copies ran while one was open for 0% of the time, Pallas kernels for 0%

profile of v14, /device:TPU:8, one launch (start us, length us, event | category | flops | bytes accessed | tf_op | source)
XLA Modules:
  0.0 71.5 jit_solution(11766153046296709940)
XLA Ops:
  0.0 1.7 %shard_map.82 = (f32[8,80,128]{2,1,0:T(8,128)S(1)}, f32[8,128]{1,0:T(8,128)S(1)}, bf16[2,2048,128]{2,1,0:T(8,128)(2,1)S(1)}) custom-call(bf16[64,1024]{1,0:T(8,128)(2,1)} %hidden_hbm.1, bf16[1024,256]{1,0:T(8,128)(2,1)} %query_hbm.1, bf16[1024,128]{1,0:T(8,128)(2,1)} %key_hbm.1, bf16[1024,128]{1,0:T(8,128)(2,1)} %value_hbm.1, s32[32]{0:T(128)} %group_hbm.1, ...), custom_call_target="tpu_custom_call" | custom-call | flops 67108864 | bytes 1179648 | tf_op jit(solution)/shard_map/pallas_call | solution.py:256
  1.8 18.1 %all_to_all.25 = f16[8,80,128]{2,1,0:T(8,128)(2,1)S(1)} all-to-all(f16[8,80,128]{2,1,0:T(8,128)(2,1)S(1)} %convert_element_type.12), channel_id=1, replica_groups=mesh['far'=2,'high'=2,'low'=2,'side'=2,'head2'=2,'head1'=2,'head0'=2,'lo..., dimensions={0} | all-to-all | bytes 327680 | tf_op jit(solution)/shard_map/all_to_all | solution.py:278
  20.0 1.9 %collective-permute-start = (bf16[2,2048,128]{2,1,0:T(8,128)(2,1)S(1)}, bf16[2,2048,128]{2,1,0:T(8,128)(2,1)S(1)}, u32[]{:S(2)}, u32[]{:S(2)}) collective-permute-start(bf16[2,2048,128]{2,1,0:T(8,128)(2,1)S(1)} %get-tuple-element.13.cache_ref), channel_id=1, source_target_pairs={{0,1},{1,0},{2,3},{3,2},{4,5},{5,4},{6,7},{7,6},{8,9},{9,8},{10,11... | collective-permute-start | bytes 3145736 | tf_op jit(solution)/shard_map/ppermute | solution.py:294
  21.9 12.1 %all_to_all.26 = f16[8,80,128]{2,1,0:T(8,128)(2,1)S(1)} all-to-all(f16[8,80,128]{2,1,0:T(8,128)(2,1)S(1)} %convert_element_type.14), channel_id=1, replica_groups=mesh['far'=2,'high'=2,'low'=2,'side'=2,'head2'=2,'head1'=2,'head0'=2,'lo..., dimensions={0} | all-to-all | bytes 327680 | tf_op jit(solution)/shard_map/all_to_all | solution.py:296
  34.1 0.0 collective-permute-done.other_ref
  34.1 1.8 %shard_map.84 = bf16[2,2,2,72,128]{4,3,2,1,0:T(8,128)(2,1)S(1)} custom-call(f32[8,80,128]{2,1,0:T(8,128)S(1)} %convert_element_type.15.query_ref.own_ref, bf16[2,2048,128]{2,1,0:T(8,128)(2,1)S(1)} %get-tuple-element.13.cache_ref, bf16[2,2048,128]{2,1,0:T(8,128)(2,1)S(1)} %collective-permute-done.other_ref, f32[8,128]{1,0:T(8,128)S(1)} %get-tuple-element.14.bias_ref), custom_call_target="tpu_custom_call" | custom-call | flops 536870912 | bytes 2097152 | tf_op jit(solution)/shard_map/pallas_call | solution.py:297
  35.9 9.1 %all_to_all.27.state_ref = bf16[8,72,128]{2,1,0:T(8,128)(2,1)S(1)} all-to-all(bf16[8,72,128]{2,1,0:T(8,128)(2,1)S(1)} %bitcast.2), channel_id=1, replica_groups=mesh['far'=2,'high'=2,'low'=2,'side'=2,'head2'=2,'head1'=2,'head0'=2,'lo..., dimensions={0} | all-to-all | bytes 294912 | tf_op jit(solution)/shard_map/all_to_all | solution.py:306
  45.0 0.0 copy-start
  45.0 0.4 shard_map.85
  45.5 10.9 %all_to_all.28 = bf16[8,72,128]{2,1,0:T(8,128)(2,1)S(1)} all-to-all(bf16[8,72,128]{2,1,0:T(8,128)(2,1)S(1)} %shard_map.85), channel_id=1, replica_groups=mesh['far'=2,'high'=2,'low'=2,'side'=2,'head2'=2,'head1'=2,'head0'=2,'lo..., dimensions={0} | all-to-all | bytes 294912 | tf_op jit(solution)/shard_map/all_to_all | solution.py:315
  56.3 0.0 copy-done
  56.3 0.3 shard_map.86
  56.7 14.2 %all_to_all.29.part_ref = bf16[8,64,128]{2,1,0:T(8,128)(2,1)S(1)} all-to-all(bf16[8,64,128]{2,1,0:T(8,128)(2,1)S(1)} %shard_map.86), channel_id=1, replica_groups=mesh['far'=2,'high'=2,'low'=2,'side'=2,'head2'=2,'head1'=2,'head0'=2,'lo..., dimensions={0} | all-to-all | bytes 262144 | tf_op jit(solution)/shard_map/all_to_all | solution.py:324
  70.8 0.6 shard_map.87
  (5 shorter events, 0.1 us)
Async XLA Ops:
  20.0 14.1 %collective-permute-start = (bf16[2,2048,128]{2,1,0:T(8,128)(2,1)S(1)}, bf16[2,2048,128]{2,1,0:T(8,128)(2,1)S(1)}, u32[]{:S(2)}, u32[]{:S(2)}) collective-permute-start(bf16[2,2048,128]{2,1,0:T(8,128)(2,1)S(1)} %get-tuple-element.13.cache_ref), channel_id=1, source_target_pairs={{0,1},{1,0},{2,3},{3,2},{4,5},{5,4},{6,7},{7,6},{8,9},{9,8},{10,11... | collective-permute-start | bytes 3145736 | tf_op jit(solution)/shard_map/ppermute | solution.py:294
  45.0 11.3 %copy-start = (bf16[256,1024]{1,0:T(8,128)(2,1)S(1)}, bf16[256,1024]{1,0:T(8,128)(2,1)}, u32[]{:S(2)}) copy-start(bf16[256,1024]{1,0:T(8,128)(2,1)} %weight_ref.1) | copy-start | bytes 1572868

commit v15 on v14

--- a/solution.py
+++ b/solution.py
@@ -60,7 +60,8 @@
     far, pairs, side = (lax.axis_size(name) for name in ("far", PAIR, "side"))
     features = hidden_ref.shape[1]
     width = query_hbm.shape[1]
-    halves = [pl.ds(i * (features // 2), features // 2) for i in range(2)]
+    first = features // 4 * 3
+    halves = [pl.ds(0, first), pl.ds(first, features - first)]
     copies = []
 
     def start(source, target):

time: 71.8 us -> 71.8 us (level)
  no operation moved by 1% of the time
where the time goes in v15:
time: 71.8 us; the launch traced here: 71.5 us
  blocking collectives  64.5 us (90%)
  Pallas kernels  4.92 us (7%)
  starting transfers between devices  1.92 us (3%)
    all_to_all x1, blocking collectives, body(): lax.all_to_all(partial.astype(jnp.float16), RING, 0, 0, tiled=True)  18.1 us
    all_to_all x1, blocking collectives, body(): projected = lax.all_to_all(projected, HEAD[::-1], 0, 0, tiled=True)  14.2 us
    all_to_all x1, blocking collectives, body(): lax.all_to_all(queries, ('far', 'lo', 'side'), 0, 0, tiled=True).astype(f32)  12.1 us
    all_to_all x1, blocking collectives, body(): state = lax.all_to_all(state, RING, 0, 0, tiled=True)  10.9 us
    all_to_all x1, blocking collectives, body(): state = lax.all_to_all(state, ('side', 'far', 'lo'), 0, 0, tiled=True)  9.13 us
    ppermute x1, starting transfers between devices, body(): other = lax.ppermute(cache, 'core', [(0, 1), (1, 0)])  1.92 us
    pallas_call x1, Pallas kernels, body(): call(attend_kernel, jax.ShapeDtypeStruct((side, far, lo, tok_dev + ANS_LE...  1.79 us
    pallas_call x1, Pallas kernels, body(): pl.pallas_call(project_kernel, out_shape=(jax.ShapeDtypeStruct((pairs * s...  1.71 us
  transfers between devices with their start and end apart: 1, of which 0 were waited for; matrix products, arithmetic and copies ran while one was open for 0% of the time, Pallas kernels for 0%

profile of v15, /device:TPU:8, one launch (start us, length us, event | category | flops | bytes accessed | tf_op | source)
XLA Modules:
  0.0 71.5 jit_solution(2613230660943170376)
XLA Ops:
  0.0 1.7 %shard_map.82 = (f32[8,80,128]{2,1,0:T(8,128)S(1)}, f32[8,128]{1,0:T(8,128)S(1)}, bf16[2,2048,128]{2,1,0:T(8,128)(2,1)S(1)}) custom-call(bf16[64,1024]{1,0:T(8,128)(2,1)} %hidden_hbm.1, bf16[1024,256]{1,0:T(8,128)(2,1)} %query_hbm.1, bf16[1024,128]{1,0:T(8,128)(2,1)} %key_hbm.1, bf16[1024,128]{1,0:T(8,128)(2,1)} %value_hbm.1, s32[32]{0:T(128)} %group_hbm.1, ...), custom_call_target="tpu_custom_call" | custom-call | flops 67108864 | bytes 1179648 | tf_op jit(solution)/shard_map/pallas_call | solution.py:257
  1.8 18.1 %all_to_all.25 = f16[8,80,128]{2,1,0:T(8,128)(2,1)S(1)} all-to-all(f16[8,80,128]{2,1,0:T(8,128)(2,1)S(1)} %convert_element_type.12), channel_id=1, replica_groups=mesh['far'=2,'high'=2,'low'=2,'side'=2,'head2'=2,'head1'=2,'head0'=2,'lo..., dimensions={0} | all-to-all | bytes 327680 | tf_op jit(solution)/shard_map/all_to_all | solution.py:279
  20.0 1.9 %collective-permute-start = (bf16[2,2048,128]{2,1,0:T(8,128)(2,1)S(1)}, bf16[2,2048,128]{2,1,0:T(8,128)(2,1)S(1)}, u32[]{:S(2)}, u32[]{:S(2)}) collective-permute-start(bf16[2,2048,128]{2,1,0:T(8,128)(2,1)S(1)} %get-tuple-element.13.cache_ref), channel_id=1, source_target_pairs={{0,1},{1,0},{2,3},{3,2},{4,5},{5,4},{6,7},{7,6},{8,9},{9,8},{10,11... | collective-permute-start | bytes 3145736 | tf_op jit(solution)/shard_map/ppermute | solution.py:295
  21.9 12.1 %all_to_all.26 = f16[8,80,128]{2,1,0:T(8,128)(2,1)S(1)} all-to-all(f16[8,80,128]{2,1,0:T(8,128)(2,1)S(1)} %convert_element_type.14), channel_id=1, replica_groups=mesh['far'=2,'high'=2,'low'=2,'side'=2,'head2'=2,'head1'=2,'head0'=2,'lo..., dimensions={0} | all-to-all | bytes 327680 | tf_op jit(solution)/shard_map/all_to_all | solution.py:297
  34.1 0.0 collective-permute-done.other_ref
  34.1 1.8 %shard_map.84 = bf16[2,2,2,72,128]{4,3,2,1,0:T(8,128)(2,1)S(1)} custom-call(f32[8,80,128]{2,1,0:T(8,128)S(1)} %convert_element_type.15.query_ref.own_ref, bf16[2,2048,128]{2,1,0:T(8,128)(2,1)S(1)} %get-tuple-element.13.cache_ref, bf16[2,2048,128]{2,1,0:T(8,128)(2,1)S(1)} %collective-permute-done.other_ref, f32[8,128]{1,0:T(8,128)S(1)} %get-tuple-element.14.bias_ref), custom_call_target="tpu_custom_call" | custom-call | flops 536870912 | bytes 2097152 | tf_op jit(solution)/shard_map/pallas_call | solution.py:298
  35.9 9.1 %all_to_all.27.state_ref = bf16[8,72,128]{2,1,0:T(8,128)(2,1)S(1)} all-to-all(bf16[8,72,128]{2,1,0:T(8,128)(2,1)S(1)} %bitcast.2), channel_id=1, replica_groups=mesh['far'=2,'high'=2,'low'=2,'side'=2,'head2'=2,'head1'=2,'head0'=2,'lo..., dimensions={0} | all-to-all | bytes 294912 | tf_op jit(solution)/shard_map/all_to_all | solution.py:307
  45.0 0.0 copy-start
  45.0 0.4 shard_map.85
  45.5 10.9 %all_to_all.28 = bf16[8,72,128]{2,1,0:T(8,128)(2,1)S(1)} all-to-all(bf16[8,72,128]{2,1,0:T(8,128)(2,1)S(1)} %shard_map.85), channel_id=1, replica_groups=mesh['far'=2,'high'=2,'low'=2,'side'=2,'head2'=2,'head1'=2,'head0'=2,'lo..., dimensions={0} | all-to-all | bytes 294912 | tf_op jit(solution)/shard_map/all_to_all | solution.py:316
  56.3 0.0 copy-done
  56.3 0.3 shard_map.86
  56.7 14.2 %all_to_all.29.part_ref = bf16[8,64,128]{2,1,0:T(8,128)(2,1)S(1)} all-to-all(bf16[8,64,128]{2,1,0:T(8,128)(2,1)S(1)} %shard_map.86), channel_id=1, replica_groups=mesh['far'=2,'high'=2,'low'=2,'side'=2,'head2'=2,'head1'=2,'head0'=2,'lo..., dimensions={0} | all-to-all | bytes 262144 | tf_op jit(solution)/shard_map/all_to_all | solution.py:325
  70.8 0.6 shard_map.87
  (5 shorter events, 0.1 us)
Async XLA Ops:
  20.0 14.1 %collective-permute-start = (bf16[2,2048,128]{2,1,0:T(8,128)(2,1)S(1)}, bf16[2,2048,128]{2,1,0:T(8,128)(2,1)S(1)}, u32[]{:S(2)}, u32[]{:S(2)}) collective-permute-start(bf16[2,2048,128]{2,1,0:T(8,128)(2,1)S(1)} %get-tuple-element.13.cache_ref), channel_id=1, source_target_pairs={{0,1},{1,0},{2,3},{3,2},{4,5},{5,4},{6,7},{7,6},{8,9},{9,8},{10,11... | collective-permute-start | bytes 3145736 | tf_op jit(solution)/shard_map/ppermute | solution.py:295
  45.0 11.3 %copy-start = (bf16[256,1024]{1,0:T(8,128)(2,1)S(1)}, bf16[256,1024]{1,0:T(8,128)(2,1)}, u32[]{:S(2)}) copy-start(bf16[256,1024]{1,0:T(8,128)(2,1)} %weight_ref.1) | copy-start | bytes 1572868
